TPU v7x, 512 devices: a whole 4x4x16 slice. The times are simulated.
512 devices in a mesh: body: 2 (over core), gx: 16 (over z), gy: 16 (over x, y).
Axes of the slice: x: 4, y: 4, z: 16, core: 2. Of those that a mesh axis runs over, the one named last changes fastest.
Arguments:
- disp: float32 [2, 3, 128, 512, 128], P('body', None, 'gx', 'gy'), may hold values from -4 to 4
- force: float32 [2, 3, 128, 512, 128], P('body', None, 'gx', 'gy'), may hold values from -12 to 12
- kappa: float32 [2, 128, 512, 128], P('body', 'gx', 'gy'), may hold values from 0.05 to 0.5
- sigma: float32 [2, 128, 512, 128], P('body', 'gx', 'gy'), may hold values from 0.2 to 1
- gap0: float32 [512, 128], P(('gx', 'gy')), may hold values from -3 to 3
- pressure: float32 [512, 128], P(('gx', 'gy')), may hold values from 0 to 1
- mortar: float32 [512, 128, 128], P(('gx', 'gy')), may hold values from -0.5 to 0.5
- partner: int32 [512], P(('gx', 'gy')), may hold values from 0 to 31
- active: int32 [512], P(('gx', 'gy')), may hold values 0 or 1
Outputs:
- increment: float32 [2, 3, 128, 512, 128], P('body', None, 'gx', 'gy')
- new_pressure: float32 [512, 128], P(('gx', 'gy'))
Inputs may be any that keep to these rules, and one draw needn't show every extreme that they name: partner numbers a master block of the same gy index: gx index times 2 plus the local block. 1 marks a block of the active contact set.
All inputs are finite; a program needn't handle non-finite values.
Results may differ from a plain program's by a relative error of at most 0.00015.
Values sent between devices are 32-bit elements; how exact they have to be, the bound alone decides.
No kernel may reach another device: no remote copies, remote signals or barrier semaphores. Data moves between devices by JAX's collectives and lax.ppermute only.
A program may use at most 64 MiB of HBM per device.

v0:
```python
import jax
import jax.numpy as jnp
from jax import lax
from jax.sharding import PartitionSpec as P

SBLK = 128
CG_ITERS = 2


def extended(block, sides, width):
    for axis, dim in sides:
        count = lax.axis_size(axis)
        forward = [(i, i + 1) for i in range(count - 1)]
        backward = [(target, source) for source, target in forward]
        low = lax.ppermute(
            lax.slice_in_dim(block, block.shape[dim] - width, None, axis=dim), axis, forward
        )
        high = lax.ppermute(lax.slice_in_dim(block, 0, width, axis=dim), axis, backward)
        block = jnp.concatenate([low, block, high], axis=dim)
    return block


def neighbours():
    result = []
    for first in (-1, 0, 1):
        for second in (-1, 0, 1):
            for third in (-1, 0, 1):
                if first != 0 or second != 0 or third != 0:
                    result.append((first, second, third))
    return result


def apply_stencil(field, padded, kappa, kappa_rim, sigma):
    sizes = field.shape[2:]
    total = sigma[:, None] * field
    for offset in neighbours():
        weight = 0.5 ** (abs(offset[0]) + abs(offset[1]) + abs(offset[2]) - 1)
        lower = [1 + offset[0], 1 + offset[1], 1 + offset[2]]
        bond = 0.5 * (
            kappa
            + kappa_rim[
                :,
                lower[0] : lower[0] + sizes[0],
                lower[1] : lower[1] + sizes[1],
                lower[2] : lower[2] + sizes[2],
            ]
        )
        near = padded[
            :,
            :,
            lower[0] : lower[0] + sizes[0],
            lower[1] : lower[1] + sizes[1],
            lower[2] : lower[2] + sizes[2],
        ]
        total = total + weight * bond[:, None] * (field - near)
    return total


def stencil(field, kappa, kappa_rim, sigma):
    padded = extended(field, (("gx", 2), ("gy", 3)), 1)
    padded = jnp.pad(padded, ((0, 0), (0, 0), (0, 0), (0, 0), (1, 1)))
    return apply_stencil(field, padded, kappa, kappa_rim, sigma)


def gap_of(field, selector, mortar):
    own = field[0, 2, :, :, 0].reshape(1, -1, SBLK)
    rows = lax.all_gather(own, ("body", "gx"), axis=0, tiled=True)
    row_count = lax.axis_size("gx")
    slave_own = lax.dynamic_index_in_dim(rows, lax.axis_index("gx"), 0, keepdims=False)
    master_row = rows[row_count:].reshape(-1, SBLK)
    picked = jnp.dot(selector, master_row, precision=lax.Precision.HIGHEST)
    pulled = jnp.einsum("bij,bj->bi", mortar, picked, precision=lax.Precision.HIGHEST)
    return -slave_own - pulled


def spread(traction, selector, mortar):
    pulled = jnp.einsum("bij,bi->bj", mortar, traction, precision=lax.Precision.HIGHEST)
    row_terms = -jnp.dot(selector.T, pulled, precision=lax.Precision.HIGHEST)
    share = lax.psum_scatter(row_terms, "gx", scatter_dimension=0, tiled=True)
    return jnp.where(lax.axis_index("body") == 0, -traction, share)


def add_surface(image, surface):
    return image.at[0, 2, :, :, 0].add(surface.reshape(image.shape[2], image.shape[3]))


def global_sum(value):
    return lax.psum(value, ("body", "gx", "gy"))


def on_device(disp, force, kappa, sigma, gap0, pressure, mortar, partner, active):
    kappa_rim = extended(kappa, (("gx", 1), ("gy", 2)), 1)
    kappa_rim = jnp.pad(kappa_rim, ((0, 0), (0, 0), (0, 0), (1, 1)))
    row_blocks = mortar.shape[0] * lax.axis_size("gx")
    selector = (partner[:, None] == jnp.arange(row_blocks, dtype=jnp.int32)[None, :]).astype(
        jnp.float32
    )
    flags = active.astype(jnp.float32)[:, None]
    gap = gap0 + gap_of(disp, selector, mortar)
    radius = jnp.sqrt(gap * gap + pressure * pressure + 0.01)
    complement = gap + pressure - radius
    slope_gap = 1.0 - gap / radius
    slope_press = 1.0 - pressure / radius
    divisor = slope_press + 0.5
    stiffness = flags * slope_gap / divisor
    excess = flags * complement / divisor
    rhs = force - stencil(disp, kappa, kappa_rim, sigma)
    rhs = add_surface(rhs, spread(flags * pressure - excess, selector, mortar))
    increment = jnp.zeros_like(rhs)
    residual = rhs
    direction = rhs
    norm_now = global_sum(jnp.sum(residual * residual))
    for step in range(CG_ITERS):
        image = stencil(direction, kappa, kappa_rim, sigma)
        image = add_surface(
            image, spread(stiffness * gap_of(direction, selector, mortar), selector, mortar)
        )
        alpha = norm_now / lax.psum(jnp.sum(direction * image), ("body", "gx", "gy"))
        increment = increment + alpha * direction
        residual = residual - alpha * image
        norm_next = global_sum(jnp.sum(residual * residual))
        direction = residual + norm_next / norm_now * direction
        norm_now = norm_next
    change = gap_of(increment, selector, mortar)
    new_press = flags * (pressure - (complement + slope_gap * change) / divisor)
    return (increment, new_press)


def solution(mesh):
    placed = (
        P("body", None, "gx", "gy", None),
        P("body", None, "gx", "gy", None),
        P("body", "gx", "gy", None),
        P("body", "gx", "gy", None),
        P(("gx", "gy"), None),
        P(("gx", "gy"), None),
        P(("gx", "gy"), None, None),
        P(("gx", "gy")),
        P(("gx", "gy")),
    )
    return jax.shard_map(
        on_device,
        mesh=mesh,
        in_specs=placed,
        out_specs=(P("body", None, "gx", "gy", None), P(("gx", "gy"), None)),
        check_vma=False,
    )
```

profile of v0, /device:TPU:1, one launch (start us, length us, event | category | flops | bytes accessed | tf_op | source)
XLA Modules:
  0.0 782.8 jit_solution(5270657747271295689)
XLA Ops:
  1.5 4.4 collective-permute-start.4
  5.9 1.3 collective-permute-start.5
  7.9 4.2 collective-permute-start
  12.1 1.3 collective-permute-start.1
  15.2 61.1 %all_gather.12 = f32[32,2,128]{2,1,0:T(2,128)S(1)} all-gather(f32[1,2,128]{2,1,0:T(2,128)S(1)} %reshape_squeeze.12), channel_id=1, replica_groups=mesh['body'=2,'gx'=16,'gy'=16] {'body','gx'}, dimensions={0}, use_global_device_ids=true | all-gather | bytes 33792 | tf_op jit(solution)/shard_map/all_gather | solution.py:67
  81.3 39.8 %all-reduce.4 = f32[32,128]{1,0:T(8,128)S(1)} all-reduce(f32[32,128]{1,0:T(8,128)S(1)} %convolution_negate_fusion.2), channel_id=2, replica_groups=mesh['body'=2,'gx'=16,'gy'=16] {'gx'}, use_global_device_ids=true, to_apply=%region_0.1.clone | all-reduce | flops 4096 | bytes 32768
  123.3 4.0 collective-permute-start.2
  130.7 4.2 collective-permute-start.6
  136.5 2.3 fusion.16
  140.4 4.0 collective-permute-start.8
  144.5 70.0 %all_gather.13 = f32[32,2,128]{2,1,0:T(2,128)S(1)} all-gather(f32[1,2,128]{2,1,0:T(2,128)S(1)} %reshape_squeeze.13), channel_id=1, replica_groups=mesh['body'=2,'gx'=16,'gy'=16] {'body','gx'}, dimensions={0}, use_global_device_ids=true | all-gather | bytes 33792 | tf_op jit(solution)/shard_map/all_gather | solution.py:67
  216.2 39.1 %all-reduce.5 = f32[32,128]{1,0:T(8,128)S(1)} all-reduce(f32[32,128]{1,0:T(8,128)S(1)} %convolution_negate_fusion.1), channel_id=3, replica_groups=mesh['body'=2,'gx'=16,'gy'=16] {'gx'}, use_global_device_ids=true, to_apply=%region_3.4.clone | all-reduce | flops 4096 | bytes 32768
  256.6 4.5 collective-permute-start.10
  263.8 2.9 fusion.95
  267.7 125.8 %all-reduce.7 = (f32[]{:T(128)}, f32[]{:T(128)}) all-reduce(f32[]{:T(128)} %get-tuple-element.39, f32[]{:T(128)} %get-tuple-element.38), channel_id=1, replica_groups=mesh['body'=2,'gx'=16,'gy'=16] {'body','gx','gy'}, use_global_device_ids=true, to_apply=%region_2.3 | all-reduce | flops 2 | bytes 16 | tf_op jit(solution)/shard_map/psum | solution.py:88
  395.5 99.7 %psum.30 = f32[]{:T(128)} all-reduce(f32[]{:T(128)} %multiply_reduce_fusion.1), channel_id=1, replica_groups=mesh['body'=2,'gx'=16,'gy'=16] {'body','gx','gy'}, use_global_device_ids=true, to_apply=%region_7.8 | all-reduce | flops 1 | bytes 8 | tf_op jit(solution)/shard_map/psum | solution.py:88
  496.7 1.3 collective-permute-start.13
  498.0 4.0 collective-permute-start.12
  502.1 52.8 %all_gather.14 = f32[32,2,128]{2,1,0:T(2,128)S(1)} all-gather(f32[1,2,128]{2,1,0:T(2,128)S(1)} %reshape_squeeze.14), channel_id=1, replica_groups=mesh['body'=2,'gx'=16,'gy'=16] {'body','gx'}, dimensions={0}, use_global_device_ids=true | all-gather | bytes 33792 | tf_op jit(solution)/shard_map/all_gather | solution.py:67
  557.9 39.2 %all-reduce.6 = f32[32,128]{1,0:T(8,128)S(1)} all-reduce(f32[32,128]{1,0:T(8,128)S(1)} %convolution_negate_fusion), channel_id=4, replica_groups=mesh['body'=2,'gx'=16,'gy'=16] {'gx'}, use_global_device_ids=true, to_apply=%region_8.9.clone | all-reduce | flops 4096 | bytes 32768
  598.4 4.2 collective-permute-start.14
  605.4 2.9 fusion.41
  609.2 117.7 %psum.31 = f32[]{:T(128)} all-reduce(f32[]{:T(128)} %multiply_reduce_fusion), channel_id=1, replica_groups=mesh['body'=2,'gx'=16,'gy'=16] {'body','gx','gy'}, use_global_device_ids=true, to_apply=%region_10.11 | all-reduce | flops 1 | bytes 8 | tf_op jit(solution)/shard_map/psum | solution.py:118
  728.5 53.1 %all_gather.15 = f32[32,2,128]{2,1,0:T(2,128)S(1)} all-gather(f32[1,2,128]{2,1,0:T(2,128)S(1)} %reshape_squeeze.15), channel_id=1, replica_groups=mesh['body'=2,'gx'=16,'gy'=16] {'body','gx'}, dimensions={0}, use_global_device_ids=true | all-gather | bytes 33792 | tf_op jit(solution)/shard_map/all_gather | solution.py:67
  (173 shorter events, 33.1 us)
Async XLA Ops:
  0.6 76.5 %copy-start = (f32[2,128,128]{2,1,0:T(8,128)S(1)}, f32[2,128,128]{2,1,0:T(8,128)}, u32[]{:S(2)}) copy-start(f32[2,128,128]{2,1,0:T(8,128)} %param.21) | copy-start | bytes 393220
  0.6 127.6 %copy-start.26 = (f32[1,8,32,128]{3,2,1,0:T(8,128)S(1)}, f32[1,8,32,128]{3,2,1,0:T(8,128)}, u32[]{:S(2)}) copy-start(f32[1,8,32,128]{3,2,1,0:T(8,128)} %param.17) | copy-start | bytes 393220
  1.5 127.2 %collective-permute-start.4 = (f32[1,3,1,32,128]{4,3,2,1,0:T(8,128)S(1)}, f32[1,3,1,32,128]{4,3,2,1,0:T(8,128)S(1)}, u32[]{:S(2)}, u32[]{:S(2)}) collective-permute-start(f32[1,3,1,32,128]{4,3,2,1,0:T(8,128)S(1)} %get-tuple-element.82), channel_id=1, source_target_pairs={{0,16},{16,32},{32,48},{48,64},{64,80},{80,96},{96,112},{112,128},... | collective-permute-start | bytes 147464 | tf_op jit(solution)/shard_map/ppermute | solution.py:15
  5.9 123.4 %collective-permute-start.5 = (f32[1,3,1,32,128]{4,3,2,1,0:T(8,128)S(1)}, f32[1,3,1,32,128]{4,3,2,1,0:T(8,128)S(1)}, u32[]{:S(2)}, u32[]{:S(2)}) collective-permute-start(f32[1,3,1,32,128]{4,3,2,1,0:T(8,128)S(1)} %get-tuple-element.81), channel_id=1, source_target_pairs={{16,0},{32,16},{48,32},{64,48},{80,64},{96,80},{112,96},{128,112},... | collective-permute-start | bytes 147464 | tf_op jit(solution)/shard_map/ppermute | solution.py:18
  7.9 113.1 %collective-permute-start = (f32[1,1,32,128]{3,2,1,0:T(8,128)S(1)}, f32[1,1,32,128]{3,2,1,0:T(8,128)S(1)}, u32[]{:S(2)}, u32[]{:S(2)}) collective-permute-start(f32[1,1,32,128]{3,2,1,0:T(8,128)S(1)} %get-tuple-element.97), channel_id=1, source_target_pairs={{0,16},{16,32},{32,48},{48,64},{64,80},{80,96},{96,112},{112,128},... | collective-permute-start | bytes 49160 | tf_op jit(solution)/shard_map/ppermute | solution.py:15
  12.1 109.8 %collective-permute-start.1 = (f32[1,1,32,128]{3,2,1,0:T(8,128)S(1)}, f32[1,1,32,128]{3,2,1,0:T(8,128)S(1)}, u32[]{:S(2)}, u32[]{:S(2)}) collective-permute-start(f32[1,1,32,128]{3,2,1,0:T(8,128)S(1)} %get-tuple-element.96), channel_id=1, source_target_pairs={{16,0},{32,16},{48,32},{64,48},{80,64},{96,80},{112,96},{128,112},... | collective-permute-start | bytes 49160 | tf_op jit(solution)/shard_map/ppermute | solution.py:18
  122.0 5.5 collective-permute-start.3
  123.3 4.7 collective-permute-start.2
  128.8 134.0 %copy-start.2 = (f32[8,32,128]{2,1,0:T(8,128)}, f32[8,32,128]{2,1,0:T(8,128)S(1)}, u32[]{:S(2)}) copy-start(f32[8,32,128]{2,1,0:T(8,128)S(1)} %get-tuple-element.66) | copy-start | bytes 393220
  129.4 5.8 collective-permute-start.7
  130.7 5.1 collective-permute-start.6
  135.1 127.6 %copy-start.4 = (f32[8,32,128]{2,1,0:T(8,128)}, f32[8,32,128]{2,1,0:T(8,128)S(1)}, u32[]{:S(2)}) copy-start(f32[8,32,128]{2,1,0:T(8,128)S(1)} %get-tuple-element.83) | copy-start | bytes 393220
  135.1 127.6 %copy-start.6 = (f32[8,32,128]{2,1,0:T(8,128)}, f32[8,32,128]{2,1,0:T(8,128)S(1)}, u32[]{:S(2)}) copy-start(f32[8,32,128]{2,1,0:T(8,128)S(1)} %get-tuple-element.84) | copy-start | bytes 393220
  136.5 78.0 %copy-start.39 = (s32[2]{0:T(128)S(1)}, s32[2]{0:T(128)}, u32[]{:S(2)}) copy-start(s32[2]{0:T(128)} %param.22) | copy-start | bytes 28
  136.5 78.5 %copy-start.38 = (f32[2,128]{1,0:T(2,128)S(1)}, f32[2,128]{1,0:T(2,128)}, u32[]{:S(2)}) copy-start(f32[2,128]{1,0:T(2,128)} %param.20) | copy-start | bytes 3076
  139.1 116.1 %collective-permute-start.9 = (f32[1,3,1,32,128]{4,3,2,1,0:T(8,128)S(1)}, f32[1,3,1,32,128]{4,3,2,1,0:T(8,128)S(1)}, u32[]{:S(2)}, u32[]{:S(2)}) collective-permute-start(f32[1,3,1,32,128]{4,3,2,1,0:T(8,128)S(1)} %get-tuple-element.80), channel_id=1, source_target_pairs={{16,0},{32,16},{48,32},{64,48},{80,64},{96,80},{112,96},{128,112},... | collective-permute-start | bytes 147464 | tf_op jit(solution)/shard_map/ppermute | solution.py:18
  140.4 114.8 %collective-permute-start.8 = (f32[1,3,1,32,128]{4,3,2,1,0:T(8,128)S(1)}, f32[1,3,1,32,128]{4,3,2,1,0:T(8,128)S(1)}, u32[]{:S(2)}, u32[]{:S(2)}) collective-permute-start(f32[1,3,1,32,128]{4,3,2,1,0:T(8,128)S(1)} %get-tuple-element.79), channel_id=1, source_target_pairs={{0,16},{16,32},{32,48},{48,64},{64,80},{80,96},{96,112},{112,128},... | collective-permute-start | bytes 147464 | tf_op jit(solution)/shard_map/ppermute | solution.py:15
  255.3 6.7 collective-permute-start.11
  256.6 5.4 collective-permute-start.10
  496.7 100.4 %collective-permute-start.13 = (f32[1,3,1,32,128]{4,3,2,1,0:T(8,128)S(1)}, f32[1,3,1,32,128]{4,3,2,1,0:T(8,128)S(1)}, u32[]{:S(2)}, u32[]{:S(2)}) collective-permute-start(f32[1,3,1,32,128]{4,3,2,1,0:T(8,128)S(1)} %get-tuple-element.78), channel_id=1, source_target_pairs={{16,0},{32,16},{48,32},{64,48},{80,64},{96,80},{112,96},{128,112},... | collective-permute-start | bytes 147464 | tf_op jit(solution)/shard_map/ppermute | solution.py:18
  498.0 99.1 %collective-permute-start.12 = (f32[1,3,1,32,128]{4,3,2,1,0:T(8,128)S(1)}, f32[1,3,1,32,128]{4,3,2,1,0:T(8,128)S(1)}, u32[]{:S(2)}, u32[]{:S(2)}) collective-permute-start(f32[1,3,1,32,128]{4,3,2,1,0:T(8,128)S(1)} %get-tuple-element.77), channel_id=1, source_target_pairs={{0,16},{16,32},{32,48},{48,64},{64,80},{80,96},{96,112},{112,128},... | collective-permute-start | bytes 147464 | tf_op jit(solution)/shard_map/ppermute | solution.py:15
  597.1 6.4 collective-permute-start.15
  598.4 5.1 collective-permute-start.14
  608.3 173.3 %copy-start.40 = (s32[2]{0:T(128)S(1)}, s32[2]{0:T(128)}, u32[]{:S(2)}) copy-start(s32[2]{0:T(128)} %param.22) | copy-start | bytes 28
  (33 other events, 134.2 us)
where the time goes:
time: 784 us; the launch traced here: 783 us
  blocking collectives  698 us (89%)
  starting transfers between devices  43.8 us (6%)
  other arithmetic  16.7 us (2%)
  local copies, waits for them, and re-layouts  10.8 us (1%)
    all_gather x4, blocking collectives, gap_of(): rows = lax.all_gather(own, ('body', 'gx'), axis=0, tiled=True)  237 us
    psum x2, blocking collectives, global_sum(): return lax.psum(value, ('body', 'gx', 'gy'))  226 us
    unnamed x3, blocking collectives  118 us
    psum x1, blocking collectives, on_device(): lax.psum(jnp.sum(direction * image), ('body', 'gx', 'gy'))  118 us
    ppermute x8, starting transfers between devices, extended(): lax.ppermute(lax.slice_in_dim(block, block.shape[dim] - width, None, axis...  33.4 us
  transfers between devices with their start and end apart: 16, of which 2 were waited for; matrix products, arithmetic and copies ran while one was open for 2% of the time, Pallas kernels for 0%

commit v1 on v0

v1 whole, which is shorter than its diff:
```python
import jax
import jax.numpy as jnp
from jax import lax
from jax.experimental import pallas as pl
from jax.experimental.pallas import tpu as pltpu
from jax.sharding import PartitionSpec as P

HIGH = lax.Precision.HIGHEST
F32 = jnp.float32
LANES = 128
DEPTHS = (3, 3, 3, 3, 2, 2, 2, 2)
STARTS = (0, 3, 6, 9, 12, 14, 16, 18)
SLABS = 20
LINES = 14
ROWS = 48
KAP0, KAP1, DIA0, DIA1, RES0, IM0, IM1, SEC0, SEC1 = 0, 1, 2, 3, 4, 6, 7, 8, 9


def roll(value, step, axis):
    return pltpu.roll(value, step % value.shape[axis], axis)


def iota(shape, axis):
    return lax.broadcasted_iota(jnp.int32, shape, axis)


def call(body, outs, args, smem=(), scratch=()):
    specs = [
        pl.BlockSpec(memory_space=pltpu.SMEM if i in smem else pltpu.VMEM)
        for i in range(len(args))
    ]
    many = isinstance(outs, list)
    shapes = [jax.ShapeDtypeStruct(s, F32) for s in (outs if many else [outs])]
    vmem = pl.BlockSpec(memory_space=pltpu.VMEM)
    return pl.pallas_call(
        body,
        out_shape=shapes if many else shapes[0],
        in_specs=specs,
        out_specs=[vmem] * len(shapes) if many else vmem,
        scratch_shapes=[pltpu.VMEM(s, F32) for s in scratch],
        compiler_params=pltpu.CompilerParams(vmem_limit_bytes=40 * 1024 * 1024),
    )(*args)


def fill(out, block):
    for at in range(0, out.shape[0], 8):
        out[at : at + 8, :] = block


def stack_rows(pieces):
    return jnp.concatenate(pieces, axis=0)


def tile_lines(disp, force, kappa, sigma):
    return (
        lambda x: disp[0, 0, x],
        lambda x: disp[0, 1, x],
        lambda x: disp[0, 2, x],
        lambda x: kappa[0, x],
        lambda x: force[0, 0, x],
        lambda x: force[0, 1, x],
        lambda x: force[0, 2, x],
        lambda x: sigma[0, x],
    )


def pack_x(partner, disp, force, kappa, sigma, up, down, package):
    for line, depth, start in zip(tile_lines(disp, force, kappa, sigma), DEPTHS, STARTS):
        for k in range(depth):
            up[start + k] = line(8 - depth + k)
            down[start + k] = line(k)
    first = disp[0, 2, 0:4].reshape(LANES, LANES).T[0:1]
    second = disp[0, 2, 4:8].reshape(LANES, LANES).T[0:1]
    lane = iota((1, LANES), 1)
    hot = []
    for k in range(2):
        q = partner[k]
        hot.append(jnp.where(lane == 4 * (q // 2) + q % 2, 1.0, 0.0).astype(F32))
    four = stack_rows([first, second, hot[0], hot[1]])
    fill(package, stack_rows([four, four]))


def ext_line(line, low, high, field, x):
    depth, start = DEPTHS[field], STARTS[field]
    if x < 3:
        k = x - (3 - depth)
        return None if k < 0 else low[start + k]
    if x < 11:
        return line(x - 3)
    k = x - 11
    return None if k >= depth else high[start + k]


def pack_y(disp, force, kappa, sigma, low, high, up, down):
    lines = tile_lines(disp, force, kappa, sigma)
    sub = iota((8, LANES), 0)
    zero = jnp.zeros((8, LANES), F32)
    for x in range(LINES):
        last, first = [], []
        for field in range(8):
            value = ext_line(lines[field], low, high, field, x)
            last.append(zero if value is None else value[24:32])
            first.append(zero if value is None else value[0:8])
        for k, (a, b, c) in enumerate(((0, 1, 4), (2, 3, 5))):
            up[x, 8 * k : 8 * k + 8] = jnp.where(
                sub >= 5, last[a], jnp.where(sub >= 2, roll(last[b], -3, 0), roll(last[c], -6, 0))
            )
            down[x, 8 * k : 8 * k + 8] = jnp.where(
                sub < 3, first[a], jnp.where(sub < 6, roll(first[b], 3, 0), roll(first[c], 6, 0))
            )
        up[x, 16:24] = jnp.where(sub >= 6, last[7], roll(last[6], -2, 0))
        down[x, 16:24] = jnp.where(sub < 2, first[7], roll(first[6], 2, 0))


def mat_vec(matrix, row):
    return lax.dot_general(
        jnp.broadcast_to(row, (8, LANES)),
        matrix,
        (((1,), (1,)), ((), ())),
        precision=HIGH,
        preferred_element_type=F32,
    )[0:1]


def vec_mat(row, matrix):
    return lax.dot_general(
        jnp.broadcast_to(row, (8, LANES)),
        matrix,
        (((1,), (0,)), ((), ())),
        precision=HIGH,
        preferred_element_type=F32,
    )[0:1]


def surface_row(q):
    return 4 * (q // 2) + q % 2


def contact_first(partner, active, rows, gap0, pressure, mortar, state):
    gx = lax.axis_index("gx")
    half = rows.shape[0] // 2
    for k in range(2):
        own = rows[pl.ds(4 * gx + k, 1), :]
        master = rows[pl.ds(half + surface_row(partner[k]), 1), :]
        matrix = mortar[k]
        press = pressure[k : k + 1, :]
        flag = jnp.full((1, LANES), active[k], jnp.int32).astype(F32)
        gap = gap0[k : k + 1, :] - own - mat_vec(matrix, master)
        radius = jnp.sqrt(gap * gap + press * press + 0.01)
        complement = gap + press - radius
        slope_gap = 1.0 - gap / radius
        slope_press = 1.0 - press / radius
        divisor = slope_press + 0.5
        stiffness = flag * slope_gap / divisor
        excess = flag * complement / divisor
        traction = flag * press - excess
        state[k : k + 1, :] = stiffness
        state[2 + k : 3 + k, :] = complement
        state[4 + k : 5 + k, :] = slope_gap
        state[6 + k : 7 + k, :] = divisor
        state[8 + k : 9 + k, :] = flag
        state[10 + k : 11 + k, :] = press
        state[12 + k : 13 + k, :] = traction
        state[14 + k : 15 + k, :] = vec_mat(traction, matrix)


def base(
    disp, force, kappa, sigma, low_x, high_x, low_y, high_y, state,
    res_out, image_out, strips, moments, package,
    fields, diag, res, image, second, smooth_a, smooth_b, smooth_k,
):
    body, gx, gy = lax.axis_index("body"), lax.axis_index("gx"), lax.axis_index("gy")
    lines = tile_lines(disp, force, kappa, sigma)
    places = ((0, 0, 0), (0, 3, -3), (1, 0, 0), (1, 3, -3), (0, 6, -6), (1, 6, -6), (2, 2, -2), (2, 0, 0))
    for field in range(8):
        group, before, after = places[field]
        for x in range(LINES):
            value = ext_line(lines[field], low_x, high_x, field, x)
            if value is None:
                continue
            part = slice(8 * group, 8 * group + 8)
            fields[field, x, 0:8] = roll(low_y[x, part], before, 0)
            fields[field, x, 8:40] = value
            fields[field, x, 40:48] = roll(high_y[x, part], after, 0)
    lane = iota((ROWS, LANES), 1)
    row = iota((ROWS, LANES), 0)
    keep_low = jnp.where(lane > 0, 0.5, 0.0).astype(F32)
    keep_high = jnp.where(lane < LANES - 1, 0.5, 0.0).astype(F32)
    row_low = jnp.where(gy == 0, 8, 0)
    row_high = jnp.where(gy == lax.axis_size("gy") - 1, 40, ROWS)
    inside_y = jnp.where((row >= row_low) & (row < row_high), 1.0, 0.0).astype(F32)
    line_low = jnp.where(gx == 0, 3, 0)
    line_high = jnp.where(gx == lax.axis_size("gx") - 1, 11, LINES)

    def in_plane(value):
        value = value + keep_low * roll(value, 1, 1) + keep_high * roll(value, -1, 1)
        return value + 0.5 * (roll(value, 1, 0) + roll(value, -1, 0))

    def along(ref, *at):
        *lead, x = at
        return ref[(*lead, x)] + 0.5 * (ref[(*lead, x - 1)] + ref[(*lead, x + 1)])

    def inside(x):
        return inside_y * jnp.where((x >= line_low) & (x < line_high), 1.0, 0.0).astype(F32)

    @pl.loop(0, LINES)
    def _(x):
        kap = fields[3, x]
        smooth_k[x] = in_plane(kap)
        for c in range(3):
            value = fields[c, x]
            smooth_a[c, x] = in_plane(value)
            smooth_b[c, x] = in_plane(kap * value)

    @pl.loop(1, LINES - 1)
    def _(x):
        kap = fields[3, x]
        dia = fields[7, x] + 8.0 * kap + along(smooth_k, x)
        diag[x] = dia
        mask = inside(x)
        for c in range(3):
            value = fields[4 + c, x] - (
                dia * fields[c, x] - kap * along(smooth_a, c, x) - along(smooth_b, c, x)
            )
            res[c, x] = mask * value

    @pl.loop(1, LINES - 1)
    def _(x):
        kap = fields[3, x]
        for c in range(3):
            value = res[c, x]
            smooth_a[c, x] = in_plane(value)
            smooth_b[c, x] = in_plane(kap * value)

    @pl.loop(2, LINES - 2)
    def _(x):
        kap = fields[3, x]
        dia = diag[x]
        mask = inside(x)
        for c in range(3):
            image[c, x] = mask * (
                dia * res[c, x] - kap * along(smooth_a, c, x) - along(smooth_b, c, x)
            )

    @pl.loop(2, LINES - 2)
    def _(x):
        kap = fields[3, x]
        for c in range(3):
            value = image[c, x]
            smooth_a[c, x] = in_plane(value)
            smooth_b[c, x] = in_plane(kap * value)

    def finish(k, sums):
        x = k + 3
        kap = fields[3, x]
        dia = diag[x]
        sums = list(sums)
        for c in range(3):
            r, p = res[c, x, 8:40], image[c, x, 8:40]
            q = (dia * image[c, x] - kap * along(smooth_a, c, x) - along(smooth_b, c, x))[8:40]
            if c == 2:
                second[k] = q
            res_out[c, k] = r
            image_out[c, k] = p
            for i, (a, b) in enumerate(((r, r), (r, p), (p, p), (p, q))):
                product = (a * b).reshape(4, 8, LANES)
                sums[i] = sums[i] + ((product[0] + product[1]) + (product[2] + product[3]))
        return tuple(sums)

    sums = lax.fori_loop(0, 8, finish, (jnp.zeros((8, LANES), F32),) * 4)
    for i in range(4):
        moments[i] = sums[i]
    strips[...] = jnp.zeros(strips.shape, F32)
    lanes = iota((LANES, LANES), 1)
    for group in range(4):
        near = [min(max(4 * group - 1 + k, 1), LINES - 2) for k in range(4)]
        wide = stack_rows([fields[3, x, 8:40] for x in near])
        wide = jnp.where(lanes < 2, wide, roll(stack_rows([diag[x, 8:40] for x in near]), 2, 1))
        count = 4
        if group in (1, 2):
            count = 10
            for at, piece in (
                (4, stack_rows([res[2, x, 8:40] for x in near])),
                (6, stack_rows([image[2, x, 8:40] for x in near])),
                (8, stack_rows([second[x - 3] for x in near])),
            ):
                wide = jnp.where(lanes < at, wide, roll(piece, at, 1))
        turned = wide.T
        for kind in range(count):
            strips[kind, group : group + 1, :] = turned[kind : kind + 1]
        if group in (1, 2):
            k = group - 1
            send = jnp.where(body == 1, state[14 + k : 15 + k, :], state[12 + k : 13 + k, :])
            if k == 0:
                sent, surface = [send], [turned[RES0 : RES0 + 1]]
            else:
                sent.append(send)
                surface.append(turned[RES0 : RES0 + 1])
    four = stack_rows(surface + sent)
    fill(package, stack_rows([four, four]))


def spread_row(select_rows, rows):
    half = rows.shape[0] // 2
    index = iota((half, LANES), 0) % 4
    select = jnp.where(index >= 2, select_rows[half:, :], 0.0)
    master = -lax.dot_general(
        select,
        rows[half:, :],
        (((0,), (0,)), ((), ())),
        precision=HIGH,
        preferred_element_type=F32,
    )[:half]
    slave = jnp.where(index < 2, -roll(rows[:half, :], -2, 0), 0.0)
    return slave, master


def own_extended(padded, gx):
    return stack_rows(
        [
            padded[pl.ds(4 * gx + 5, 1), :],
            padded[pl.ds(4 * gx + 8, 2), :],
            padded[pl.ds(4 * gx + 12, 1), :],
            jnp.zeros((4, LANES), F32),
        ]
    )


def put_padded(padded, value):
    half = value.shape[0]
    padded[0:8, :] = jnp.zeros((8, LANES), F32)
    padded[8 : 8 + half, :] = value
    padded[8 + half : 16 + half, :] = jnp.zeros((8, LANES), F32)


def contact_second(partner, select_rows, rows, state, mortar, strips, edges, out, padded, surf0, surf1):
    body, gx = lax.axis_index("body"), lax.axis_index("gx")
    half = rows.shape[0] // 2
    slave, master = spread_row(select_rows, rows)
    put_padded(padded, jnp.where(body == 0, slave, master))
    surf0[...] = rows[:half, :] + slave
    surf1[...] = rows[half:, :] + master
    first = own_extended(padded, gx)
    edges[0:8, :] = first
    edges[8:16, :] = strips[KAP0] * first
    for k in range(2):
        matrix = mortar[k]
        gap = -surf0[pl.ds(4 * gx + k, 1), :] - mat_vec(
            matrix, surf1[pl.ds(surface_row(partner[k]), 1), :]
        )
        push = state[k : k + 1, :] * gap
        pulled = vec_mat(push, matrix)
        out[k : k + 1, :] = gap
        out[2 + k : 3 + k, :] = push
        out[4 + k : 5 + k, :] = jnp.where(body == 1, pulled, push)
        out[6 + k : 7 + k, :] = strips[IM0, 1 + k : 2 + k, :]


def line_smooth(value):
    lane = iota(value.shape, 1)
    back, ahead = roll(value, 32, 1), roll(value, -32, 1)
    back = jnp.where(lane >= 32, back, roll(back, 1, 0))
    ahead = jnp.where(lane < 96, ahead, roll(ahead, -1, 0))
    return value + 0.5 * (back + ahead)


def row_smooth(value, low=None, high=None):
    y = iota(value.shape, 1) % 32
    before = 0.0 if low is None else roll(low, -31, 1)
    after = 0.0 if high is None else roll(high, 31, 1)
    before = jnp.where(y > 0, roll(value, 1, 1), before)
    after = jnp.where(y < 31, roll(value, -1, 1), after)
    return value + 0.5 * (before + after)


def couple(edges, low, high, strips, second, moved, package):
    gx = lax.axis_index("gx")
    first = edges[0:8, :]
    plain = line_smooth(row_smooth(first, low[0:8, :], high[0:8, :]))
    weighted = line_smooth(row_smooth(edges[8:16, :], low[8:16, :], high[8:16, :]))
    row = iota((8, LANES), 0)
    lowest = jnp.where(gx == 0, 1, 0)
    highest = jnp.where(gx == lax.axis_size("gx") - 1, 3, 4)
    mask = (row >= lowest) & (row < highest)
    kap0 = strips[KAP0]
    top = jnp.where(mask, strips[DIA0] * first - kap0 * plain - weighted, 0.0)
    below = jnp.where(mask, -0.5 * (strips[KAP1] * plain + weighted), 0.0)
    moved[0:8, :] = top
    moved[8:16, :] = below
    four = stack_rows([second[6:8, :] + top[1:3], second[4:6, :]])
    fill(package, stack_rows([four, four]))


def total(value):
    return jnp.sum(jnp.sum(value, axis=1, keepdims=True), axis=0, keepdims=True)


def measure_moments(
    partner, select_rows, rows, state, mortar, strips, edges, second, moved, moments,
    package, image_out, padded, surf0, surf1,
):
    body, gx = lax.axis_index("body"), lax.axis_index("gx")
    half = rows.shape[0] // 2
    slave, master = spread_row(select_rows, rows)
    put_padded(padded, jnp.where(body == 0, slave, master))
    surf0[...] = rows[:half, :] + slave
    surf1[...] = rows[half:, :] + master
    first = edges[0:8, :]
    k_first = moved[0:8, :]
    top = k_first + own_extended(padded, gx)
    below = moved[8:16, :]
    once = jnp.where(body == 0, 1.0, 0.0).astype(F32)
    push_sum = jnp.zeros((1, LANES), F32)
    gap_sum = jnp.zeros((1, LANES), F32)
    for k in range(2):
        gap = -surf0[pl.ds(4 * gx + k, 1), :] - mat_vec(
            mortar[k], surf1[pl.ds(surface_row(partner[k]), 1), :]
        )
        image_out[k : k + 1, :] = gap
        push_sum = push_sum + second[k : k + 1, :] * second[2 + k : 3 + k, :]
        gap_sum = gap_sum + state[k : k + 1, :] * gap * gap
    image_out[2:8, :] = jnp.zeros((6, LANES), F32)
    image_out[8:16, :] = top
    image_out[16:24, :] = below
    row = iota((8, LANES), 0)
    own = (row == 1) | (row == 2)
    kap0, kap1 = strips[KAP0], strips[KAP1]

    def surface_sum(value):
        return total(jnp.where(own, value, 0.0))

    im0, im1 = strips[IM0], strips[IM1]
    mu0 = total(moments[0]) + surface_sum(first * (2.0 * strips[RES0] + first))
    mu1 = total(moments[1]) + surface_sum(first * (2.0 * im0 + k_first)) + once * total(push_sum)
    mu2 = total(moments[2]) + surface_sum(top * (2.0 * im0 + top) + below * (2.0 * im1 + below))
    t_top = line_smooth(row_smooth(top + 0.5 * below))
    t_below = line_smooth(row_smooth(0.5 * top + below))
    mu3 = (
        total(moments[3])
        + surface_sum(
            top * (2.0 * strips[SEC0] + strips[DIA0] * top - 2.0 * kap0 * t_top)
            + below * (2.0 * strips[SEC1] + strips[DIA1] * below - 2.0 * kap1 * t_below)
        )
        + once * total(gap_sum)
    )
    lane = iota((8, LANES), 1)
    y = lane % 32
    send = jnp.zeros((8, LANES), F32)
    for k, value in enumerate((top, below, kap0 * top, kap1 * below)):
        send = send + jnp.where(y == 2 * k, roll(value, 2 * k, 1), 0.0)
        send = send + jnp.where(y == 2 * k + 1, roll(value, 2 * k + 1 - 31, 1), 0.0)
    for k, value in enumerate((mu0, mu1, mu2, mu3)):
        send = send + jnp.where((row == 0) & (lane == 16 + k), value, 0.0)
    send = send[0:4]
    fill(package, stack_rows([send, send]))


def reduce_column(rows, package):
    value = rows[...]
    count = value.shape[0]
    row, lane = iota(value.shape, 0), iota(value.shape, 1)
    place = row % 4
    following = roll(value, -4, 0)
    upper = [roll(value, -(2 * k + 1), 1) for k in range(4)]
    lower = [roll(following, -2 * k, 1) for k in range(4)]
    across = (
        upper[2] * line_smooth(lower[0] + 0.5 * lower[1])
        + upper[3] * line_smooth(0.5 * lower[0] + lower[1])
        + upper[0] * line_smooth(lower[2] + 0.5 * lower[3])
        + upper[1] * line_smooth(0.5 * lower[2] + lower[3])
    )
    counted = ((place == 1) | (place == 2)) & (lane % 32 == 0) & (row < count - 4)
    across = total(jnp.where(counted, across, 0.0))
    sums = jnp.sum(jnp.where(place == 0, value, 0.0), axis=0, keepdims=True)
    lane1 = iota((1, LANES), 1)
    sums = jnp.where((lane1 >= 16) & (lane1 < 20), sums, 0.0)
    sums = sums - jnp.where(lane1 == 19, across, 0.0)
    index = iota((8, LANES), 0)
    fill(package, jnp.where(index % 2 == 0, sums, 0.0))


def finish(rows, res, image, state, edges, second, last, increment, new_press):
    sums = jnp.sum(rows[...], axis=0, keepdims=True)
    lane = iota((1, LANES), 1)
    m0, m1, m2, m3 = [
        jnp.sum(jnp.where(lane == 16 + k, sums, 0.0), axis=1, keepdims=True) for k in range(4)
    ]
    alpha = m0 / m1
    left = alpha * alpha * m2 - m0
    beta = left / m0
    energy = (m1 - 2.0 * alpha * m2 + alpha * alpha * m3) - beta * left / alpha
    step = left / energy
    c_res = alpha + step * (1.0 + beta)
    c_im = -step * alpha
    for k in range(2):
        at = slice(k, k + 1)
        change = c_res * second[at, :] + c_im * last[at, :]
        press = state[10 + k : 11 + k, :]
        flag = state[8 + k : 9 + k, :]
        complement, slope = state[2 + k : 3 + k, :], state[4 + k : 5 + k, :]
        divisor = state[6 + k : 7 + k, :]
        new_press[at, :] = flag * (press - (complement + slope * change) / divisor)
    wide_res = jnp.broadcast_to(c_res, (8, LANES)).reshape(1, 8, LANES)
    wide_im = jnp.broadcast_to(c_im, (8, LANES)).reshape(1, 8, LANES)
    for c in range(3):
        for x in range(8):
            r = res[c, x].reshape(4, 8, LANES)
            p = image[c, x].reshape(4, 8, LANES)
            increment[0, c, x] = (wide_res * r + wide_im * p).reshape(32, LANES)
    for k in range(2):
        top = c_res * edges[1 + k : 2 + k, :] + c_im * last[9 + k : 10 + k, :]
        below = c_im * last[17 + k : 18 + k, :]
        wide = stack_rows([top, below, jnp.zeros((LANES - 2, LANES), F32)]).T
        for x in range(4):
            at = 4 * k + x
            increment[0, 2, at] = increment[0, 2, at] + wide[32 * x : 32 * x + 32]


def shifted(block, axis, step):
    count = lax.axis_size(axis)
    pairs = [(i, i + step) for i in range(count) if 0 <= i + step < count]
    return lax.ppermute(block, axis, pairs)


def on_device(disp, force, kappa, sigma, gap0, pressure, mortar, partner, active):
    nx, ny = lax.axis_size("gx"), lax.axis_size("gy")
    tile = (disp, force, kappa, sigma)
    whole = (8 * nx, LANES)
    row = ("body", "gx")

    def trade(package, axes):
        return lax.all_to_all(package, axes, 0, 0, tiled=True)

    slabs = (SLABS, 32, LANES)
    up, down, package = call(pack_x, [slabs, slabs, whole], (partner, *tile), smem=(0,))
    low_x, high_x = shifted(up, "gx", 1), shifted(down, "gx", -1)
    surfaces = trade(package, row)
    rims = (LINES, 24, LANES)
    up, down = call(pack_y, [rims, rims], (*tile, low_x, high_x))
    low_y, high_y = shifted(up, "gy", 1), shifted(down, "gy", -1)
    state = call(
        contact_first,
        (16, LANES),
        (partner, active, surfaces, gap0, pressure, mortar),
        smem=(0, 1),
    )
    lines = (LINES, ROWS, LANES)
    res, image, strips, moments, package = call(
        base,
        [(3, 8, 32, LANES), (3, 8, 32, LANES), (16, 8, LANES), (4, 8, LANES), whole],
        (*tile, low_x, high_x, low_y, high_y, state),
        scratch=[(8, *lines), lines, (3, *lines), (3, *lines), (8, 32, LANES), (3, *lines), (3, *lines), lines],
    )
    rows = trade(package, row)
    half = 4 * nx
    work = [(half + 16, LANES), (half, LANES), (half, LANES)]
    edges, second = call(
        contact_second,
        [(16, LANES), (8, LANES)],
        (partner, surfaces, rows, state, mortar, strips),
        smem=(0,),
        scratch=work,
    )
    low, high = shifted(edges, "gy", 1), shifted(edges, "gy", -1)
    moved, package = call(
        couple, [(16, LANES), whole], (edges, low, high, strips, second)
    )
    rows = trade(package, row)
    package, last = call(
        measure_moments,
        [(4 * ny, LANES), (24, LANES)],
        (partner, surfaces, rows, state, mortar, strips, edges, second, moved, moments),
        smem=(0,),
        scratch=work,
    )
    package = call(reduce_column, (4 * nx, LANES), (trade(package, "gy"),))
    sums = trade(package, row)
    increment, new_press = call(
        finish,
        [disp.shape, gap0.shape],
        (sums, res, image, state, edges, second, last),
    )
    return (increment, new_press)


def solution(mesh):
    placed = (
        P("body", None, "gx", "gy", None),
        P("body", None, "gx", "gy", None),
        P("body", "gx", "gy", None),
        P("body", "gx", "gy", None),
        P(("gx", "gy"), None),
        P(("gx", "gy"), None),
        P(("gx", "gy"), None, None),
        P(("gx", "gy")),
        P(("gx", "gy")),
    )
    return jax.shard_map(
        on_device,
        mesh=mesh,
        in_specs=placed,
        out_specs=(P("body", None, "gx", "gy", None), P(("gx", "gy"), None)),
        check_vma=False,
    )
```

time: 784 us -> 138 us (0.18)
  blocking collectives: 698 us -> 73.8 us
  other arithmetic: 16.7 us -> 0 us
  Pallas kernels: 0 us -> 14.6 us
  starting transfers between devices: 43.8 us -> 33.9 us
  waiting for transfers between devices: 1.14 us -> 9.69 us
    psum x3 -> x0, blocking collectives: 343 us -> none  [the longest x2 226 us: global_sum(): return lax.psum(value, ('body', 'gx', 'gy'))]
    all_gather x4 -> x0, blocking collectives: 237 us -> none  [gap_of(): rows = lax.all_gather(own, ('body', 'gx'), axis=0, tiled=True)]
    unnamed x3 -> x0, blocking collectives: 118 us -> none
    all_to_all x0 -> x4, blocking collectives: none -> 73.8 us  [trade(): return lax.all_to_all(package, axes, 0, 0, tiled=True)]
    ppermute x16 -> x6, starting transfers between devices: 43.8 us -> 15.7 us  [shifted(): return lax.ppermute(block, axis, pairs)]
    all_to_all x0 -> x1, starting transfers between devices: none -> 18.1 us  [trade(): return lax.all_to_all(package, axes, 0, 0, tiled=True)]
    pallas_call x0 -> x9, Pallas kernels: none -> 14.6 us  [call(): pl.pallas_call(body, out_shape=shapes if many else shapes[0], in_specs=sp...]
    all_to_all x0 -> x1, waiting for transfers between devices: none -> 8.91 us  [trade(): return lax.all_to_all(package, axes, 0, 0, tiled=True)]
  transfers between devices with their start and end apart: 16 -> 7, of which waited for: 2 -> 2; matrix products, arithmetic and copies ran while one was open for 2% -> 0% of each run, Pallas kernels for 0% -> 1%
where the time goes in v1:
time: 138 us; the launch traced here: 137 us
  blocking collectives  73.8 us (53%)
  starting transfers between devices  33.9 us (25%)
  Pallas kernels  14.6 us (11%)
  waiting for transfers between devices  9.69 us (7%)
  local copies, waits for them, and re-layouts  4.49 us (3%)
    all_to_all x4, blocking collectives, trade(): return lax.all_to_all(package, axes, 0, 0, tiled=True)  73.8 us
    all_to_all x1, starting transfers between devices, trade(): return lax.all_to_all(package, axes, 0, 0, tiled=True)  18.1 us
    ppermute x6, starting transfers between devices, shifted(): return lax.ppermute(block, axis, pairs)  15.7 us
    pallas_call x9, Pallas kernels, call(): pl.pallas_call(body, out_shape=shapes if many else shapes[0], in_specs=sp...  14.6 us
    all_to_all x1, waiting for transfers between devices, trade(): return lax.all_to_all(package, axes, 0, 0, tiled=True)  8.91 us
    unnamed x28, local copies, waits for them, and re-layouts  4.49 us
  transfers between devices with their start and end apart: 7, of which 2 were waited for; matrix products, arithmetic and copies ran while one was open for 0% of the time, Pallas kernels for 1%

profile of v1, /device:TPU:1, one launch (start us, length us, event | category | flops | bytes accessed | tf_op | source)
XLA Modules:
  0.0 137.3 jit_solution(17671540192563242237)
XLA Ops:
  0.6 1.0 copy-done
  1.6 1.0 copy-done.2
  2.6 0.9 copy-done.5
  3.5 0.9 copy-done.7
  4.4 0.7 copy-done.9
  5.1 1.3 shard_map.104
  6.4 4.5 %collective-permute-start = (f32[20,32,128]{2,1,0:T(8,128)S(1)}, f32[20,32,128]{2,1,0:T(8,128)S(1)}, u32[]{:S(2)}, u32[]{:S(2)}) collective-permute-start(f32[20,32,128]{2,1,0:T(8,128)S(1)} %get-tuple-element.19), channel_id=1, source_target_pairs={{0,16},{16,32},{32,48},{48,64},{64,80},{80,96},{96,112},{112,128},... | collective-permute-start | bytes 983048 | tf_op jit(solution)/shard_map/ppermute | solution.py:522
  10.9 1.3 collective-permute-start.1
  12.2 18.1 %all-to-all-start = ((f32[32,4,128]{2,1,0:T(4,128)}), f32[32,4,128]{2,1,0:T(4,128)S(1)}, u32[]{:S(2)}, u32[]{:S(2)}) async-start(f32[32,4,128]{2,1,0:T(4,128)} %bitcast), calls=%async_computation | async-start | bytes 131072 | tf_op jit(solution)/shard_map/all_to_all | solution.py:532
  30.5 3.2 %collective-permute-start.2 = (f32[14,24,128]{2,1,0:T(8,128)S(1)}, f32[14,24,128]{2,1,0:T(8,128)S(1)}, u32[]{:S(2)}, u32[]{:S(2)}) collective-permute-start(f32[14,24,128]{2,1,0:T(8,128)S(1)} %get-tuple-element.21), channel_id=1, source_target_pairs={{0,1},{1,2},{2,3},{3,4},{4,5},{5,6},{6,7},{7,8},{8,9},{9,10},{10,1... | collective-permute-start | bytes 516104 | tf_op jit(solution)/shard_map/ppermute | solution.py:522
  33.7 1.4 %collective-permute-start.3 = (f32[14,24,128]{2,1,0:T(8,128)S(1)}, f32[14,24,128]{2,1,0:T(8,128)S(1)}, u32[]{:S(2)}, u32[]{:S(2)}) collective-permute-start(f32[14,24,128]{2,1,0:T(8,128)S(1)} %get-tuple-element.22), channel_id=1, source_target_pairs={{1,0},{2,1},{3,2},{4,3},{5,4},{6,5},{7,6},{8,7},{9,8},{10,9},{11,1... | collective-permute-start | bytes 516104 | tf_op jit(solution)/shard_map/ppermute | solution.py:522
  35.2 8.9 %all-to-all-done = f32[32,4,128]{2,1,0:T(4,128)S(1)} async-done(((f32[32,4,128]{2,1,0:T(4,128)}), f32[32,4,128]{2,1,0:T(4,128)S(1)}, u32[]{:S(2)}, u32[]{:S(2)}) %all-to-all-start) | async-done | bytes 65568 | tf_op jit(solution)/shard_map/all_to_all | solution.py:532
  44.1 1.5 %shard_map.106.state = f32[16,128]{1,0:T(8,128)S(1)} custom-call(s32[2]{0:T(128)S(1)} %copy-done.10, s32[2]{0:T(128)S(1)} %copy-done.13, f32[128,128]{1,0:T(8,128)S(1)} %bitcast.10, f32[2,128]{1,0:T(2,128)S(1)} %copy-done.11, f32[2,128]{1,0:T(2,128)S(1)} %copy-done.12, f32[2,128,128]{2,1,0:T(8,128)S(1)} %copy-done.4), custom_call_target="tpu_custom_call" | custom-call | tf_op jit(solution)/shard_map/pallas_call | solution.py:35
  45.6 7.4 %shard_map.107 = (f32[3,8,32,128]{3,2,1,0:T(8,128)S(1)}, f32[3,8,32,128]{3,2,1,0:T(8,128)S(1)}, f32[16,8,128]{2,1,0:T(8,128)S(1)}, f32[4,8,128]{2,1,0:T(8,128)S(1)}, f32[128,128]{1,0:T(8,128)S(1)}) custom-call(f32[1,3,8,32,128]{4,3,2,1,0:T(8,128)S(1)} %copy-done.1, f32[1,3,8,32,128]{4,3,2,1,0:T(8,128)S(1)} %copy-done.3, f32[1,8,32,128]{3,2,1,0:T(8,128)S(1)} %copy-done.6, ...), custom_call_target="tpu_custom_call" | custom-call | tf_op jit(solution)/shard_map/pallas_call | solution.py:35
  53.0 22.3 %all_to_all.55 = f32[32,4,128]{2,1,0:T(4,128)S(1)} all-to-all(f32[32,4,128]{2,1,0:T(4,128)S(1)} %bitcast.18), channel_id=1, replica_groups=mesh['body'=2,'gx'=16,'gy'=16] {'body','gx'}, dimensions={0} | all-to-all | bytes 131072 | tf_op jit(solution)/shard_map/all_to_all | solution.py:532
  75.3 1.7 %shard_map.108 = (f32[16,128]{1,0:T(8,128)S(1)}, f32[8,128]{1,0:T(8,128)S(1)}) custom-call(s32[2]{0:T(128)S(1)} %copy-done.10, f32[128,128]{1,0:T(8,128)S(1)} %bitcast.11, f32[128,128]{1,0:T(8,128)S(1)} %bitcast.14, f32[16,128]{1,0:T(8,128)S(1)} %shard_map.106.state, f32[2,128,128]{2,1,0:T(8,128)S(1)} %copy-done.4, f32[16,8,128]{2,1,0:T(8,128)S(1)} %get-tuple-element.24.strips), custom_call_target="tpu_custom_call" | custom-call | tf_op jit(solution)/shard_map/pallas_call | solution.py:35
  77.0 1.3 collective-permute-start.5
  78.3 4.0 %collective-permute-start.4 = (f32[16,128]{1,0:T(8,128)S(1)}, f32[16,128]{1,0:T(8,128)S(1)}, u32[]{:S(2)}, u32[]{:S(2)}) collective-permute-start(f32[16,128]{1,0:T(8,128)S(1)} %get-tuple-element.25.edges), channel_id=1, source_target_pairs={{0,1},{1,2},{2,3},{3,4},{4,5},{5,6},{6,7},{7,8},{8,9},{9,10},{10,1... | collective-permute-start | bytes 24584 | tf_op jit(solution)/shard_map/ppermute | solution.py:522
  82.3 0.8 collective-permute-done.4.low
  83.2 17.6 %all_to_all.56 = f32[32,4,128]{2,1,0:T(4,128)S(1)} all-to-all(f32[32,4,128]{2,1,0:T(4,128)S(1)} %bitcast.19), channel_id=1, replica_groups=mesh['body'=2,'gx'=16,'gy'=16] {'body','gx'}, dimensions={0} | all-to-all | bytes 131072 | tf_op jit(solution)/shard_map/all_to_all | solution.py:532
  100.8 1.2 shard_map.110
  102.0 17.4 %all_to_all.57 = f32[16,4,128]{2,1,0:T(4,128)S(1)} all-to-all(f32[16,4,128]{2,1,0:T(4,128)S(1)} %bitcast.20), channel_id=1, replica_groups=mesh['body'=2,'gx'=16,'gy'=16] {'gy'}, dimensions={0} | all-to-all | bytes 65536 | tf_op jit(solution)/shard_map/all_to_all | solution.py:532
  119.8 16.6 %all_to_all.58 = f32[32,2,128]{2,1,0:T(2,128)S(1)} all-to-all(f32[32,2,128]{2,1,0:T(2,128)S(1)} %bitcast.16), channel_id=1, replica_groups=mesh['body'=2,'gx'=16,'gy'=16] {'body','gx'}, dimensions={0} | all-to-all | bytes 65536 | tf_op jit(solution)/shard_map/all_to_all | solution.py:532
  136.3 1.0 shard_map.112
  (31 shorter events, 0.6 us)
Async XLA Ops:
  0.6 1.0 copy-start
  1.6 1.0 copy-start.2
  2.6 0.9 copy-start.5
  3.5 0.9 copy-start.7
  4.4 0.7 copy-start.9
  5.1 25.3 %copy-start.1 = (f32[1,3,8,32,128]{4,3,2,1,0:T(8,128)S(1)}, f32[1,3,8,32,128]{4,3,2,1,0:T(8,128)}, u32[]{:S(2)}) copy-start(f32[1,3,8,32,128]{4,3,2,1,0:T(8,128)} %disp.5) | copy-start | bytes 1179652
  5.1 25.3 %copy-start.3 = (f32[1,3,8,32,128]{4,3,2,1,0:T(8,128)S(1)}, f32[1,3,8,32,128]{4,3,2,1,0:T(8,128)}, u32[]{:S(2)}) copy-start(f32[1,3,8,32,128]{4,3,2,1,0:T(8,128)} %force.5) | copy-start | bytes 1179652
  5.1 25.3 %copy-start.8 = (f32[1,8,32,128]{3,2,1,0:T(8,128)S(1)}, f32[1,8,32,128]{3,2,1,0:T(8,128)}, u32[]{:S(2)}) copy-start(f32[1,8,32,128]{3,2,1,0:T(8,128)} %sigma.5) | copy-start | bytes 393220
  6.3 24.0 %copy-start.6 = (f32[1,8,32,128]{3,2,1,0:T(8,128)S(1)}, f32[1,8,32,128]{3,2,1,0:T(8,128)}, u32[]{:S(2)}) copy-start(f32[1,8,32,128]{3,2,1,0:T(8,128)} %kappa.5) | copy-start | bytes 393220
  6.4 24.0 %collective-permute-start = (f32[20,32,128]{2,1,0:T(8,128)S(1)}, f32[20,32,128]{2,1,0:T(8,128)S(1)}, u32[]{:S(2)}, u32[]{:S(2)}) collective-permute-start(f32[20,32,128]{2,1,0:T(8,128)S(1)} %get-tuple-element.19), channel_id=1, source_target_pairs={{0,16},{16,32},{32,48},{48,64},{64,80},{80,96},{96,112},{112,128},... | collective-permute-start | bytes 983048 | tf_op jit(solution)/shard_map/ppermute | solution.py:522
  10.9 19.5 %collective-permute-start.1 = (f32[20,32,128]{2,1,0:T(8,128)S(1)}, f32[20,32,128]{2,1,0:T(8,128)S(1)}, u32[]{:S(2)}, u32[]{:S(2)}) collective-permute-start(f32[20,32,128]{2,1,0:T(8,128)S(1)} %get-tuple-element.20), channel_id=1, source_target_pairs={{16,0},{32,16},{48,32},{64,48},{80,64},{96,80},{112,96},{128,112},... | collective-permute-start | bytes 983048 | tf_op jit(solution)/shard_map/ppermute | solution.py:522
  12.2 31.9 %all-to-all-start = ((f32[32,4,128]{2,1,0:T(4,128)}), f32[32,4,128]{2,1,0:T(4,128)S(1)}, u32[]{:S(2)}, u32[]{:S(2)}) async-start(f32[32,4,128]{2,1,0:T(4,128)} %bitcast), calls=%async_computation | async-start | bytes 131072 | tf_op jit(solution)/shard_map/all_to_all | solution.py:532
  30.3 13.8 %copy-start.4 = (f32[2,128,128]{2,1,0:T(8,128)S(1)}, f32[2,128,128]{2,1,0:T(8,128)}, u32[]{:S(2)}) copy-start(f32[2,128,128]{2,1,0:T(8,128)} %mortar.5) | copy-start | bytes 393220
  30.5 15.2 %collective-permute-start.2 = (f32[14,24,128]{2,1,0:T(8,128)S(1)}, f32[14,24,128]{2,1,0:T(8,128)S(1)}, u32[]{:S(2)}, u32[]{:S(2)}) collective-permute-start(f32[14,24,128]{2,1,0:T(8,128)S(1)} %get-tuple-element.21), channel_id=1, source_target_pairs={{0,1},{1,2},{2,3},{3,4},{4,5},{5,6},{6,7},{7,8},{8,9},{9,10},{10,1... | collective-permute-start | bytes 516104 | tf_op jit(solution)/shard_map/ppermute | solution.py:522
  33.7 10.4 %copy-start.12 = (f32[2,128]{1,0:T(2,128)S(1)}, f32[2,128]{1,0:T(2,128)}, u32[]{:S(2)}) copy-start(f32[2,128]{1,0:T(2,128)} %pressure.1) | copy-start | bytes 3076
  33.7 10.4 %copy-start.13 = (s32[2]{0:T(128)S(1)}, s32[2]{0:T(128)}, u32[]{:S(2)}) copy-start(s32[2]{0:T(128)} %active.1) | copy-start | bytes 28
  33.7 10.4 %copy-start.10 = (s32[2]{0:T(128)S(1)}, s32[2]{0:T(128)}, u32[]{:S(2)}) copy-start(s32[2]{0:T(128)} %partner.7) | copy-start | bytes 28
  33.7 10.4 %copy-start.11 = (f32[2,128]{1,0:T(2,128)S(1)}, f32[2,128]{1,0:T(2,128)}, u32[]{:S(2)}) copy-start(f32[2,128]{1,0:T(2,128)} %gap0.1) | copy-start | bytes 3076
  33.7 11.9 %collective-permute-start.3 = (f32[14,24,128]{2,1,0:T(8,128)S(1)}, f32[14,24,128]{2,1,0:T(8,128)S(1)}, u32[]{:S(2)}, u32[]{:S(2)}) collective-permute-start(f32[14,24,128]{2,1,0:T(8,128)S(1)} %get-tuple-element.22), channel_id=1, source_target_pairs={{1,0},{2,1},{3,2},{4,3},{5,4},{6,5},{7,6},{8,7},{9,8},{10,9},{11,1... | collective-permute-start | bytes 516104 | tf_op jit(solution)/shard_map/ppermute | solution.py:522
  77.0 5.3 %collective-permute-start.5 = (f32[16,128]{1,0:T(8,128)S(1)}, f32[16,128]{1,0:T(8,128)S(1)}, u32[]{:S(2)}, u32[]{:S(2)}) collective-permute-start(f32[16,128]{1,0:T(8,128)S(1)} %get-tuple-element.25.edges), channel_id=1, source_target_pairs={{1,0},{2,1},{3,2},{4,3},{5,4},{6,5},{7,6},{8,7},{9,8},{10,9},{11,1... | collective-permute-start | bytes 24584 | tf_op jit(solution)/shard_map/ppermute | solution.py:522
  78.3 4.8 %collective-permute-start.4 = (f32[16,128]{1,0:T(8,128)S(1)}, f32[16,128]{1,0:T(8,128)S(1)}, u32[]{:S(2)}, u32[]{:S(2)}) collective-permute-start(f32[16,128]{1,0:T(8,128)S(1)} %get-tuple-element.25.edges), channel_id=1, source_target_pairs={{0,1},{1,2},{2,3},{3,4},{4,5},{5,6},{6,7},{7,8},{8,9},{9,10},{10,1... | collective-permute-start | bytes 24584 | tf_op jit(solution)/shard_map/ppermute | solution.py:522

commit v2 on v1

--- a/solution.py
+++ b/solution.py
@@ -24,21 +24,21 @@
     return lax.broadcasted_iota(jnp.int32, shape, axis)
 
 
-def call(body, outs, args, smem=(), scratch=()):
-    specs = [
-        pl.BlockSpec(memory_space=pltpu.SMEM if i in smem else pltpu.VMEM)
-        for i in range(len(args))
-    ]
+def call(body, outs, args, smem=(), away=(), scratch=(), more=(), limit=40, put=pltpu.VMEM):
+    def space(i):
+        return pltpu.SMEM if i in smem else pltpu.HBM if i in away else pltpu.VMEM
+
+    specs = [pl.BlockSpec(memory_space=space(i)) for i in range(len(args))]
     many = isinstance(outs, list)
     shapes = [jax.ShapeDtypeStruct(s, F32) for s in (outs if many else [outs])]
-    vmem = pl.BlockSpec(memory_space=pltpu.VMEM)
+    spec = pl.BlockSpec(memory_space=put)
     return pl.pallas_call(
         body,
         out_shape=shapes if many else shapes[0],
         in_specs=specs,
-        out_specs=[vmem] * len(shapes) if many else vmem,
-        scratch_shapes=[pltpu.VMEM(s, F32) for s in scratch],
-        compiler_params=pltpu.CompilerParams(vmem_limit_bytes=40 * 1024 * 1024),
+        out_specs=[spec] * len(shapes) if many else spec,
+        scratch_shapes=[pltpu.VMEM(s, F32) for s in scratch] + list(more),
+        compiler_params=pltpu.CompilerParams(vmem_limit_bytes=limit * 1024 * 1024),
     )(*args)
 
 
@@ -64,20 +64,36 @@
     )
 
 
-def pack_x(partner, disp, force, kappa, sigma, up, down, package):
-    for line, depth, start in zip(tile_lines(disp, force, kappa, sigma), DEPTHS, STARTS):
-        for k in range(depth):
-            up[start + k] = line(8 - depth + k)
-            down[start + k] = line(k)
-    first = disp[0, 2, 0:4].reshape(LANES, LANES).T[0:1]
-    second = disp[0, 2, 4:8].reshape(LANES, LANES).T[0:1]
+def pack_surface(partner, disp, package, tile, sem):
+    copy = pltpu.make_async_copy(disp.at[0, 2], tile, sem)
+    copy.start()
+    copy.wait()
+    first = tile[0:4].reshape(LANES, LANES).T[0:1]
+    second = tile[4:8].reshape(LANES, LANES).T[0:1]
     lane = iota((1, LANES), 1)
     hot = []
     for k in range(2):
-        q = partner[k]
-        hot.append(jnp.where(lane == 4 * (q // 2) + q % 2, 1.0, 0.0).astype(F32))
+        hot.append(jnp.where(lane == surface_row(partner[k]), 1.0, 0.0).astype(F32))
     four = stack_rows([first, second, hot[0], hot[1]])
     fill(package, stack_rows([four, four]))
+
+
+def pack_x(disp, force, kappa, sigma, after, up, down, sems):
+    sources = [disp.at[0, c] for c in range(3)] + [kappa.at[0]]
+    sources += [force.at[0, c] for c in range(3)] + [sigma.at[0]]
+    copies = []
+    for k, (source, depth, start) in enumerate(zip(sources, DEPTHS, STARTS)):
+        into = pl.ds(start, depth)
+        copies.append(
+            pltpu.make_async_copy(source.at[pl.ds(8 - depth, depth)], up.at[into], sems.at[2 * k])
+        )
+        copies.append(
+            pltpu.make_async_copy(source.at[pl.ds(0, depth)], down.at[into], sems.at[2 * k + 1])
+        )
+    for copy in copies:
+        copy.start()
+    for copy in copies:
+        copy.wait()
 
 
 def ext_line(line, low, high, field, x):
@@ -164,41 +180,87 @@
         state[14 + k : 15 + k, :] = vec_mat(traction, matrix)
 
 
+PLACES = ((0, 0, 0), (0, 3, -3), (1, 0, 0), (1, 3, -3), (0, 6, -6), (1, 6, -6), (2, 2, -2), (2, 0, 0))
+
+
+def put_line(target, value, low_y, high_y, field, x):
+    group, before, after = PLACES[field]
+    part = slice(8 * group, 8 * group + 8)
+    target[x, 0:8] = roll(low_y[x, part], before, 0)
+    target[x, 8:40] = value
+    target[x, 40:48] = roll(high_y[x, part], after, 0)
+
+
+def plane_smoother():
+    lane = iota((ROWS, LANES), 1)
+    keep_low = jnp.where(lane > 0, 0.5, 0.0).astype(F32)
+    keep_high = jnp.where(lane < LANES - 1, 0.5, 0.0).astype(F32)
+
+    def in_plane(value):
+        value = value + keep_low * roll(value, 1, 1) + keep_high * roll(value, -1, 1)
+        return value + 0.5 * (roll(value, 1, 0) + roll(value, -1, 0))
+
+    return in_plane
+
+
+def along(ref, *at):
+    *lead, x = at
+    return ref[(*lead, x)] + 0.5 * (ref[(*lead, x - 1)] + ref[(*lead, x + 1)])
+
+
+def base_surface(
+    disp, force, kappa, sigma, low_x, high_x, low_y, high_y, state, package,
+    moved, kap_lines, smooth_a, smooth_b, smooth_k, res,
+):
+    body = lax.axis_index("body")
+    lines = tile_lines(disp, force, kappa, sigma)
+    for x in range(2, LINES - 2):
+        put_line(moved, ext_line(lines[2], low_x, high_x, 2, x), low_y, high_y, 2, x)
+        put_line(kap_lines, ext_line(lines[3], low_x, high_x, 3, x), low_y, high_y, 3, x)
+    in_plane = plane_smoother()
+
+    @pl.loop(2, LINES - 2)
+    def _(x):
+        kap, value = kap_lines[x], moved[x]
+        smooth_k[x] = in_plane(kap)
+        smooth_a[x] = in_plane(value)
+        smooth_b[x] = in_plane(kap * value)
+
+    @pl.loop(0, 8)
+    def _(k):
+        x = k + 3
+        kap = kap_lines[x]
+        part = (8.0 * kap + along(smooth_k, x)) * moved[x] - kap * along(smooth_a, x) - along(smooth_b, x)
+        res[k] = force[0, 2, k] - sigma[0, k] * moved[x, 8:40] - part[8:40]
+
+    pieces = []
+    for k in range(2):
+        pieces.append(res[4 * k : 4 * k + 4].reshape(LANES, LANES).T[0:1])
+    for k in range(2):
+        pieces.append(jnp.where(body == 1, state[14 + k : 15 + k, :], state[12 + k : 13 + k, :]))
+    four = stack_rows(pieces)
+    fill(package, stack_rows([four, four]))
+
+
 def base(
-    disp, force, kappa, sigma, low_x, high_x, low_y, high_y, state,
-    res_out, image_out, strips, moments, package,
+    disp, force, kappa, sigma, low_x, high_x, low_y, high_y,
+    res_out, image_out, strips, moments,
     fields, diag, res, image, second, smooth_a, smooth_b, smooth_k,
 ):
-    body, gx, gy = lax.axis_index("body"), lax.axis_index("gx"), lax.axis_index("gy")
+    gx, gy = lax.axis_index("gx"), lax.axis_index("gy")
     lines = tile_lines(disp, force, kappa, sigma)
-    places = ((0, 0, 0), (0, 3, -3), (1, 0, 0), (1, 3, -3), (0, 6, -6), (1, 6, -6), (2, 2, -2), (2, 0, 0))
     for field in range(8):
-        group, before, after = places[field]
         for x in range(LINES):
             value = ext_line(lines[field], low_x, high_x, field, x)
-            if value is None:
-                continue
-            part = slice(8 * group, 8 * group + 8)
-            fields[field, x, 0:8] = roll(low_y[x, part], before, 0)
-            fields[field, x, 8:40] = value
-            fields[field, x, 40:48] = roll(high_y[x, part], after, 0)
-    lane = iota((ROWS, LANES), 1)
+            if value is not None:
+                put_line(fields.at[field], value, low_y, high_y, field, x)
     row = iota((ROWS, LANES), 0)
-    keep_low = jnp.where(lane > 0, 0.5, 0.0).astype(F32)
-    keep_high = jnp.where(lane < LANES - 1, 0.5, 0.0).astype(F32)
+    in_plane = plane_smoother()
     row_low = jnp.where(gy == 0, 8, 0)
     row_high = jnp.where(gy == lax.axis_size("gy") - 1, 40, ROWS)
     inside_y = jnp.where((row >= row_low) & (row < row_high), 1.0, 0.0).astype(F32)
     line_low = jnp.where(gx == 0, 3, 0)
     line_high = jnp.where(gx == lax.axis_size("gx") - 1, 11, LINES)
-
-    def in_plane(value):
-        value = value + keep_low * roll(value, 1, 1) + keep_high * roll(value, -1, 1)
-        return value + 0.5 * (roll(value, 1, 0) + roll(value, -1, 0))
-
-    def along(ref, *at):
-        *lead, x = at
-        return ref[(*lead, x)] + 0.5 * (ref[(*lead, x - 1)] + ref[(*lead, x + 1)])
 
     def inside(x):
         return inside_y * jnp.where((x >= line_low) & (x < line_high), 1.0, 0.0).astype(F32)
@@ -288,16 +350,6 @@
         turned = wide.T
         for kind in range(count):
             strips[kind, group : group + 1, :] = turned[kind : kind + 1]
-        if group in (1, 2):
-            k = group - 1
-            send = jnp.where(body == 1, state[14 + k : 15 + k, :], state[12 + k : 13 + k, :])
-            if k == 0:
-                sent, surface = [send], [turned[RES0 : RES0 + 1]]
-            else:
-                sent.append(send)
-                surface.append(turned[RES0 : RES0 + 1])
-    four = stack_rows(surface + sent)
-    fill(package, stack_rows([four, four]))
 
 
 def spread_row(select_rows, rows):
@@ -532,9 +584,27 @@
         return lax.all_to_all(package, axes, 0, 0, tiled=True)
 
     slabs = (SLABS, 32, LANES)
-    up, down, package = call(pack_x, [slabs, slabs, whole], (partner, *tile), smem=(0,))
+    package = call(
+        pack_surface,
+        whole,
+        (partner, disp),
+        smem=(0,),
+        away=(1,),
+        scratch=[(8, 32, LANES)],
+        more=[pltpu.SemaphoreType.DMA],
+        limit=60,
+    )
+    surfaces = trade(package, row)
+    up, down = call(
+        pack_x,
+        [slabs, slabs],
+        (*tile, package),
+        away=range(5),
+        more=[pltpu.SemaphoreType.DMA((16,))],
+        put=pltpu.HBM,
+        limit=60,
+    )
     low_x, high_x = shifted(up, "gx", 1), shifted(down, "gx", -1)
-    surfaces = trade(package, row)
     rims = (LINES, 24, LANES)
     up, down = call(pack_y, [rims, rims], (*tile, low_x, high_x))
     low_y, high_y = shifted(up, "gy", 1), shifted(down, "gy", -1)
@@ -545,13 +615,20 @@
         smem=(0, 1),
     )
     lines = (LINES, ROWS, LANES)
-    res, image, strips, moments, package = call(
+    rims = (low_x, high_x, low_y, high_y)
+    package = call(
+        base_surface,
+        whole,
+        (*tile, *rims, state),
+        scratch=[lines, lines, lines, lines, lines, (8, 32, LANES)],
+    )
+    rows = trade(package, row)
+    res, image, strips, moments = call(
         base,
-        [(3, 8, 32, LANES), (3, 8, 32, LANES), (16, 8, LANES), (4, 8, LANES), whole],
-        (*tile, low_x, high_x, low_y, high_y, state),
+        [(3, 8, 32, LANES), (3, 8, 32, LANES), (16, 8, LANES), (4, 8, LANES)],
+        (*tile, *rims),
         scratch=[(8, *lines), lines, (3, *lines), (3, *lines), (8, 32, LANES), (3, *lines), (3, *lines), lines],
     )
-    rows = trade(package, row)
     half = 4 * nx
     work = [(half + 16, LANES), (half, LANES), (half, LANES)]
     edges, second = call(

time: 138 us -> 153 us (1.11)
  Pallas kernels: 14.6 us -> 38.7 us
  blocking collectives: 73.8 us -> 54.5 us
  starting transfers between devices: 33.9 us -> 42.6 us
  waiting for transfers between devices: 9.69 us -> 16.1 us
  local copies, waits for them, and re-layouts: 4.49 us -> 0.06 us
    pallas_call x9 -> x11, Pallas kernels: 14.6 us -> 38.7 us  [call(): pl.pallas_call(body, out_shape=shapes if many else shapes[0], in_specs=sp...]
    all_to_all x4 -> x3, blocking collectives: 73.8 us -> 54.5 us  [trade(): return lax.all_to_all(package, axes, 0, 0, tiled=True)]
    all_to_all x1 -> x2, starting transfers between devices: 18.1 us -> 26.9 us  [trade(): return lax.all_to_all(package, axes, 0, 0, tiled=True)]
    all_to_all x1 -> x2, waiting for transfers between devices: 8.91 us -> 15.3 us  [trade(): return lax.all_to_all(package, axes, 0, 0, tiled=True)]
    unnamed x28 -> x18, local copies, waits for them, and re-layouts: 4.49 us -> 0.06 us
  transfers between devices with their start and end apart: 7 -> 8, of which waited for: 2 -> 3; matrix products, arithmetic and copies ran while one was open for 0% -> 0% of each run, Pallas kernels for 1% -> 6%
where the time goes in v2:
time: 153 us
  blocking collectives  54.5 us (36%)
  starting transfers between devices  42.6 us (28%)
  Pallas kernels  38.7 us (25%)
  waiting for transfers between devices  16.1 us (11%)
    all_to_all x3, blocking collectives, trade(): return lax.all_to_all(package, axes, 0, 0, tiled=True)  54.5 us
    pallas_call x11, Pallas kernels, call(): pl.pallas_call(body, out_shape=shapes if many else shapes[0], in_specs=sp...  38.7 us
    all_to_all x2, starting transfers between devices, trade(): return lax.all_to_all(package, axes, 0, 0, tiled=True)  26.9 us
    ppermute x6, starting transfers between devices, shifted(): return lax.ppermute(block, axis, pairs)  15.7 us
    all_to_all x2, waiting for transfers between devices, trade(): return lax.all_to_all(package, axes, 0, 0, tiled=True)  15.3 us
  transfers between devices with their start and end apart: 8, of which 3 were waited for; matrix products, arithmetic and copies ran while one was open for 0% of the time, Pallas kernels for 6%

profile of v2, /device:TPU:1, one launch (start us, length us, event | category | flops | bytes accessed | tf_op | source)
XLA Modules:
  0.0 152.8 jit_solution(9815132087201175232)
XLA Ops:
  0.6 2.3 %shard_map.104.after = f32[128,128]{1,0:T(8,128)} custom-call(s32[2]{0:T(128)} %partner.7, f32[1,3,8,32,128]{4,3,2,1,0:T(8,128)} %disp.9), custom_call_target="tpu_custom_call" | custom-call | tf_op jit(solution)/shard_map/pallas_call | solution.py:35
  2.9 21.1 %shard_map.105 = (f32[20,32,128]{2,1,0:T(8,128)}, f32[20,32,128]{2,1,0:T(8,128)}) custom-call(f32[1,3,8,32,128]{4,3,2,1,0:T(8,128)} %disp.9, f32[1,3,8,32,128]{4,3,2,1,0:T(8,128)} %force.7, f32[1,8,32,128]{3,2,1,0:T(8,128)} %kappa.7, f32[1,8,32,128]{3,2,1,0:T(8,128)} %sigma.7, f32[128,128]{1,0:T(8,128)} %shard_map.104.after), custom_call_target="tpu_custom_call" | custom-call | tf_op jit(solution)/shard_map/pallas_call | solution.py:35
  24.1 4.5 %collective-permute-start = (f32[20,32,128]{2,1,0:T(8,128)}, f32[20,32,128]{2,1,0:T(8,128)S(1)}, u32[]{:S(2)}, u32[]{:S(2)}) collective-permute-start(f32[20,32,128]{2,1,0:T(8,128)} %get-tuple-element.16), channel_id=1, source_target_pairs={{0,16},{16,32},{32,48},{48,64},{64,80},{80,96},{96,112},{112,128},... | collective-permute-start | bytes 983048 | tf_op jit(solution)/shard_map/ppermute | solution.py:574
  28.6 1.3 collective-permute-start.1
  29.9 18.1 %all-to-all-start = ((f32[32,4,128]{2,1,0:T(4,128)}), f32[32,4,128]{2,1,0:T(4,128)S(1)}, u32[]{:S(2)}, u32[]{:S(2)}) async-start(f32[32,4,128]{2,1,0:T(4,128)} %bitcast), calls=%async_computation | async-start | bytes 131072 | tf_op jit(solution)/shard_map/all_to_all | solution.py:584
  48.2 3.2 %collective-permute-start.2 = (f32[14,24,128]{2,1,0:T(8,128)S(1)}, f32[14,24,128]{2,1,0:T(8,128)S(1)}, u32[]{:S(2)}, u32[]{:S(2)}) collective-permute-start(f32[14,24,128]{2,1,0:T(8,128)S(1)} %get-tuple-element.18), channel_id=1, source_target_pairs={{0,1},{1,2},{2,3},{3,4},{4,5},{5,6},{6,7},{7,8},{8,9},{9,10},{10,1... | collective-permute-start | bytes 516104 | tf_op jit(solution)/shard_map/ppermute | solution.py:574
  51.5 1.4 collective-permute-start.3
  52.9 8.9 %all-to-all-done = f32[32,4,128]{2,1,0:T(4,128)S(1)} async-done(((f32[32,4,128]{2,1,0:T(4,128)}), f32[32,4,128]{2,1,0:T(4,128)S(1)}, u32[]{:S(2)}, u32[]{:S(2)}) %all-to-all-start) | async-done | bytes 65568 | tf_op jit(solution)/shard_map/all_to_all | solution.py:584
  61.8 1.5 shard_map.107.state
  63.3 2.1 %shard_map.108 = f32[128,128]{1,0:T(8,128)} custom-call(f32[1,3,8,32,128]{4,3,2,1,0:T(8,128)S(1)} %copy-done, f32[1,3,8,32,128]{4,3,2,1,0:T(8,128)S(1)} %copy-done.1, f32[1,8,32,128]{3,2,1,0:T(8,128)S(1)} %copy-done.2, f32[1,8,32,128]{3,2,1,0:T(8,128)S(1)} %copy-done.3, f32[20,32,128]{2,1,0:T(8,128)S(1)} %collective-permute-done.low.low_x, ...), custom_call_target="tpu_custom_call" | custom-call | tf_op jit(solution)/shard_map/pallas_call | solution.py:35
  65.4 8.7 %all-to-all-start.1 = ((f32[32,4,128]{2,1,0:T(4,128)}), f32[32,4,128]{2,1,0:T(4,128)S(1)}, u32[]{:S(2)}, u32[]{:S(2)}) async-start(f32[32,4,128]{2,1,0:T(4,128)} %bitcast.2), calls=%async_computation.1 | async-start | bytes 131072 | tf_op jit(solution)/shard_map/all_to_all | solution.py:584
  74.1 7.4 %shard_map.109 = (f32[3,8,32,128]{3,2,1,0:T(8,128)S(1)}, f32[3,8,32,128]{3,2,1,0:T(8,128)S(1)}, f32[16,8,128]{2,1,0:T(8,128)S(1)}, f32[4,8,128]{2,1,0:T(8,128)S(1)}) custom-call(f32[1,3,8,32,128]{4,3,2,1,0:T(8,128)S(1)} %copy-done, f32[1,3,8,32,128]{4,3,2,1,0:T(8,128)S(1)} %copy-done.1, f32[1,8,32,128]{3,2,1,0:T(8,128)S(1)} %copy-done.2, ...), custom_call_target="tpu_custom_call" | custom-call | tf_op jit(solution)/shard_map/pallas_call | solution.py:35
  81.5 6.4 %all-to-all-done.1 = f32[32,4,128]{2,1,0:T(4,128)S(1)} async-done(((f32[32,4,128]{2,1,0:T(4,128)}), f32[32,4,128]{2,1,0:T(4,128)S(1)}, u32[]{:S(2)}, u32[]{:S(2)}) %all-to-all-start.1) | async-done | bytes 65568 | tf_op jit(solution)/shard_map/all_to_all | solution.py:584
  87.9 1.7 %shard_map.110 = (f32[16,128]{1,0:T(8,128)S(1)}, f32[8,128]{1,0:T(8,128)S(1)}) custom-call(s32[2]{0:T(128)S(1)} %copy-done.5, f32[128,128]{1,0:T(8,128)S(1)} %bitcast.11, f32[128,128]{1,0:T(8,128)S(1)} %bitcast.13, f32[16,128]{1,0:T(8,128)S(1)} %shard_map.107.state, f32[2,128,128]{2,1,0:T(8,128)S(1)} %copy-done.4, f32[16,8,128]{2,1,0:T(8,128)S(1)} %get-tuple-element.20.strips), custom_call_target="tpu_custom_call" | custom-call | tf_op jit(solution)/shard_map/pallas_call | solution.py:35
  89.6 1.3 collective-permute-start.5
  90.9 4.0 %collective-permute-start.4 = (f32[16,128]{1,0:T(8,128)S(1)}, f32[16,128]{1,0:T(8,128)S(1)}, u32[]{:S(2)}, u32[]{:S(2)}) collective-permute-start(f32[16,128]{1,0:T(8,128)S(1)} %get-tuple-element.21.edges), channel_id=1, source_target_pairs={{0,1},{1,2},{2,3},{3,4},{4,5},{5,6},{6,7},{7,8},{8,9},{9,10},{10,1... | collective-permute-start | bytes 24584 | tf_op jit(solution)/shard_map/ppermute | solution.py:574
  94.9 0.8 collective-permute-done.4.low
  95.6 0.2 shard_map.111
  95.8 20.5 %all_to_all.55 = f32[32,4,128]{2,1,0:T(4,128)S(1)} all-to-all(f32[32,4,128]{2,1,0:T(4,128)S(1)} %bitcast.18), channel_id=1, replica_groups=mesh['body'=2,'gx'=16,'gy'=16] {'body','gx'}, dimensions={0} | all-to-all | bytes 131072 | tf_op jit(solution)/shard_map/all_to_all | solution.py:584
  116.3 1.2 shard_map.112
  117.5 17.4 %all_to_all.56 = f32[16,4,128]{2,1,0:T(4,128)S(1)} all-to-all(f32[16,4,128]{2,1,0:T(4,128)S(1)} %bitcast.19), channel_id=1, replica_groups=mesh['body'=2,'gx'=16,'gy'=16] {'gy'}, dimensions={0} | all-to-all | bytes 65536 | tf_op jit(solution)/shard_map/all_to_all | solution.py:584
  135.0 0.3 shard_map.113
  135.3 16.6 %all_to_all.57 = f32[32,2,128]{2,1,0:T(2,128)S(1)} all-to-all(f32[32,2,128]{2,1,0:T(2,128)S(1)} %bitcast.16), channel_id=1, replica_groups=mesh['body'=2,'gx'=16,'gy'=16] {'body','gx'}, dimensions={0} | all-to-all | bytes 65536 | tf_op jit(solution)/shard_map/all_to_all | solution.py:584
  151.9 1.0 shard_map.114
  (24 shorter events, 0.1 us)
Async XLA Ops:
  2.9 45.2 %copy-start = (f32[1,3,8,32,128]{4,3,2,1,0:T(8,128)S(1)}, f32[1,3,8,32,128]{4,3,2,1,0:T(8,128)}, u32[]{:S(2)}) copy-start(f32[1,3,8,32,128]{4,3,2,1,0:T(8,128)} %disp.9) | copy-start | bytes 1179652
  2.9 45.2 %copy-start.1 = (f32[1,3,8,32,128]{4,3,2,1,0:T(8,128)S(1)}, f32[1,3,8,32,128]{4,3,2,1,0:T(8,128)}, u32[]{:S(2)}) copy-start(f32[1,3,8,32,128]{4,3,2,1,0:T(8,128)} %force.7) | copy-start | bytes 1179652
  2.9 45.2 %copy-start.3 = (f32[1,8,32,128]{3,2,1,0:T(8,128)S(1)}, f32[1,8,32,128]{3,2,1,0:T(8,128)}, u32[]{:S(2)}) copy-start(f32[1,8,32,128]{3,2,1,0:T(8,128)} %sigma.7) | copy-start | bytes 393220
  24.1 24.1 %copy-start.2 = (f32[1,8,32,128]{3,2,1,0:T(8,128)S(1)}, f32[1,8,32,128]{3,2,1,0:T(8,128)}, u32[]{:S(2)}) copy-start(f32[1,8,32,128]{3,2,1,0:T(8,128)} %kappa.7) | copy-start | bytes 393220
  24.1 24.0 %collective-permute-start = (f32[20,32,128]{2,1,0:T(8,128)}, f32[20,32,128]{2,1,0:T(8,128)S(1)}, u32[]{:S(2)}, u32[]{:S(2)}) collective-permute-start(f32[20,32,128]{2,1,0:T(8,128)} %get-tuple-element.16), channel_id=1, source_target_pairs={{0,16},{16,32},{32,48},{48,64},{64,80},{80,96},{96,112},{112,128},... | collective-permute-start | bytes 983048 | tf_op jit(solution)/shard_map/ppermute | solution.py:574
  28.6 19.5 %collective-permute-start.1 = (f32[20,32,128]{2,1,0:T(8,128)}, f32[20,32,128]{2,1,0:T(8,128)S(1)}, u32[]{:S(2)}, u32[]{:S(2)}) collective-permute-start(f32[20,32,128]{2,1,0:T(8,128)} %get-tuple-element.17), channel_id=1, source_target_pairs={{16,0},{32,16},{48,32},{64,48},{80,64},{96,80},{112,96},{128,112},... | collective-permute-start | bytes 983048 | tf_op jit(solution)/shard_map/ppermute | solution.py:574
  29.9 31.9 %all-to-all-start = ((f32[32,4,128]{2,1,0:T(4,128)}), f32[32,4,128]{2,1,0:T(4,128)S(1)}, u32[]{:S(2)}, u32[]{:S(2)}) async-start(f32[32,4,128]{2,1,0:T(4,128)} %bitcast), calls=%async_computation | async-start | bytes 131072 | tf_op jit(solution)/shard_map/all_to_all | solution.py:584
  48.0 13.8 %copy-start.4 = (f32[2,128,128]{2,1,0:T(8,128)S(1)}, f32[2,128,128]{2,1,0:T(8,128)}, u32[]{:S(2)}) copy-start(f32[2,128,128]{2,1,0:T(8,128)} %mortar.5) | copy-start | bytes 393220
  48.2 15.2 %collective-permute-start.2 = (f32[14,24,128]{2,1,0:T(8,128)S(1)}, f32[14,24,128]{2,1,0:T(8,128)S(1)}, u32[]{:S(2)}, u32[]{:S(2)}) collective-permute-start(f32[14,24,128]{2,1,0:T(8,128)S(1)} %get-tuple-element.18), channel_id=1, source_target_pairs={{0,1},{1,2},{2,3},{3,4},{4,5},{5,6},{6,7},{7,8},{8,9},{9,10},{10,1... | collective-permute-start | bytes 516104 | tf_op jit(solution)/shard_map/ppermute | solution.py:574
  51.4 10.4 %copy-start.7 = (f32[2,128]{1,0:T(2,128)S(1)}, f32[2,128]{1,0:T(2,128)}, u32[]{:S(2)}) copy-start(f32[2,128]{1,0:T(2,128)} %pressure.1) | copy-start | bytes 3076
  51.4 10.4 %copy-start.8 = (s32[2]{0:T(128)S(1)}, s32[2]{0:T(128)}, u32[]{:S(2)}) copy-start(s32[2]{0:T(128)} %active.1) | copy-start | bytes 28
  51.4 10.4 %copy-start.5 = (s32[2]{0:T(128)S(1)}, s32[2]{0:T(128)}, u32[]{:S(2)}) copy-start(s32[2]{0:T(128)} %partner.7) | copy-start | bytes 28
  51.4 10.4 %copy-start.6 = (f32[2,128]{1,0:T(2,128)S(1)}, f32[2,128]{1,0:T(2,128)}, u32[]{:S(2)}) copy-start(f32[2,128]{1,0:T(2,128)} %gap0.1) | copy-start | bytes 3076
  51.5 11.9 %collective-permute-start.3 = (f32[14,24,128]{2,1,0:T(8,128)S(1)}, f32[14,24,128]{2,1,0:T(8,128)S(1)}, u32[]{:S(2)}, u32[]{:S(2)}) collective-permute-start(f32[14,24,128]{2,1,0:T(8,128)S(1)} %get-tuple-element.19), channel_id=1, source_target_pairs={{1,0},{2,1},{3,2},{4,3},{5,4},{6,5},{7,6},{8,7},{9,8},{10,9},{11,1... | collective-permute-start | bytes 516104 | tf_op jit(solution)/shard_map/ppermute | solution.py:574
  65.4 22.5 %all-to-all-start.1 = ((f32[32,4,128]{2,1,0:T(4,128)}), f32[32,4,128]{2,1,0:T(4,128)S(1)}, u32[]{:S(2)}, u32[]{:S(2)}) async-start(f32[32,4,128]{2,1,0:T(4,128)} %bitcast.2), calls=%async_computation.1 | async-start | bytes 131072 | tf_op jit(solution)/shard_map/all_to_all | solution.py:584
  89.6 5.3 %collective-permute-start.5 = (f32[16,128]{1,0:T(8,128)S(1)}, f32[16,128]{1,0:T(8,128)S(1)}, u32[]{:S(2)}, u32[]{:S(2)}) collective-permute-start(f32[16,128]{1,0:T(8,128)S(1)} %get-tuple-element.21.edges), channel_id=1, source_target_pairs={{1,0},{2,1},{3,2},{4,3},{5,4},{6,5},{7,6},{8,7},{9,8},{10,9},{11,1... | collective-permute-start | bytes 24584 | tf_op jit(solution)/shard_map/ppermute | solution.py:574
  90.9 4.8 %collective-permute-start.4 = (f32[16,128]{1,0:T(8,128)S(1)}, f32[16,128]{1,0:T(8,128)S(1)}, u32[]{:S(2)}, u32[]{:S(2)}) collective-permute-start(f32[16,128]{1,0:T(8,128)S(1)} %get-tuple-element.21.edges), channel_id=1, source_target_pairs={{0,1},{1,2},{2,3},{3,4},{4,5},{5,6},{6,7},{7,8},{8,9},{9,10},{10,1... | collective-permute-start | bytes 24584 | tf_op jit(solution)/shard_map/ppermute | solution.py:574

commit v3 on v2

--- a/solution.py
+++ b/solution.py
@@ -13,7 +13,7 @@
 SLABS = 20
 LINES = 14
 ROWS = 48
-KAP0, KAP1, DIA0, DIA1, RES0, IM0, IM1, SEC0, SEC1 = 0, 1, 2, 3, 4, 6, 7, 8, 9
+KAP0, KAP1, DIA0, DIA1, RES0, IM0, IM1 = 0, 1, 2, 3, 4, 6, 7
 
 
 def roll(value, step, axis):
@@ -24,14 +24,14 @@
     return lax.broadcasted_iota(jnp.int32, shape, axis)
 
 
-def call(body, outs, args, smem=(), away=(), scratch=(), more=(), limit=40, put=pltpu.VMEM):
+def call(body, outs, args, smem=(), away=(), scratch=(), more=(), limit=16):
     def space(i):
         return pltpu.SMEM if i in smem else pltpu.HBM if i in away else pltpu.VMEM
 
     specs = [pl.BlockSpec(memory_space=space(i)) for i in range(len(args))]
     many = isinstance(outs, list)
     shapes = [jax.ShapeDtypeStruct(s, F32) for s in (outs if many else [outs])]
-    spec = pl.BlockSpec(memory_space=put)
+    spec = pl.BlockSpec(memory_space=pltpu.VMEM)
     return pl.pallas_call(
         body,
         out_shape=shapes if many else shapes[0],
@@ -64,36 +64,45 @@
     )
 
 
-def pack_surface(partner, disp, package, tile, sem):
-    copy = pltpu.make_async_copy(disp.at[0, 2], tile, sem)
-    copy.start()
-    copy.wait()
-    first = tile[0:4].reshape(LANES, LANES).T[0:1]
-    second = tile[4:8].reshape(LANES, LANES).T[0:1]
-    lane = iota((1, LANES), 1)
-    hot = []
-    for k in range(2):
-        hot.append(jnp.where(lane == surface_row(partner[k]), 1.0, 0.0).astype(F32))
-    four = stack_rows([first, second, hot[0], hot[1]])
-    fill(package, stack_rows([four, four]))
-
-
-def pack_x(disp, force, kappa, sigma, after, up, down, sems):
+def pack_x(partner, disp, force, kappa, sigma, up, down, package, surface, sems):
     sources = [disp.at[0, c] for c in range(3)] + [kappa.at[0]]
     sources += [force.at[0, c] for c in range(3)] + [sigma.at[0]]
-    copies = []
+    copies = [
+        pltpu.make_async_copy(disp.at[0, 2], surface.at[0], sems.at[0]),
+        pltpu.make_async_copy(kappa.at[0], surface.at[1], sems.at[1]),
+    ]
     for k, (source, depth, start) in enumerate(zip(sources, DEPTHS, STARTS)):
         into = pl.ds(start, depth)
+        at = 2 + 2 * k
         copies.append(
-            pltpu.make_async_copy(source.at[pl.ds(8 - depth, depth)], up.at[into], sems.at[2 * k])
+            pltpu.make_async_copy(source.at[pl.ds(8 - depth, depth)], up.at[into], sems.at[at])
         )
         copies.append(
-            pltpu.make_async_copy(source.at[pl.ds(0, depth)], down.at[into], sems.at[2 * k + 1])
+            pltpu.make_async_copy(source.at[pl.ds(0, depth)], down.at[into], sems.at[at + 1])
         )
     for copy in copies:
         copy.start()
-    for copy in copies:
+    for copy in copies[:2]:
         copy.wait()
+    lanes = iota((LANES, LANES), 1)
+    lane = iota((1, LANES), 1)
+    first, second = [], []
+    for k in range(2):
+        field = surface[0, 4 * k : 4 * k + 4].reshape(LANES, LANES)
+        kap = surface[1, 4 * k : 4 * k + 4].reshape(LANES, LANES)
+        turned = jnp.where(lanes < 1, field, roll(kap, 1, 1)).T
+        first.append(turned[0:1])
+        place = surface_row(partner[k])
+        hot = jnp.where(lane == 32 * (place // 16) + 1 + place % 16, 1.0, 0.0).astype(F32)
+        second.append(jnp.where(edge_lanes(lane), turned[1:2], hot))
+    four = stack_rows(first + second)
+    fill(package, stack_rows([four, four]))
+    for copy in copies[2:]:
+        copy.wait()
+
+
+def edge_lanes(lane):
+    return (lane % 32 == 0) | (lane % 32 == 31)
 
 
 def ext_line(line, low, high, field, x):
@@ -244,8 +253,8 @@
 
 def base(
     disp, force, kappa, sigma, low_x, high_x, low_y, high_y,
-    res_out, image_out, strips, moments,
-    fields, diag, res, image, second, smooth_a, smooth_b, smooth_k,
+    res_out, strips, image_out, kap_out, diag_out,
+    fields, diag, res, image, smooth_a, smooth_b, smooth_k,
 ):
     gx, gy = lax.axis_index("gx"), lax.axis_index("gy")
     lines = tile_lines(disp, force, kappa, sigma)
@@ -304,34 +313,15 @@
                 dia * res[c, x] - kap * along(smooth_a, c, x) - along(smooth_b, c, x)
             )
 
-    @pl.loop(2, LINES - 2)
-    def _(x):
-        kap = fields[3, x]
+    for c in range(3):
+        for k in range(8):
+            res_out[c, k] = res[c, k + 3, 8:40]
+    for k in range(8):
+        diag_out[k] = diag[k + 3, 8:40]
+    for k in range(10):
+        kap_out[k] = fields[3, k + 2]
         for c in range(3):
-            value = image[c, x]
-            smooth_a[c, x] = in_plane(value)
-            smooth_b[c, x] = in_plane(kap * value)
-
-    def finish(k, sums):
-        x = k + 3
-        kap = fields[3, x]
-        dia = diag[x]
-        sums = list(sums)
-        for c in range(3):
-            r, p = res[c, x, 8:40], image[c, x, 8:40]
-            q = (dia * image[c, x] - kap * along(smooth_a, c, x) - along(smooth_b, c, x))[8:40]
-            if c == 2:
-                second[k] = q
-            res_out[c, k] = r
-            image_out[c, k] = p
-            for i, (a, b) in enumerate(((r, r), (r, p), (p, p), (p, q))):
-                product = (a * b).reshape(4, 8, LANES)
-                sums[i] = sums[i] + ((product[0] + product[1]) + (product[2] + product[3]))
-        return tuple(sums)
-
-    sums = lax.fori_loop(0, 8, finish, (jnp.zeros((8, LANES), F32),) * 4)
-    for i in range(4):
-        moments[i] = sums[i]
+            image_out[c, k] = image[c, k + 2]
     strips[...] = jnp.zeros(strips.shape, F32)
     lanes = iota((LANES, LANES), 1)
     for group in range(4):
@@ -340,11 +330,10 @@
         wide = jnp.where(lanes < 2, wide, roll(stack_rows([diag[x, 8:40] for x in near]), 2, 1))
         count = 4
         if group in (1, 2):
-            count = 10
+            count = 8
             for at, piece in (
                 (4, stack_rows([res[2, x, 8:40] for x in near])),
                 (6, stack_rows([image[2, x, 8:40] for x in near])),
-                (8, stack_rows([second[x - 3] for x in near])),
             ):
                 wide = jnp.where(lanes < at, wide, roll(piece, at, 1))
         turned = wide.T
@@ -352,19 +341,77 @@
             strips[kind, group : group + 1, :] = turned[kind : kind + 1]
 
 
+def base_moments(after, image, kap_lines, diag, res_own, moments, strips, smooth_a, smooth_b, second):
+    in_plane = plane_smoother()
+
+    @pl.loop(0, 10)
+    def _(x):
+        kap = kap_lines[x]
+        for c in range(3):
+            value = image[c, x]
+            smooth_a[c, x] = in_plane(value)
+            smooth_b[c, x] = in_plane(kap * value)
+
+    def finish_line(k, sums):
+        x = k + 1
+        kap, dia = kap_lines[x, 8:40], diag[k]
+        sums = list(sums)
+        for c in range(3):
+            r, p = res_own[c, k], image[c, x, 8:40]
+            q = dia * p - kap * along(smooth_a, c, x)[8:40] - along(smooth_b, c, x)[8:40]
+            if c == 2:
+                second[k] = q
+            for i, (a, b) in enumerate(((r, r), (r, p), (p, p), (p, q))):
+                product = (a * b).reshape(4, 8, LANES)
+                sums[i] = sums[i] + ((product[0] + product[1]) + (product[2] + product[3]))
+        return tuple(sums)
+
+    sums = lax.fori_loop(0, 8, finish_line, (jnp.zeros((8, LANES), F32),) * 4)
+    for i in range(4):
+        moments[i] = sums[i]
+    strips[...] = jnp.zeros(strips.shape, F32)
+    for group in range(2):
+        turned = second[4 * group : 4 * group + 4].reshape(LANES, LANES).T
+        for kind in range(2):
+            strips[kind, 1 + group : 2 + group, :] = turned[kind : kind + 1]
+
+
 def spread_row(select_rows, rows):
     half = rows.shape[0] // 2
-    index = iota((half, LANES), 0) % 4
-    select = jnp.where(index >= 2, select_rows[half:, :], 0.0)
-    master = -lax.dot_general(
+    shape = (half, LANES)
+    index, lane = iota(shape, 0) % 4, iota(shape, 1) % 32
+    hot = (index >= 2) & (lane >= 1) & (lane <= 16)
+    select = jnp.where(hot, select_rows[half:, :], 0.0)
+    spots = lax.dot_general(
         select,
         rows[half:, :],
         (((0,), (0,)), ((), ())),
         precision=HIGH,
         preferred_element_type=F32,
-    )[:half]
+    )
+    size = min(half, 16)
+    master = -stack_rows([spots[32 * k + 1 : 32 * k + 1 + size] for k in range(half // size)])
     slave = jnp.where(index < 2, -roll(rows[:half, :], -2, 0), 0.0)
     return slave, master
+
+
+def edge_kappa(select_rows):
+    value = roll(select_rows[...], -2, 0)
+    shape = value.shape
+    return jnp.where((iota(shape, 0) % 4 < 2) & edge_lanes(iota(shape, 1)), value, 0.0)
+
+
+def row_line_smooth(value):
+    row, lane = iota(value.shape, 0), iota(value.shape, 1)
+    place, spot = row % 4, row % (value.shape[0] // 2)
+    back, ahead = roll(value, 32, 1), roll(value, -32, 1)
+    before = jnp.where(place == 0, roll(back, 3, 0), roll(back, 1, 0))
+    before = jnp.where(spot == 0, 0.0, before)
+    after = jnp.where(place == 0, roll(ahead, -1, 0), roll(ahead, -3, 0))
+    after = jnp.where(spot == value.shape[0] // 2 - 3, 0.0, after)
+    back = jnp.where(lane >= 32, back, before)
+    ahead = jnp.where(lane < 96, ahead, after)
+    return jnp.where(place < 2, value + 0.5 * (back + ahead), 0.0)
 
 
 def own_extended(padded, gx):
@@ -385,7 +432,10 @@
     padded[8 + half : 16 + half, :] = jnp.zeros((8, LANES), F32)
 
 
-def contact_second(partner, select_rows, rows, state, mortar, strips, edges, out, padded, surf0, surf1):
+def contact_second(
+    partner, select_rows, rows, state, mortar, strips,
+    edges, out, moved, message, package, padded, surf0, surf1,
+):
     body, gx = lax.axis_index("body"), lax.axis_index("gx")
     half = rows.shape[0] // 2
     slave, master = spread_row(select_rows, rows)
@@ -393,8 +443,13 @@
     surf0[...] = rows[:half, :] + slave
     surf1[...] = rows[half:, :] + master
     first = own_extended(padded, gx)
-    edges[0:8, :] = first
-    edges[8:16, :] = strips[KAP0] * first
+    edges[...] = first
+    both = stack_rows([slave, master])
+    scaled = edge_kappa(select_rows) * both
+    y = iota(both.shape, 1) % 32
+    scaled = jnp.where(y == 1, roll(scaled, 1, 1), jnp.where(y == 30, roll(scaled, -1, 1), 0.0))
+    message[...] = jnp.where((y == 0) | (y == 31), both, scaled)
+    sent = []
     for k in range(2):
         matrix = mortar[k]
         gap = -surf0[pl.ds(4 * gx + k, 1), :] - mat_vec(
@@ -404,8 +459,24 @@
         pulled = vec_mat(push, matrix)
         out[k : k + 1, :] = gap
         out[2 + k : 3 + k, :] = push
-        out[4 + k : 5 + k, :] = jnp.where(body == 1, pulled, push)
-        out[6 + k : 7 + k, :] = strips[IM0, 1 + k : 2 + k, :]
+        sent.append(jnp.where(body == 1, pulled, push))
+    out[4:8, :] = jnp.zeros((4, LANES), F32)
+    plain = line_smooth(row_smooth(first))
+    weighted = line_smooth(row_smooth(strips[KAP0] * first))
+    mask = inside_rows()
+    top = jnp.where(mask, strips[DIA0] * first - strips[KAP0] * plain - weighted, 0.0)
+    moved[0:8, :] = top
+    moved[8:16, :] = jnp.where(mask, -0.5 * (strips[KAP1] * plain + weighted), 0.0)
+    four = stack_rows([(strips[IM0] + top)[1:3]] + sent)
+    fill(package, stack_rows([four, four]))
+
+
+def inside_rows():
+    gx = lax.axis_index("gx")
+    row = iota((8, LANES), 0)
+    lowest = jnp.where(gx == 0, 1, 0)
+    highest = jnp.where(gx == lax.axis_size("gx") - 1, 3, 4)
+    return (row >= lowest) & (row < highest)
 
 
 def line_smooth(value):
@@ -416,31 +487,11 @@
     return value + 0.5 * (back + ahead)
 
 
-def row_smooth(value, low=None, high=None):
+def row_smooth(value):
     y = iota(value.shape, 1) % 32
-    before = 0.0 if low is None else roll(low, -31, 1)
-    after = 0.0 if high is None else roll(high, 31, 1)
-    before = jnp.where(y > 0, roll(value, 1, 1), before)
-    after = jnp.where(y < 31, roll(value, -1, 1), after)
+    before = jnp.where(y > 0, roll(value, 1, 1), 0.0)
+    after = jnp.where(y < 31, roll(value, -1, 1), 0.0)
     return value + 0.5 * (before + after)
-
-
-def couple(edges, low, high, strips, second, moved, package):
-    gx = lax.axis_index("gx")
-    first = edges[0:8, :]
-    plain = line_smooth(row_smooth(first, low[0:8, :], high[0:8, :]))
-    weighted = line_smooth(row_smooth(edges[8:16, :], low[8:16, :], high[8:16, :]))
-    row = iota((8, LANES), 0)
-    lowest = jnp.where(gx == 0, 1, 0)
-    highest = jnp.where(gx == lax.axis_size("gx") - 1, 3, 4)
-    mask = (row >= lowest) & (row < highest)
-    kap0 = strips[KAP0]
-    top = jnp.where(mask, strips[DIA0] * first - kap0 * plain - weighted, 0.0)
-    below = jnp.where(mask, -0.5 * (strips[KAP1] * plain + weighted), 0.0)
-    moved[0:8, :] = top
-    moved[8:16, :] = below
-    four = stack_rows([second[6:8, :] + top[1:3], second[4:6, :]])
-    fill(package, stack_rows([four, four]))
 
 
 def total(value):
@@ -448,19 +499,33 @@
 
 
 def measure_moments(
-    partner, select_rows, rows, state, mortar, strips, edges, second, moved, moments,
-    package, image_out, padded, surf0, surf1,
+    partner, select_rows, rows, state, mortar, strips, edges, second, moved, low, high,
+    more_strips, moments, package, image_out, padded, surf0, surf1,
 ):
     body, gx = lax.axis_index("body"), lax.axis_index("gx")
     half = rows.shape[0] // 2
     slave, master = spread_row(select_rows, rows)
+    y = iota(rows.shape, 1) % 32
+    below_row, above_row = low[...], high[...]
+    plain = jnp.where(y == 0, roll(below_row, -31, 1), jnp.where(y == 31, roll(above_row, 31, 1), 0.0))
+    scaled = jnp.where(y == 0, roll(below_row, -30, 1), jnp.where(y == 31, roll(above_row, 30, 1), 0.0))
+    plain, scaled = row_line_smooth(plain), row_line_smooth(scaled)
+    added = -0.5 * (edge_kappa(select_rows) * plain + scaled)
+    surf0[...] = rows[:half, :] + slave + added[:half]
+    surf1[...] = rows[half:, :] + master + added[half:]
+
+    def own_rows(value):
+        put_padded(padded, jnp.where(body == 0, value[:half], value[half:]))
+        return own_extended(padded, gx)
+
+    plain, scaled = own_rows(plain), own_rows(scaled)
     put_padded(padded, jnp.where(body == 0, slave, master))
-    surf0[...] = rows[:half, :] + slave
-    surf1[...] = rows[half:, :] + master
-    first = edges[0:8, :]
-    k_first = moved[0:8, :]
+    mask = inside_rows()
+    kap0, kap1 = strips[KAP0], strips[KAP1]
+    first = edges[...]
+    k_first = moved[0:8, :] - jnp.where(mask, 0.5 * (kap0 * plain + scaled), 0.0)
     top = k_first + own_extended(padded, gx)
-    below = moved[8:16, :]
+    below = moved[8:16, :] - jnp.where(mask, 0.25 * (kap1 * plain + scaled), 0.0)
     once = jnp.where(body == 0, 1.0, 0.0).astype(F32)
     push_sum = jnp.zeros((1, LANES), F32)
     gap_sum = jnp.zeros((1, LANES), F32)
@@ -476,7 +541,6 @@
     image_out[16:24, :] = below
     row = iota((8, LANES), 0)
     own = (row == 1) | (row == 2)
-    kap0, kap1 = strips[KAP0], strips[KAP1]
 
     def surface_sum(value):
         return total(jnp.where(own, value, 0.0))
@@ -490,8 +554,8 @@
     mu3 = (
         total(moments[3])
         + surface_sum(
-            top * (2.0 * strips[SEC0] + strips[DIA0] * top - 2.0 * kap0 * t_top)
-            + below * (2.0 * strips[SEC1] + strips[DIA1] * below - 2.0 * kap1 * t_below)
+            top * (2.0 * more_strips[0] + strips[DIA0] * top - 2.0 * kap0 * t_top)
+            + below * (2.0 * more_strips[1] + strips[DIA1] * below - 2.0 * kap1 * t_below)
         )
         + once * total(gap_sum)
     )
@@ -557,7 +621,7 @@
     for c in range(3):
         for x in range(8):
             r = res[c, x].reshape(4, 8, LANES)
-            p = image[c, x].reshape(4, 8, LANES)
+            p = image[c, x + 1, 8:40].reshape(4, 8, LANES)
             increment[0, c, x] = (wide_res * r + wide_im * p).reshape(32, LANES)
     for k in range(2):
         top = c_res * edges[1 + k : 2 + k, :] + c_im * last[9 + k : 10 + k, :]
@@ -584,26 +648,17 @@
         return lax.all_to_all(package, axes, 0, 0, tiled=True)
 
     slabs = (SLABS, 32, LANES)
-    package = call(
-        pack_surface,
-        whole,
-        (partner, disp),
+    up, down, package = call(
+        pack_x,
+        [slabs, slabs, whole],
+        (partner, *tile),
         smem=(0,),
-        away=(1,),
-        scratch=[(8, 32, LANES)],
-        more=[pltpu.SemaphoreType.DMA],
+        away=range(1, 5),
+        scratch=[(2, 8, 32, LANES)],
+        more=[pltpu.SemaphoreType.DMA((18,))],
         limit=60,
     )
     surfaces = trade(package, row)
-    up, down = call(
-        pack_x,
-        [slabs, slabs],
-        (*tile, package),
-        away=range(5),
-        more=[pltpu.SemaphoreType.DMA((16,))],
-        put=pltpu.HBM,
-        limit=60,
-    )
     low_x, high_x = shifted(up, "gx", 1), shifted(down, "gx", -1)
     rims = (LINES, 24, LANES)
     up, down = call(pack_y, [rims, rims], (*tile, low_x, high_x))
@@ -623,30 +678,34 @@
         scratch=[lines, lines, lines, lines, lines, (8, 32, LANES)],
     )
     rows = trade(package, row)
-    res, image, strips, moments = call(
+    wide, near = (3, *lines), (10, ROWS, LANES)
+    res, strips, image, ext_kappa, diag = call(
         base,
-        [(3, 8, 32, LANES), (3, 8, 32, LANES), (16, 8, LANES), (4, 8, LANES)],
+        [(3, 8, 32, LANES), (8, 8, LANES), (3, *near), near, (8, 32, LANES)],
         (*tile, *rims),
-        scratch=[(8, *lines), lines, (3, *lines), (3, *lines), (8, 32, LANES), (3, *lines), (3, *lines), lines],
+        scratch=[(8, *lines), lines, wide, wide, wide, wide, lines],
     )
     half = 4 * nx
     work = [(half + 16, LANES), (half, LANES), (half, LANES)]
-    edges, second = call(
+    edges, second, moved, message, package = call(
         contact_second,
-        [(16, LANES), (8, LANES)],
+        [(8, LANES), (8, LANES), (16, LANES), whole, whole],
         (partner, surfaces, rows, state, mortar, strips),
         smem=(0,),
         scratch=work,
     )
-    low, high = shifted(edges, "gy", 1), shifted(edges, "gy", -1)
-    moved, package = call(
-        couple, [(16, LANES), whole], (edges, low, high, strips, second)
-    )
+    low, high = shifted(message, "gy", 1), shifted(message, "gy", -1)
     rows = trade(package, row)
+    moments, more_strips = call(
+        base_moments,
+        [(4, 8, LANES), (2, 8, LANES)],
+        (edges, image, ext_kappa, diag, res),
+        scratch=[(3, *near), (3, *near), (8, 32, LANES)],
+    )
     package, last = call(
         measure_moments,
         [(4 * ny, LANES), (24, LANES)],
-        (partner, surfaces, rows, state, mortar, strips, edges, second, moved, moments),
+        (partner, surfaces, rows, state, mortar, strips, edges, second, moved, low, high, more_strips, moments),
         smem=(0,),
         scratch=work,
     )

time: 153 us -> 129 us (0.84)
  Pallas kernels: 38.7 us -> 18.9 us
  blocking collectives: 54.5 us -> 37.4 us
  waiting for transfers between devices: 16.1 us -> 22.3 us
  starting transfers between devices: 42.6 us -> 48 us
    pallas_call x11 -> x10, Pallas kernels: 38.7 us -> 18.9 us  [call(): pl.pallas_call(body, out_shape=shapes if many else shapes[0], in_specs=sp...]
    all_to_all x3 -> x2, blocking collectives: 54.5 us -> 37.4 us  [trade(): return lax.all_to_all(package, axes, 0, 0, tiled=True)]
    all_to_all x2 -> x3, waiting for transfers between devices: 15.3 us -> 22.3 us  [trade(): return lax.all_to_all(package, axes, 0, 0, tiled=True)]
    all_to_all x2 -> x3, starting transfers between devices: 26.9 us -> 32.3 us  [trade(): return lax.all_to_all(package, axes, 0, 0, tiled=True)]
  transfers between devices with their start and end apart: 8 -> 9, of which waited for: 3 -> 3; matrix products, arithmetic and copies ran while one was open for 0% -> 0% of each run, Pallas kernels for 6% -> 7%
where the time goes in v3:
time: 129 us
  starting transfers between devices  48 us (37%)
  blocking collectives  37.4 us (29%)
  waiting for transfers between devices  22.3 us (17%)
  Pallas kernels  18.9 us (15%)
  local copies, waits for them, and re-layouts  1.4 us (1%)
    all_to_all x2, blocking collectives, trade(): return lax.all_to_all(package, axes, 0, 0, tiled=True)  37.4 us
    all_to_all x3, starting transfers between devices, trade(): return lax.all_to_all(package, axes, 0, 0, tiled=True)  32.3 us
    all_to_all x3, waiting for transfers between devices, trade(): return lax.all_to_all(package, axes, 0, 0, tiled=True)  22.3 us
    pallas_call x10, Pallas kernels, call(): pl.pallas_call(body, out_shape=shapes if many else shapes[0], in_specs=sp...  18.9 us
    ppermute x6, starting transfers between devices, shifted(): return lax.ppermute(block, axis, pairs)  15.7 us
  transfers between devices with their start and end apart: 9, of which 3 were waited for; matrix products, arithmetic and copies ran while one was open for 0% of the time, Pallas kernels for 7%

profile of v3, /device:TPU:1, one launch (start us, length us, event | category | flops | bytes accessed | tf_op | source)
XLA Modules:
  0.0 128.9 jit_solution(14345081539465319529)
XLA Ops:
  0.7 3.0 %shard_map.104 = (f32[20,32,128]{2,1,0:T(8,128)}, f32[20,32,128]{2,1,0:T(8,128)}, f32[128,128]{1,0:T(8,128)}) custom-call(s32[2]{0:T(128)} %partner.7, f32[1,3,8,32,128]{4,3,2,1,0:T(8,128)} %disp.7, f32[1,3,8,32,128]{4,3,2,1,0:T(8,128)} %force.7, f32[1,8,32,128]{3,2,1,0:T(8,128)} %kappa.7, f32[1,8,32,128]{3,2,1,0:T(8,128)} %sigma.7), custom_call_target="tpu_custom_call" | custom-call | tf_op jit(solution)/shard_map/pallas_call | solution.py:35
  3.6 4.5 %collective-permute-start = (f32[20,32,128]{2,1,0:T(8,128)}, f32[20,32,128]{2,1,0:T(8,128)S(1)}, u32[]{:S(2)}, u32[]{:S(2)}) collective-permute-start(f32[20,32,128]{2,1,0:T(8,128)} %get-tuple-element.22), channel_id=1, source_target_pairs={{0,16},{16,32},{32,48},{48,64},{64,80},{80,96},{96,112},{112,128},... | collective-permute-start | bytes 983048 | tf_op jit(solution)/shard_map/ppermute | solution.py:638
  8.2 1.3 %collective-permute-start.1 = (f32[20,32,128]{2,1,0:T(8,128)}, f32[20,32,128]{2,1,0:T(8,128)S(1)}, u32[]{:S(2)}, u32[]{:S(2)}) collective-permute-start(f32[20,32,128]{2,1,0:T(8,128)} %get-tuple-element.23), channel_id=1, source_target_pairs={{16,0},{32,16},{48,32},{64,48},{80,64},{96,80},{112,96},{128,112},... | collective-permute-start | bytes 983048 | tf_op jit(solution)/shard_map/ppermute | solution.py:638
  9.5 18.1 %all-to-all-start = ((f32[32,4,128]{2,1,0:T(4,128)}), f32[32,4,128]{2,1,0:T(4,128)S(1)}, u32[]{:S(2)}, u32[]{:S(2)}) async-start(f32[32,4,128]{2,1,0:T(4,128)} %bitcast.19), calls=%async_computation | async-start | bytes 131072 | tf_op jit(solution)/shard_map/all_to_all | solution.py:648
  27.8 3.2 %collective-permute-start.2 = (f32[14,24,128]{2,1,0:T(8,128)S(1)}, f32[14,24,128]{2,1,0:T(8,128)S(1)}, u32[]{:S(2)}, u32[]{:S(2)}) collective-permute-start(f32[14,24,128]{2,1,0:T(8,128)S(1)} %get-tuple-element.24), channel_id=1, source_target_pairs={{0,1},{1,2},{2,3},{3,4},{4,5},{5,6},{6,7},{7,8},{8,9},{9,10},{10,1... | collective-permute-start | bytes 516104 | tf_op jit(solution)/shard_map/ppermute | solution.py:638
  31.0 1.4 %collective-permute-start.3 = (f32[14,24,128]{2,1,0:T(8,128)S(1)}, f32[14,24,128]{2,1,0:T(8,128)S(1)}, u32[]{:S(2)}, u32[]{:S(2)}) collective-permute-start(f32[14,24,128]{2,1,0:T(8,128)S(1)} %get-tuple-element.25), channel_id=1, source_target_pairs={{1,0},{2,1},{3,2},{4,3},{5,4},{6,5},{7,6},{8,7},{9,8},{10,9},{11,1... | collective-permute-start | bytes 516104 | tf_op jit(solution)/shard_map/ppermute | solution.py:638
  32.5 8.9 %all-to-all-done = f32[32,4,128]{2,1,0:T(4,128)S(1)} async-done(((f32[32,4,128]{2,1,0:T(4,128)}), f32[32,4,128]{2,1,0:T(4,128)S(1)}, u32[]{:S(2)}, u32[]{:S(2)}) %all-to-all-start) | async-done | bytes 65568 | tf_op jit(solution)/shard_map/all_to_all | solution.py:648
  41.4 1.5 %shard_map.106.state = f32[16,128]{1,0:T(8,128)S(1)} custom-call(s32[2]{0:T(128)S(1)} %copy-done.9, s32[2]{0:T(128)S(1)} %copy-done.12, f32[128,128]{1,0:T(8,128)S(1)} %bitcast.10, f32[2,128]{1,0:T(2,128)S(1)} %copy-done.10, f32[2,128]{1,0:T(2,128)S(1)} %copy-done.11, f32[2,128,128]{2,1,0:T(8,128)S(1)} %copy-done.4), custom_call_target="tpu_custom_call" | custom-call | tf_op jit(solution)/shard_map/pallas_call | solution.py:35
  42.9 2.1 %shard_map.107 = f32[128,128]{1,0:T(8,128)} custom-call(f32[1,3,8,32,128]{4,3,2,1,0:T(8,128)S(1)} %copy-done, f32[1,3,8,32,128]{4,3,2,1,0:T(8,128)S(1)} %copy-done.1, f32[1,8,32,128]{3,2,1,0:T(8,128)S(1)} %copy-done.2, f32[1,8,32,128]{3,2,1,0:T(8,128)S(1)} %copy-done.3, f32[20,32,128]{2,1,0:T(8,128)S(1)} %collective-permute-done.low.low_x, ...), custom_call_target="tpu_custom_call" | custom-call | tf_op jit(solution)/shard_map/pallas_call | solution.py:35
  45.0 8.7 %all-to-all-start.1 = ((f32[32,4,128]{2,1,0:T(4,128)}), f32[32,4,128]{2,1,0:T(4,128)S(1)}, u32[]{:S(2)}, u32[]{:S(2)}) async-start(f32[32,4,128]{2,1,0:T(4,128)} %bitcast.2), calls=%async_computation.1 | async-start | bytes 131072 | tf_op jit(solution)/shard_map/all_to_all | solution.py:648
  53.7 5.5 %shard_map.108 = (f32[3,8,32,128]{3,2,1,0:T(8,128)S(1)}, f32[8,8,128]{2,1,0:T(8,128)S(1)}, f32[3,10,48,128]{3,2,1,0:T(8,128)S(1)}, f32[10,48,128]{2,1,0:T(8,128)S(1)}, f32[8,32,128]{2,1,0:T(8,128)S(1)}) custom-call(f32[1,3,8,32,128]{4,3,2,1,0:T(8,128)S(1)} %copy-done, f32[1,3,8,32,128]{4,3,2,1,0:T(8,128)S(1)} %copy-done.1, f32[1,8,32,128]{3,2,1,0:T(8,128)S(1)} %copy-done.2, ...), custom_call_target="tpu_custom_call" | custom-call | tf_op jit(solution)/shard_map/pallas_call | solution.py:35
  59.3 0.7 copy-done.5
  60.0 0.6 copy-done.7
  60.6 6.9 %all-to-all-done.1 = f32[32,4,128]{2,1,0:T(4,128)S(1)} async-done(((f32[32,4,128]{2,1,0:T(4,128)}), f32[32,4,128]{2,1,0:T(4,128)S(1)}, u32[]{:S(2)}, u32[]{:S(2)}) %all-to-all-start.1) | async-done | bytes 65568 | tf_op jit(solution)/shard_map/all_to_all | solution.py:648
  67.5 2.3 %shard_map.109 = (f32[8,128]{1,0:T(8,128)S(1)}, f32[8,128]{1,0:T(8,128)S(1)}, f32[16,128]{1,0:T(8,128)S(1)}, f32[128,128]{1,0:T(8,128)S(1)}, f32[128,128]{1,0:T(8,128)}) custom-call(s32[2]{0:T(128)S(1)} %copy-done.9, f32[128,128]{1,0:T(8,128)S(1)} %bitcast.11, f32[128,128]{1,0:T(8,128)S(1)} %bitcast.13, f32[16,128]{1,0:T(8,128)S(1)} %shard_map.106.state, ...), custom_call_target="tpu_custom_call" | custom-call | tf_op jit(solution)/shard_map/pallas_call | solution.py:35
  69.8 5.5 %all-to-all-start.2 = ((f32[32,4,128]{2,1,0:T(4,128)}), f32[32,4,128]{2,1,0:T(4,128)S(1)}, u32[]{:S(2)}, u32[]{:S(2)}) async-start(f32[32,4,128]{2,1,0:T(4,128)} %bitcast.4), calls=%async_computation.2 | async-start | bytes 131072 | tf_op jit(solution)/shard_map/all_to_all | solution.py:648
  75.3 1.3 %collective-permute-start.5 = (f32[128,128]{1,0:T(8,128)S(1)}, f32[128,128]{1,0:T(8,128)S(1)}, u32[]{:S(2)}, u32[]{:S(2)}) collective-permute-start(f32[128,128]{1,0:T(8,128)S(1)} %get-tuple-element.31), channel_id=1, source_target_pairs={{1,0},{2,1},{3,2},{4,3},{5,4},{6,5},{7,6},{8,7},{9,8},{10,9},{11,1... | collective-permute-start | bytes 196616 | tf_op jit(solution)/shard_map/ppermute | solution.py:638
  76.6 4.0 %collective-permute-start.4 = (f32[128,128]{1,0:T(8,128)S(1)}, f32[128,128]{1,0:T(8,128)S(1)}, u32[]{:S(2)}, u32[]{:S(2)}) collective-permute-start(f32[128,128]{1,0:T(8,128)S(1)} %get-tuple-element.31), channel_id=1, source_target_pairs={{0,1},{1,2},{2,3},{3,4},{4,5},{5,6},{6,7},{7,8},{8,9},{9,10},{10,1... | collective-permute-start | bytes 196616 | tf_op jit(solution)/shard_map/ppermute | solution.py:638
  80.6 1.9 %shard_map.110 = (f32[4,8,128]{2,1,0:T(8,128)S(1)}, f32[2,8,128]{2,1,0:T(8,128)S(1)}) custom-call(f32[8,128]{1,0:T(8,128)S(1)} %get-tuple-element.28.after.edges, f32[3,10,48,128]{3,2,1,0:T(8,128)S(1)} %get-tuple-element.32.image, f32[10,48,128]{2,1,0:T(8,128)S(1)} %copy-done.6, f32[8,32,128]{2,1,0:T(8,128)S(1)} %copy-done.8, ...), custom_call_target="tpu_custom_call" | custom-call | tf_op jit(solution)/shard_map/pallas_call | solution.py:35
  82.5 6.5 %all-to-all-done.2 = f32[32,4,128]{2,1,0:T(4,128)S(1)} async-done(((f32[32,4,128]{2,1,0:T(4,128)}), f32[32,4,128]{2,1,0:T(4,128)S(1)}, u32[]{:S(2)}, u32[]{:S(2)}) %all-to-all-start.2) | async-done | bytes 65568 | tf_op jit(solution)/shard_map/all_to_all | solution.py:648
  89.0 1.3 shard_map.111
  90.3 14.2 %all_to_all.55 = f32[16,4,128]{2,1,0:T(4,128)S(1)} all-to-all(f32[16,4,128]{2,1,0:T(4,128)S(1)} %bitcast.18), channel_id=1, replica_groups=mesh['body'=2,'gx'=16,'gy'=16] {'gy'}, dimensions={0} | all-to-all | bytes 65536 | tf_op jit(solution)/shard_map/all_to_all | solution.py:648
  104.8 23.1 %all_to_all.56 = f32[32,2,128]{2,1,0:T(2,128)S(1)} all-to-all(f32[32,2,128]{2,1,0:T(2,128)S(1)} %bitcast.17), channel_id=1, replica_groups=mesh['body'=2,'gx'=16,'gy'=16] {'body','gx'}, dimensions={0} | all-to-all | bytes 65536 | tf_op jit(solution)/shard_map/all_to_all | solution.py:648
  128.0 1.0 shard_map.113
  (32 shorter events, 0.5 us)
Async XLA Ops:
  0.6 27.0 %copy-start.1 = (f32[1,3,8,32,128]{4,3,2,1,0:T(8,128)S(1)}, f32[1,3,8,32,128]{4,3,2,1,0:T(8,128)}, u32[]{:S(2)}) copy-start(f32[1,3,8,32,128]{4,3,2,1,0:T(8,128)} %force.7) | copy-start | bytes 1179652
  0.6 27.0 %copy-start = (f32[1,3,8,32,128]{4,3,2,1,0:T(8,128)S(1)}, f32[1,3,8,32,128]{4,3,2,1,0:T(8,128)}, u32[]{:S(2)}) copy-start(f32[1,3,8,32,128]{4,3,2,1,0:T(8,128)} %disp.7) | copy-start | bytes 1179652
  0.6 27.0 %copy-start.3 = (f32[1,8,32,128]{3,2,1,0:T(8,128)S(1)}, f32[1,8,32,128]{3,2,1,0:T(8,128)}, u32[]{:S(2)}) copy-start(f32[1,8,32,128]{3,2,1,0:T(8,128)} %sigma.7) | copy-start | bytes 393220
  3.6 24.1 %copy-start.2 = (f32[1,8,32,128]{3,2,1,0:T(8,128)S(1)}, f32[1,8,32,128]{3,2,1,0:T(8,128)}, u32[]{:S(2)}) copy-start(f32[1,8,32,128]{3,2,1,0:T(8,128)} %kappa.7) | copy-start | bytes 393220
  3.6 24.0 %collective-permute-start = (f32[20,32,128]{2,1,0:T(8,128)}, f32[20,32,128]{2,1,0:T(8,128)S(1)}, u32[]{:S(2)}, u32[]{:S(2)}) collective-permute-start(f32[20,32,128]{2,1,0:T(8,128)} %get-tuple-element.22), channel_id=1, source_target_pairs={{0,16},{16,32},{32,48},{48,64},{64,80},{80,96},{96,112},{112,128},... | collective-permute-start | bytes 983048 | tf_op jit(solution)/shard_map/ppermute | solution.py:638
  8.2 19.5 %collective-permute-start.1 = (f32[20,32,128]{2,1,0:T(8,128)}, f32[20,32,128]{2,1,0:T(8,128)S(1)}, u32[]{:S(2)}, u32[]{:S(2)}) collective-permute-start(f32[20,32,128]{2,1,0:T(8,128)} %get-tuple-element.23), channel_id=1, source_target_pairs={{16,0},{32,16},{48,32},{64,48},{80,64},{96,80},{112,96},{128,112},... | collective-permute-start | bytes 983048 | tf_op jit(solution)/shard_map/ppermute | solution.py:638
  9.5 31.9 %all-to-all-start = ((f32[32,4,128]{2,1,0:T(4,128)}), f32[32,4,128]{2,1,0:T(4,128)S(1)}, u32[]{:S(2)}, u32[]{:S(2)}) async-start(f32[32,4,128]{2,1,0:T(4,128)} %bitcast.19), calls=%async_computation | async-start | bytes 131072 | tf_op jit(solution)/shard_map/all_to_all | solution.py:648
  27.6 13.8 %copy-start.4 = (f32[2,128,128]{2,1,0:T(8,128)S(1)}, f32[2,128,128]{2,1,0:T(8,128)}, u32[]{:S(2)}) copy-start(f32[2,128,128]{2,1,0:T(8,128)} %mortar.5) | copy-start | bytes 393220
  27.8 15.2 %collective-permute-start.2 = (f32[14,24,128]{2,1,0:T(8,128)S(1)}, f32[14,24,128]{2,1,0:T(8,128)S(1)}, u32[]{:S(2)}, u32[]{:S(2)}) collective-permute-start(f32[14,24,128]{2,1,0:T(8,128)S(1)} %get-tuple-element.24), channel_id=1, source_target_pairs={{0,1},{1,2},{2,3},{3,4},{4,5},{5,6},{6,7},{7,8},{8,9},{9,10},{10,1... | collective-permute-start | bytes 516104 | tf_op jit(solution)/shard_map/ppermute | solution.py:638
  31.0 10.4 %copy-start.11 = (f32[2,128]{1,0:T(2,128)S(1)}, f32[2,128]{1,0:T(2,128)}, u32[]{:S(2)}) copy-start(f32[2,128]{1,0:T(2,128)} %pressure.1) | copy-start | bytes 3076
  31.0 10.4 %copy-start.12 = (s32[2]{0:T(128)S(1)}, s32[2]{0:T(128)}, u32[]{:S(2)}) copy-start(s32[2]{0:T(128)} %active.1) | copy-start | bytes 28
  31.0 10.4 %copy-start.9 = (s32[2]{0:T(128)S(1)}, s32[2]{0:T(128)}, u32[]{:S(2)}) copy-start(s32[2]{0:T(128)} %partner.7) | copy-start | bytes 28
  31.0 10.4 %copy-start.10 = (f32[2,128]{1,0:T(2,128)S(1)}, f32[2,128]{1,0:T(2,128)}, u32[]{:S(2)}) copy-start(f32[2,128]{1,0:T(2,128)} %gap0.1) | copy-start | bytes 3076
  31.0 11.9 %collective-permute-start.3 = (f32[14,24,128]{2,1,0:T(8,128)S(1)}, f32[14,24,128]{2,1,0:T(8,128)S(1)}, u32[]{:S(2)}, u32[]{:S(2)}) collective-permute-start(f32[14,24,128]{2,1,0:T(8,128)S(1)} %get-tuple-element.25), channel_id=1, source_target_pairs={{1,0},{2,1},{3,2},{4,3},{5,4},{6,5},{7,6},{8,7},{9,8},{10,9},{11,1... | collective-permute-start | bytes 516104 | tf_op jit(solution)/shard_map/ppermute | solution.py:638
  45.0 22.5 %all-to-all-start.1 = ((f32[32,4,128]{2,1,0:T(4,128)}), f32[32,4,128]{2,1,0:T(4,128)S(1)}, u32[]{:S(2)}, u32[]{:S(2)}) async-start(f32[32,4,128]{2,1,0:T(4,128)} %bitcast.2), calls=%async_computation.1 | async-start | bytes 131072 | tf_op jit(solution)/shard_map/all_to_all | solution.py:648
  59.2 0.7 copy-start.5
  59.9 0.7 copy-start.7
  67.5 13.1 %copy-start.6 = (f32[10,48,128]{2,1,0:T(8,128)S(1)}, f32[10,48,128]{2,1,0:T(8,128)}, u32[]{:S(2)}) copy-start(f32[10,48,128]{2,1,0:T(8,128)} %copy-done.5) | copy-start | bytes 737284
  69.8 10.8 %copy-start.8 = (f32[8,32,128]{2,1,0:T(8,128)S(1)}, f32[8,32,128]{2,1,0:T(8,128)}, u32[]{:S(2)}) copy-start(f32[8,32,128]{2,1,0:T(8,128)} %copy-done.7) | copy-start | bytes 393220
  69.8 19.2 %all-to-all-start.2 = ((f32[32,4,128]{2,1,0:T(4,128)}), f32[32,4,128]{2,1,0:T(4,128)S(1)}, u32[]{:S(2)}, u32[]{:S(2)}) async-start(f32[32,4,128]{2,1,0:T(4,128)} %bitcast.4), calls=%async_computation.2 | async-start | bytes 131072 | tf_op jit(solution)/shard_map/all_to_all | solution.py:648
  75.3 7.2 %collective-permute-start.5 = (f32[128,128]{1,0:T(8,128)S(1)}, f32[128,128]{1,0:T(8,128)S(1)}, u32[]{:S(2)}, u32[]{:S(2)}) collective-permute-start(f32[128,128]{1,0:T(8,128)S(1)} %get-tuple-element.31), channel_id=1, source_target_pairs={{1,0},{2,1},{3,2},{4,3},{5,4},{6,5},{7,6},{8,7},{9,8},{10,9},{11,1... | collective-permute-start | bytes 196616 | tf_op jit(solution)/shard_map/ppermute | solution.py:638
  76.6 5.9 %collective-permute-start.4 = (f32[128,128]{1,0:T(8,128)S(1)}, f32[128,128]{1,0:T(8,128)S(1)}, u32[]{:S(2)}, u32[]{:S(2)}) collective-permute-start(f32[128,128]{1,0:T(8,128)S(1)} %get-tuple-element.31), channel_id=1, source_target_pairs={{0,1},{1,2},{2,3},{3,4},{4,5},{5,6},{6,7},{7,8},{8,9},{9,10},{10,1... | collective-permute-start | bytes 196616 | tf_op jit(solution)/shard_map/ppermute | solution.py:638

commit v4 on v3

--- a/solution.py
+++ b/solution.py
@@ -24,19 +24,21 @@
     return lax.broadcasted_iota(jnp.int32, shape, axis)
 
 
-def call(body, outs, args, smem=(), away=(), scratch=(), more=(), limit=16):
+def call(body, outs, args, smem=(), away=(), far=(), scratch=(), more=(), limit=16):
     def space(i):
         return pltpu.SMEM if i in smem else pltpu.HBM if i in away else pltpu.VMEM
 
     specs = [pl.BlockSpec(memory_space=space(i)) for i in range(len(args))]
     many = isinstance(outs, list)
     shapes = [jax.ShapeDtypeStruct(s, F32) for s in (outs if many else [outs])]
-    spec = pl.BlockSpec(memory_space=pltpu.VMEM)
+    kept = [
+        pl.BlockSpec(memory_space=pltpu.HBM if i in far else pltpu.VMEM) for i in range(len(shapes))
+    ]
     return pl.pallas_call(
         body,
         out_shape=shapes if many else shapes[0],
         in_specs=specs,
-        out_specs=[spec] * len(shapes) if many else spec,
+        out_specs=kept if many else kept[0],
         scratch_shapes=[pltpu.VMEM(s, F32) for s in scratch] + list(more),
         compiler_params=pltpu.CompilerParams(vmem_limit_bytes=limit * 1024 * 1024),
     )(*args)
@@ -254,7 +256,7 @@
 def base(
     disp, force, kappa, sigma, low_x, high_x, low_y, high_y,
     res_out, strips, image_out, kap_out, diag_out,
-    fields, diag, res, image, smooth_a, smooth_b, smooth_k,
+    fields, diag, res, image, smooth_a, smooth_b, smooth_k, sems,
 ):
     gx, gy = lax.axis_index("gx"), lax.axis_index("gy")
     lines = tile_lines(disp, force, kappa, sigma)
@@ -295,6 +297,15 @@
             )
             res[c, x] = mask * value
 
+    copies = [
+        pltpu.make_async_copy(
+            res.at[c, pl.ds(3, 8), pl.ds(8, 32)], res_out.at[c], sems.at[c]
+        )
+        for c in range(3)
+    ]
+    for copy in copies:
+        copy.start()
+
     @pl.loop(1, LINES - 1)
     def _(x):
         kap = fields[3, x]
@@ -313,9 +324,6 @@
                 dia * res[c, x] - kap * along(smooth_a, c, x) - along(smooth_b, c, x)
             )
 
-    for c in range(3):
-        for k in range(8):
-            res_out[c, k] = res[c, k + 3, 8:40]
     for k in range(8):
         diag_out[k] = diag[k + 3, 8:40]
     for k in range(10):
@@ -339,6 +347,8 @@
         turned = wide.T
         for kind in range(count):
             strips[kind, group : group + 1, :] = turned[kind : kind + 1]
+    for copy in copies:
+        copy.wait()
 
 
 def base_moments(after, image, kap_lines, diag, res_own, moments, strips, smooth_a, smooth_b, second):
@@ -499,14 +509,14 @@
 
 
 def measure_moments(
-    partner, select_rows, rows, state, mortar, strips, edges, second, moved, low, high,
+    partner, select_rows, rows, state, mortar, strips, edges, second, moved, beside,
     more_strips, moments, package, image_out, padded, surf0, surf1,
 ):
     body, gx = lax.axis_index("body"), lax.axis_index("gx")
     half = rows.shape[0] // 2
     slave, master = spread_row(select_rows, rows)
     y = iota(rows.shape, 1) % 32
-    below_row, above_row = low[...], high[...]
+    below_row, above_row = beside[: 2 * half, :], beside[2 * half :, :]
     plain = jnp.where(y == 0, roll(below_row, -31, 1), jnp.where(y == 31, roll(above_row, 31, 1), 0.0))
     scaled = jnp.where(y == 0, roll(below_row, -30, 1), jnp.where(y == 31, roll(above_row, 30, 1), 0.0))
     plain, scaled = row_line_smooth(plain), row_line_smooth(scaled)
@@ -683,7 +693,9 @@
         base,
         [(3, 8, 32, LANES), (8, 8, LANES), (3, *near), near, (8, 32, LANES)],
         (*tile, *rims),
+        far=(0,),
         scratch=[(8, *lines), lines, wide, wide, wide, wide, lines],
+        more=[pltpu.SemaphoreType.DMA((3,))],
     )
     half = 4 * nx
     work = [(half + 16, LANES), (half, LANES), (half, LANES)]
@@ -694,7 +706,9 @@
         smem=(0,),
         scratch=work,
     )
-    low, high = shifted(message, "gy", 1), shifted(message, "gy", -1)
+    pairs = [(j, j + 1) for j in range(ny - 1)] + [(ny + j + 1, ny + j) for j in range(ny - 1)]
+    message = lax.ppermute(message, ("body", "gy"), pairs)
+    beside = lax.all_gather(message, "body", axis=0, tiled=True)
     rows = trade(package, row)
     moments, more_strips = call(
         base_moments,
@@ -705,7 +719,7 @@
     package, last = call(
         measure_moments,
         [(4 * ny, LANES), (24, LANES)],
-        (partner, surfaces, rows, state, mortar, strips, edges, second, moved, low, high, more_strips, moments),
+        (partner, surfaces, rows, state, mortar, strips, edges, second, moved, beside, more_strips, moments),
         smem=(0,),
         scratch=work,
     )

time: 129 us -> 127 us (0.984)
  starting transfers between devices: 48 us -> 44.2 us
  waiting for transfers between devices: 22.3 us -> 24.3 us
    ppermute x6 -> x4, starting transfers between devices: 15.7 us -> 10.4 us  [shifted(): return lax.ppermute(block, axis, pairs)]
    all_to_all x2, blocking collectives: 37.4 us -> 35.2 us  [trade(): return lax.all_to_all(package, axes, 0, 0, tiled=True)]
    ppermute x0 -> x1, waiting for transfers between devices: none -> 2.1 us  [on_device(): message = lax.ppermute(message, ('body', 'gy'), pairs)]
    all_gather x0 -> x1, blocking collectives: none -> 1.89 us  [on_device(): beside = lax.all_gather(message, 'body', axis=0, tiled=True)]
    ppermute x0 -> x1, starting transfers between devices: none -> 1.29 us  [on_device(): message = lax.ppermute(message, ('body', 'gy'), pairs)]
  transfers between devices with their start and end apart: 9 -> 8, of which waited for: 3 -> 4; matrix products, arithmetic and copies ran while one was open for 0% -> 0% of each run, Pallas kernels for 7% -> 7%
where the time goes in v4:
time: 127 us
  starting transfers between devices  44.2 us (35%)
  blocking collectives  37 us (29%)
  waiting for transfers between devices  24.3 us (19%)
  Pallas kernels  19 us (15%)
  local copies, waits for them, and re-layouts  1.39 us (1%)
    all_to_all x2, blocking collectives, trade(): return lax.all_to_all(package, axes, 0, 0, tiled=True)  35.2 us
    all_to_all x3, starting transfers between devices, trade(): return lax.all_to_all(package, axes, 0, 0, tiled=True)  32.4 us
    all_to_all x3, waiting for transfers between devices, trade(): return lax.all_to_all(package, axes, 0, 0, tiled=True)  22.2 us
    pallas_call x10, Pallas kernels, call(): pl.pallas_call(body, out_shape=shapes if many else shapes[0], in_specs=sp...  19 us
    ppermute x4, starting transfers between devices, shifted(): return lax.ppermute(block, axis, pairs)  10.4 us
  transfers between devices with their start and end apart: 8, of which 4 were waited for; matrix products, arithmetic and copies ran while one was open for 0% of the time, Pallas kernels for 7%

profile of v4, /device:TPU:1, one launch (start us, length us, event | category | flops | bytes accessed | tf_op | source)
XLA Modules:
  0.0 126.8 jit_solution(5697955672805124648)
XLA Ops:
  0.7 2.9 %shard_map.104 = (f32[20,32,128]{2,1,0:T(8,128)}, f32[20,32,128]{2,1,0:T(8,128)}, f32[128,128]{1,0:T(8,128)}) custom-call(s32[2]{0:T(128)} %partner.7, f32[1,3,8,32,128]{4,3,2,1,0:T(8,128)} %disp.7, f32[1,3,8,32,128]{4,3,2,1,0:T(8,128)} %force.7, f32[1,8,32,128]{3,2,1,0:T(8,128)} %kappa.7, f32[1,8,32,128]{3,2,1,0:T(8,128)} %sigma.7), custom_call_target="tpu_custom_call" | custom-call | tf_op jit(solution)/shard_map/pallas_call | solution.py:37
  3.6 4.5 %collective-permute-start = (f32[20,32,128]{2,1,0:T(8,128)}, f32[20,32,128]{2,1,0:T(8,128)S(1)}, u32[]{:S(2)}, u32[]{:S(2)}) collective-permute-start(f32[20,32,128]{2,1,0:T(8,128)} %get-tuple-element.22), channel_id=1, source_target_pairs={{0,16},{16,32},{32,48},{48,64},{64,80},{80,96},{96,112},{112,128},... | collective-permute-start | bytes 983048 | tf_op jit(solution)/shard_map/ppermute | solution.py:648
  8.2 1.3 %collective-permute-start.1 = (f32[20,32,128]{2,1,0:T(8,128)}, f32[20,32,128]{2,1,0:T(8,128)S(1)}, u32[]{:S(2)}, u32[]{:S(2)}) collective-permute-start(f32[20,32,128]{2,1,0:T(8,128)} %get-tuple-element.23), channel_id=1, source_target_pairs={{16,0},{32,16},{48,32},{64,48},{80,64},{96,80},{112,96},{128,112},... | collective-permute-start | bytes 983048 | tf_op jit(solution)/shard_map/ppermute | solution.py:648
  9.5 18.1 %all-to-all-start = ((f32[32,4,128]{2,1,0:T(4,128)}), f32[32,4,128]{2,1,0:T(4,128)S(1)}, u32[]{:S(2)}, u32[]{:S(2)}) async-start(f32[32,4,128]{2,1,0:T(4,128)} %bitcast.19), calls=%async_computation | async-start | bytes 131072 | tf_op jit(solution)/shard_map/all_to_all | solution.py:658
  27.7 3.2 %collective-permute-start.2 = (f32[14,24,128]{2,1,0:T(8,128)S(1)}, f32[14,24,128]{2,1,0:T(8,128)S(1)}, u32[]{:S(2)}, u32[]{:S(2)}) collective-permute-start(f32[14,24,128]{2,1,0:T(8,128)S(1)} %get-tuple-element.24), channel_id=1, source_target_pairs={{0,1},{1,2},{2,3},{3,4},{4,5},{5,6},{6,7},{7,8},{8,9},{9,10},{10,1... | collective-permute-start | bytes 516104 | tf_op jit(solution)/shard_map/ppermute | solution.py:648
  31.0 1.4 %collective-permute-start.3 = (f32[14,24,128]{2,1,0:T(8,128)S(1)}, f32[14,24,128]{2,1,0:T(8,128)S(1)}, u32[]{:S(2)}, u32[]{:S(2)}) collective-permute-start(f32[14,24,128]{2,1,0:T(8,128)S(1)} %get-tuple-element.25), channel_id=1, source_target_pairs={{1,0},{2,1},{3,2},{4,3},{5,4},{6,5},{7,6},{8,7},{9,8},{10,9},{11,1... | collective-permute-start | bytes 516104 | tf_op jit(solution)/shard_map/ppermute | solution.py:648
  32.4 8.9 %all-to-all-done = f32[32,4,128]{2,1,0:T(4,128)S(1)} async-done(((f32[32,4,128]{2,1,0:T(4,128)}), f32[32,4,128]{2,1,0:T(4,128)S(1)}, u32[]{:S(2)}, u32[]{:S(2)}) %all-to-all-start) | async-done | bytes 65568 | tf_op jit(solution)/shard_map/all_to_all | solution.py:658
  41.4 1.5 %shard_map.106.state = f32[16,128]{1,0:T(8,128)S(1)} custom-call(s32[2]{0:T(128)S(1)} %copy-done.9, s32[2]{0:T(128)S(1)} %copy-done.12, f32[128,128]{1,0:T(8,128)S(1)} %bitcast.10, f32[2,128]{1,0:T(2,128)S(1)} %copy-done.10, f32[2,128]{1,0:T(2,128)S(1)} %copy-done.11, f32[2,128,128]{2,1,0:T(8,128)S(1)} %copy-done.4), custom_call_target="tpu_custom_call" | custom-call | tf_op jit(solution)/shard_map/pallas_call | solution.py:37
  42.9 2.0 %shard_map.107 = f32[128,128]{1,0:T(8,128)} custom-call(f32[1,3,8,32,128]{4,3,2,1,0:T(8,128)S(1)} %copy-done, f32[1,3,8,32,128]{4,3,2,1,0:T(8,128)S(1)} %copy-done.1, f32[1,8,32,128]{3,2,1,0:T(8,128)S(1)} %copy-done.2, f32[1,8,32,128]{3,2,1,0:T(8,128)S(1)} %copy-done.3, f32[20,32,128]{2,1,0:T(8,128)S(1)} %collective-permute-done.low.low_x, ...), custom_call_target="tpu_custom_call" | custom-call | tf_op jit(solution)/shard_map/pallas_call | solution.py:37
  44.9 8.7 %all-to-all-start.1 = ((f32[32,4,128]{2,1,0:T(4,128)}), f32[32,4,128]{2,1,0:T(4,128)S(1)}, u32[]{:S(2)}, u32[]{:S(2)}) async-start(f32[32,4,128]{2,1,0:T(4,128)} %bitcast.2), calls=%async_computation.1 | async-start | bytes 131072 | tf_op jit(solution)/shard_map/all_to_all | solution.py:658
  53.7 5.6 %shard_map.108 = (f32[3,8,32,128]{3,2,1,0:T(8,128)S(1)}, f32[8,8,128]{2,1,0:T(8,128)S(1)}, f32[3,10,48,128]{3,2,1,0:T(8,128)S(1)}, f32[10,48,128]{2,1,0:T(8,128)S(1)}, f32[8,32,128]{2,1,0:T(8,128)S(1)}) custom-call(f32[1,3,8,32,128]{4,3,2,1,0:T(8,128)S(1)} %copy-done, f32[1,3,8,32,128]{4,3,2,1,0:T(8,128)S(1)} %copy-done.1, f32[1,8,32,128]{3,2,1,0:T(8,128)S(1)} %copy-done.2, ...), custom_call_target="tpu_custom_call" | custom-call | tf_op jit(solution)/shard_map/pallas_call | solution.py:37
  59.3 0.7 copy-done.5
  60.7 6.8 %all-to-all-done.1 = f32[32,4,128]{2,1,0:T(4,128)S(1)} async-done(((f32[32,4,128]{2,1,0:T(4,128)}), f32[32,4,128]{2,1,0:T(4,128)S(1)}, u32[]{:S(2)}, u32[]{:S(2)}) %all-to-all-start.1) | async-done | bytes 65568 | tf_op jit(solution)/shard_map/all_to_all | solution.py:658
  67.4 2.3 %shard_map.109 = (f32[8,128]{1,0:T(8,128)S(1)}, f32[8,128]{1,0:T(8,128)S(1)}, f32[16,128]{1,0:T(8,128)S(1)}, f32[128,128]{1,0:T(8,128)S(1)}, f32[128,128]{1,0:T(8,128)}) custom-call(s32[2]{0:T(128)S(1)} %copy-done.9, f32[128,128]{1,0:T(8,128)S(1)} %bitcast.11, f32[128,128]{1,0:T(8,128)S(1)} %bitcast.13, f32[16,128]{1,0:T(8,128)S(1)} %shard_map.106.state, ...), custom_call_target="tpu_custom_call" | custom-call | tf_op jit(solution)/shard_map/pallas_call | solution.py:37
  69.8 5.5 %all-to-all-start.2 = ((f32[32,4,128]{2,1,0:T(4,128)}), f32[32,4,128]{2,1,0:T(4,128)S(1)}, u32[]{:S(2)}, u32[]{:S(2)}) async-start(f32[32,4,128]{2,1,0:T(4,128)} %bitcast.4), calls=%async_computation.2 | async-start | bytes 131072 | tf_op jit(solution)/shard_map/all_to_all | solution.py:658
  75.3 1.3 %collective-permute-start.4 = (f32[128,128]{1,0:T(8,128)S(1)}, f32[128,128]{1,0:T(8,128)S(1)}, u32[]{:S(2)}, u32[]{:S(2)}) collective-permute-start(f32[128,128]{1,0:T(8,128)S(1)} %get-tuple-element.31), channel_id=1, source_target_pairs={{0,1},{1,2},{2,3},{3,4},{4,5},{5,6},{6,7},{7,8},{8,9},{9,10},{10,1... | collective-permute-start | bytes 196616 | tf_op jit(solution)/shard_map/ppermute | solution.py:710
  76.6 1.9 %shard_map.110 = (f32[4,8,128]{2,1,0:T(8,128)S(1)}, f32[2,8,128]{2,1,0:T(8,128)S(1)}) custom-call(f32[8,128]{1,0:T(8,128)S(1)} %get-tuple-element.28.after.edges, f32[3,10,48,128]{3,2,1,0:T(8,128)S(1)} %get-tuple-element.32.image, f32[10,48,128]{2,1,0:T(8,128)S(1)} %copy-done.6, f32[8,32,128]{2,1,0:T(8,128)S(1)} %copy-done.8, ...), custom_call_target="tpu_custom_call" | custom-call | tf_op jit(solution)/shard_map/pallas_call | solution.py:37
  78.5 2.1 %collective-permute-done.4 = f32[128,128]{1,0:T(8,128)S(1)} collective-permute-done((f32[128,128]{1,0:T(8,128)S(1)}, f32[128,128]{1,0:T(8,128)S(1)}, u32[]{:S(2)}, u32[]{:S(2)}) %collective-permute-start.4) | collective-permute-done | bytes 65568 | tf_op jit(solution)/shard_map/ppermute | solution.py:710
  80.6 1.9 %all_gather.3.beside = f32[256,128]{1,0:T(8,128)S(1)} all-gather(f32[128,128]{1,0:T(8,128)S(1)} %collective-permute-done.4), channel_id=1, replica_groups=mesh['body'=2,'gx'=16,'gy'=16] {'body'}, dimensions={0}, use_global_device_ids=true | all-gather | bytes 196608 | tf_op jit(solution)/shard_map/all_gather | solution.py:711
  82.5 6.6 %all-to-all-done.2 = f32[32,4,128]{2,1,0:T(4,128)S(1)} async-done(((f32[32,4,128]{2,1,0:T(4,128)}), f32[32,4,128]{2,1,0:T(4,128)S(1)}, u32[]{:S(2)}, u32[]{:S(2)}) %all-to-all-start.2) | async-done | bytes 65568 | tf_op jit(solution)/shard_map/all_to_all | solution.py:658
  89.1 1.3 %shard_map.111 = (f32[64,128]{1,0:T(8,128)S(1)}, f32[24,128]{1,0:T(8,128)S(1)}) custom-call(s32[2]{0:T(128)S(1)} %copy-done.9, f32[128,128]{1,0:T(8,128)S(1)} %bitcast.12, f32[128,128]{1,0:T(8,128)S(1)} %bitcast.14, f32[16,128]{1,0:T(8,128)S(1)} %shard_map.106.state, f32[2,128,128]{2,1,0:T(8,128)S(1)} %copy-done.4, ...), custom_call_target="tpu_custom_call" | custom-call | tf_op jit(solution)/shard_map/pallas_call | solution.py:37
  90.3 14.2 %all_to_all.55 = f32[16,4,128]{2,1,0:T(4,128)S(1)} all-to-all(f32[16,4,128]{2,1,0:T(4,128)S(1)} %bitcast.18), channel_id=1, replica_groups=mesh['body'=2,'gx'=16,'gy'=16] {'gy'}, dimensions={0} | all-to-all | bytes 65536 | tf_op jit(solution)/shard_map/all_to_all | solution.py:658
  104.9 20.9 %all_to_all.56 = f32[32,2,128]{2,1,0:T(2,128)S(1)} all-to-all(f32[32,2,128]{2,1,0:T(2,128)S(1)} %bitcast.17), channel_id=1, replica_groups=mesh['body'=2,'gx'=16,'gy'=16] {'body','gx'}, dimensions={0} | all-to-all | bytes 65536 | tf_op jit(solution)/shard_map/all_to_all | solution.py:658
  125.8 1.0 shard_map.113
  (31 shorter events, 1.1 us)
Async XLA Ops:
  0.6 27.0 %copy-start.1 = (f32[1,3,8,32,128]{4,3,2,1,0:T(8,128)S(1)}, f32[1,3,8,32,128]{4,3,2,1,0:T(8,128)}, u32[]{:S(2)}) copy-start(f32[1,3,8,32,128]{4,3,2,1,0:T(8,128)} %force.7) | copy-start | bytes 1179652
  0.6 27.0 %copy-start = (f32[1,3,8,32,128]{4,3,2,1,0:T(8,128)S(1)}, f32[1,3,8,32,128]{4,3,2,1,0:T(8,128)}, u32[]{:S(2)}) copy-start(f32[1,3,8,32,128]{4,3,2,1,0:T(8,128)} %disp.7) | copy-start | bytes 1179652
  0.6 27.0 %copy-start.3 = (f32[1,8,32,128]{3,2,1,0:T(8,128)S(1)}, f32[1,8,32,128]{3,2,1,0:T(8,128)}, u32[]{:S(2)}) copy-start(f32[1,8,32,128]{3,2,1,0:T(8,128)} %sigma.7) | copy-start | bytes 393220
  3.6 24.1 %copy-start.2 = (f32[1,8,32,128]{3,2,1,0:T(8,128)S(1)}, f32[1,8,32,128]{3,2,1,0:T(8,128)}, u32[]{:S(2)}) copy-start(f32[1,8,32,128]{3,2,1,0:T(8,128)} %kappa.7) | copy-start | bytes 393220
  3.6 24.0 %collective-permute-start = (f32[20,32,128]{2,1,0:T(8,128)}, f32[20,32,128]{2,1,0:T(8,128)S(1)}, u32[]{:S(2)}, u32[]{:S(2)}) collective-permute-start(f32[20,32,128]{2,1,0:T(8,128)} %get-tuple-element.22), channel_id=1, source_target_pairs={{0,16},{16,32},{32,48},{48,64},{64,80},{80,96},{96,112},{112,128},... | collective-permute-start | bytes 983048 | tf_op jit(solution)/shard_map/ppermute | solution.py:648
  8.2 19.5 %collective-permute-start.1 = (f32[20,32,128]{2,1,0:T(8,128)}, f32[20,32,128]{2,1,0:T(8,128)S(1)}, u32[]{:S(2)}, u32[]{:S(2)}) collective-permute-start(f32[20,32,128]{2,1,0:T(8,128)} %get-tuple-element.23), channel_id=1, source_target_pairs={{16,0},{32,16},{48,32},{64,48},{80,64},{96,80},{112,96},{128,112},... | collective-permute-start | bytes 983048 | tf_op jit(solution)/shard_map/ppermute | solution.py:648
  9.5 31.9 %all-to-all-start = ((f32[32,4,128]{2,1,0:T(4,128)}), f32[32,4,128]{2,1,0:T(4,128)S(1)}, u32[]{:S(2)}, u32[]{:S(2)}) async-start(f32[32,4,128]{2,1,0:T(4,128)} %bitcast.19), calls=%async_computation | async-start | bytes 131072 | tf_op jit(solution)/shard_map/all_to_all | solution.py:658
  27.6 13.8 %copy-start.4 = (f32[2,128,128]{2,1,0:T(8,128)S(1)}, f32[2,128,128]{2,1,0:T(8,128)}, u32[]{:S(2)}) copy-start(f32[2,128,128]{2,1,0:T(8,128)} %mortar.5) | copy-start | bytes 393220
  27.7 15.2 %collective-permute-start.2 = (f32[14,24,128]{2,1,0:T(8,128)S(1)}, f32[14,24,128]{2,1,0:T(8,128)S(1)}, u32[]{:S(2)}, u32[]{:S(2)}) collective-permute-start(f32[14,24,128]{2,1,0:T(8,128)S(1)} %get-tuple-element.24), channel_id=1, source_target_pairs={{0,1},{1,2},{2,3},{3,4},{4,5},{5,6},{6,7},{7,8},{8,9},{9,10},{10,1... | collective-permute-start | bytes 516104 | tf_op jit(solution)/shard_map/ppermute | solution.py:648
  31.0 10.4 %copy-start.11 = (f32[2,128]{1,0:T(2,128)S(1)}, f32[2,128]{1,0:T(2,128)}, u32[]{:S(2)}) copy-start(f32[2,128]{1,0:T(2,128)} %pressure.1) | copy-start | bytes 3076
  31.0 10.4 %copy-start.12 = (s32[2]{0:T(128)S(1)}, s32[2]{0:T(128)}, u32[]{:S(2)}) copy-start(s32[2]{0:T(128)} %active.1) | copy-start | bytes 28
  31.0 10.4 %copy-start.9 = (s32[2]{0:T(128)S(1)}, s32[2]{0:T(128)}, u32[]{:S(2)}) copy-start(s32[2]{0:T(128)} %partner.7) | copy-start | bytes 28
  31.0 10.4 %copy-start.10 = (f32[2,128]{1,0:T(2,128)S(1)}, f32[2,128]{1,0:T(2,128)}, u32[]{:S(2)}) copy-start(f32[2,128]{1,0:T(2,128)} %gap0.1) | copy-start | bytes 3076
  31.0 11.9 %collective-permute-start.3 = (f32[14,24,128]{2,1,0:T(8,128)S(1)}, f32[14,24,128]{2,1,0:T(8,128)S(1)}, u32[]{:S(2)}, u32[]{:S(2)}) collective-permute-start(f32[14,24,128]{2,1,0:T(8,128)S(1)} %get-tuple-element.25), channel_id=1, source_target_pairs={{1,0},{2,1},{3,2},{4,3},{5,4},{6,5},{7,6},{8,7},{9,8},{10,9},{11,1... | collective-permute-start | bytes 516104 | tf_op jit(solution)/shard_map/ppermute | solution.py:648
  44.9 22.5 %all-to-all-start.1 = ((f32[32,4,128]{2,1,0:T(4,128)}), f32[32,4,128]{2,1,0:T(4,128)S(1)}, u32[]{:S(2)}, u32[]{:S(2)}) async-start(f32[32,4,128]{2,1,0:T(4,128)} %bitcast.2), calls=%async_computation.1 | async-start | bytes 131072 | tf_op jit(solution)/shard_map/all_to_all | solution.py:658
  59.3 0.7 copy-start.5
  60.0 0.6 copy-start.7
  67.4 9.2 %copy-start.6 = (f32[10,48,128]{2,1,0:T(8,128)S(1)}, f32[10,48,128]{2,1,0:T(8,128)}, u32[]{:S(2)}) copy-start(f32[10,48,128]{2,1,0:T(8,128)} %copy-done.5) | copy-start | bytes 737284
  69.8 6.9 %copy-start.8 = (f32[8,32,128]{2,1,0:T(8,128)S(1)}, f32[8,32,128]{2,1,0:T(8,128)}, u32[]{:S(2)}) copy-start(f32[8,32,128]{2,1,0:T(8,128)} %copy-done.7) | copy-start | bytes 393220
  69.8 19.3 %all-to-all-start.2 = ((f32[32,4,128]{2,1,0:T(4,128)}), f32[32,4,128]{2,1,0:T(4,128)S(1)}, u32[]{:S(2)}, u32[]{:S(2)}) async-start(f32[32,4,128]{2,1,0:T(4,128)} %bitcast.4), calls=%async_computation.2 | async-start | bytes 131072 | tf_op jit(solution)/shard_map/all_to_all | solution.py:658
  75.3 5.3 %collective-permute-start.4 = (f32[128,128]{1,0:T(8,128)S(1)}, f32[128,128]{1,0:T(8,128)S(1)}, u32[]{:S(2)}, u32[]{:S(2)}) collective-permute-start(f32[128,128]{1,0:T(8,128)S(1)} %get-tuple-element.31), channel_id=1, source_target_pairs={{0,1},{1,2},{2,3},{3,4},{4,5},{5,6},{6,7},{7,8},{8,9},{9,10},{10,1... | collective-permute-start | bytes 196616 | tf_op jit(solution)/shard_map/ppermute | solution.py:710

commit v5 on v4

--- a/solution.py
+++ b/solution.py
@@ -13,7 +13,7 @@
 SLABS = 20
 LINES = 14
 ROWS = 48
-KAP0, KAP1, DIA0, DIA1, RES0, IM0, IM1 = 0, 1, 2, 3, 4, 6, 7
+KAP0, KAP1, DIA0, DIA1, RES0, IM0, IM1, SEC0, SEC1 = 0, 1, 2, 3, 4, 6, 7, 8, 9
 
 
 def roll(value, step, axis):
@@ -64,6 +64,14 @@
         lambda x: force[0, 2, x],
         lambda x: sigma[0, x],
     )
+
+
+def each(first, last):
+    def run(body):
+        for k in range(first, last):
+            body(k)
+
+    return run
 
 
 def pack_x(partner, disp, force, kappa, sigma, up, down, package, surface, sems):
@@ -230,14 +238,14 @@
         put_line(kap_lines, ext_line(lines[3], low_x, high_x, 3, x), low_y, high_y, 3, x)
     in_plane = plane_smoother()
 
-    @pl.loop(2, LINES - 2)
+    @each(2, LINES - 2)
     def _(x):
         kap, value = kap_lines[x], moved[x]
         smooth_k[x] = in_plane(kap)
         smooth_a[x] = in_plane(value)
         smooth_b[x] = in_plane(kap * value)
 
-    @pl.loop(0, 8)
+    @each(0, 8)
     def _(k):
         x = k + 3
         kap = kap_lines[x]
@@ -253,137 +261,127 @@
     fill(package, stack_rows([four, four]))
 
 
-def base(
-    disp, force, kappa, sigma, low_x, high_x, low_y, high_y,
-    res_out, strips, image_out, kap_out, diag_out,
-    fields, diag, res, image, smooth_a, smooth_b, smooth_k, sems,
-):
-    gx, gy = lax.axis_index("gx"), lax.axis_index("gy")
-    lines = tile_lines(disp, force, kappa, sigma)
-    for field in range(8):
-        for x in range(LINES):
-            value = ext_line(lines[field], low_x, high_x, field, x)
-            if value is not None:
-                put_line(fields.at[field], value, low_y, high_y, field, x)
-    row = iota((ROWS, LANES), 0)
-    in_plane = plane_smoother()
-    row_low = jnp.where(gy == 0, 8, 0)
-    row_high = jnp.where(gy == lax.axis_size("gy") - 1, 40, ROWS)
-    inside_y = jnp.where((row >= row_low) & (row < row_high), 1.0, 0.0).astype(F32)
-    line_low = jnp.where(gx == 0, 3, 0)
-    line_high = jnp.where(gx == lax.axis_size("gx") - 1, 11, LINES)
-
-    def inside(x):
-        return inside_y * jnp.where((x >= line_low) & (x < line_high), 1.0, 0.0).astype(F32)
-
-    @pl.loop(0, LINES)
-    def _(x):
-        kap = fields[3, x]
-        smooth_k[x] = in_plane(kap)
-        for c in range(3):
-            value = fields[c, x]
-            smooth_a[c, x] = in_plane(value)
-            smooth_b[c, x] = in_plane(kap * value)
-
-    @pl.loop(1, LINES - 1)
-    def _(x):
-        kap = fields[3, x]
-        dia = fields[7, x] + 8.0 * kap + along(smooth_k, x)
-        diag[x] = dia
-        mask = inside(x)
-        for c in range(3):
-            value = fields[4 + c, x] - (
-                dia * fields[c, x] - kap * along(smooth_a, c, x) - along(smooth_b, c, x)
-            )
-            res[c, x] = mask * value
-
-    copies = [
-        pltpu.make_async_copy(
-            res.at[c, pl.ds(3, 8), pl.ds(8, 32)], res_out.at[c], sems.at[c]
+def base(comps, surface):
+    count = len(comps)
+
+    def kernel(disp, force, kappa, sigma, low_x, high_x, low_y, high_y, after, *rest):
+        res_out, image_out, moments, *rest = rest
+        if surface:
+            strips, *rest = rest
+        inputs, pushes, kap_lines, sig_lines, diag, res, image, smooth_a, smooth_b, smooth_k, second = rest
+        gx, gy = lax.axis_index("gx"), lax.axis_index("gy")
+        lines = tile_lines(disp, force, kappa, sigma)
+        targets = [(c, inputs.at[k]) for k, c in enumerate(comps)]
+        targets += [(4 + c, pushes.at[k]) for k, c in enumerate(comps)]
+        targets += [(3, kap_lines), (7, sig_lines)]
+        for field, target in targets:
+            for x in range(LINES):
+                value = ext_line(lines[field], low_x, high_x, field, x)
+                if value is not None:
+                    put_line(target, value, low_y, high_y, field, x)
+        row = iota((ROWS, LANES), 0)
+        in_plane = plane_smoother()
+        row_low = jnp.where(gy == 0, 8, 0)
+        row_high = jnp.where(gy == lax.axis_size("gy") - 1, 40, ROWS)
+        inside_y = jnp.where((row >= row_low) & (row < row_high), 1.0, 0.0).astype(F32)
+        line_low = jnp.where(gx == 0, 3, 0)
+        line_high = jnp.where(gx == lax.axis_size("gx") - 1, 11, LINES)
+
+        def inside(x):
+            return inside_y * jnp.where((x >= line_low) & (x < line_high), 1.0, 0.0).astype(F32)
+
+        def smooth_all(source, first):
+            @each(first, LINES - first)
+            def _(x):
+                kap = kap_lines[x]
+                if first == 0:
+                    smooth_k[x] = in_plane(kap)
+                for c in range(count):
+                    value = source[c, x]
+                    smooth_a[c, x] = in_plane(value)
+                    smooth_b[c, x] = in_plane(kap * value)
+
+        smooth_all(inputs, 0)
+
+        @each(1, LINES - 1)
+        def _(x):
+            kap = kap_lines[x]
+            dia = sig_lines[x] + 8.0 * kap + along(smooth_k, x)
+            diag[x] = dia
+            mask = inside(x)
+            for c in range(count):
+                value = pushes[c, x] - (
+                    dia * inputs[c, x] - kap * along(smooth_a, c, x) - along(smooth_b, c, x)
+                )
+                res[c, x] = mask * value
+
+        smooth_all(res, 1)
+
+        @each(2, LINES - 2)
+        def _(x):
+            kap, dia = kap_lines[x], diag[x]
+            mask = inside(x)
+            for c in range(count):
+                image[c, x] = mask * (
+                    dia * res[c, x] - kap * along(smooth_a, c, x) - along(smooth_b, c, x)
+                )
+
+        smooth_all(image, 2)
+
+        def finish_line(k, sums):
+            x = k + 3
+            kap, dia = kap_lines[x, 8:40], diag[x, 8:40]
+            sums = list(sums)
+            for c in range(count):
+                r, p = res[c, x, 8:40], image[c, x, 8:40]
+                q = dia * p - kap * along(smooth_a, c, x)[8:40] - along(smooth_b, c, x)[8:40]
+                if surface:
+                    second[k] = q
+                res_out[c, k] = r
+                image_out[c, k] = p
+                for i, (a, b) in enumerate(((r, r), (r, p), (p, p), (p, q))):
+                    product = (a * b).reshape(4, 8, LANES)
+                    sums[i] = sums[i] + ((product[0] + product[1]) + (product[2] + product[3]))
+            return tuple(sums)
+
+        sums = (jnp.zeros((8, LANES), F32),) * 4
+        for k in range(8):
+            sums = finish_line(k, sums)
+        for i in range(4):
+            moments[i] = sums[i]
+        if not surface:
+            return
+        strips[...] = jnp.zeros(strips.shape, F32)
+        lanes = iota((LANES, LANES), 1)
+        for group in range(4):
+            near = [min(max(4 * group - 1 + k, 1), LINES - 2) for k in range(4)]
+            wide = stack_rows([kap_lines[x, 8:40] for x in near])
+            wide = jnp.where(lanes < 2, wide, roll(stack_rows([diag[x, 8:40] for x in near]), 2, 1))
+            total_kinds = 4
+            if group in (1, 2):
+                total_kinds = 10
+                for at, piece in (
+                    (4, stack_rows([res[0, x, 8:40] for x in near])),
+                    (6, stack_rows([image[0, x, 8:40] for x in near])),
+                    (8, stack_rows([second[x - 3] for x in near])),
+                ):
+                    wide = jnp.where(lanes < at, wide, roll(piece, at, 1))
+            turned = wide.T
+            for kind in range(total_kinds):
+                strips[kind, group : group + 1, :] = turned[kind : kind + 1]
+
+    def run(args):
+        lines, wide = (LINES, ROWS, LANES), (count, LINES, ROWS, LANES)
+        own = (count, 8, 32, LANES)
+        outs = [own, own, (4, 8, LANES)] + ([(16, 8, LANES)] if surface else [])
+        return call(
+            kernel,
+            outs,
+            args,
+            scratch=[wide, wide, lines, lines, lines, wide, wide, wide, wide, lines, (8, 32, LANES)],
         )
-        for c in range(3)
-    ]
-    for copy in copies:
-        copy.start()
-
-    @pl.loop(1, LINES - 1)
-    def _(x):
-        kap = fields[3, x]
-        for c in range(3):
-            value = res[c, x]
-            smooth_a[c, x] = in_plane(value)
-            smooth_b[c, x] = in_plane(kap * value)
-
-    @pl.loop(2, LINES - 2)
-    def _(x):
-        kap = fields[3, x]
-        dia = diag[x]
-        mask = inside(x)
-        for c in range(3):
-            image[c, x] = mask * (
-                dia * res[c, x] - kap * along(smooth_a, c, x) - along(smooth_b, c, x)
-            )
-
-    for k in range(8):
-        diag_out[k] = diag[k + 3, 8:40]
-    for k in range(10):
-        kap_out[k] = fields[3, k + 2]
-        for c in range(3):
-            image_out[c, k] = image[c, k + 2]
-    strips[...] = jnp.zeros(strips.shape, F32)
-    lanes = iota((LANES, LANES), 1)
-    for group in range(4):
-        near = [min(max(4 * group - 1 + k, 1), LINES - 2) for k in range(4)]
-        wide = stack_rows([fields[3, x, 8:40] for x in near])
-        wide = jnp.where(lanes < 2, wide, roll(stack_rows([diag[x, 8:40] for x in near]), 2, 1))
-        count = 4
-        if group in (1, 2):
-            count = 8
-            for at, piece in (
-                (4, stack_rows([res[2, x, 8:40] for x in near])),
-                (6, stack_rows([image[2, x, 8:40] for x in near])),
-            ):
-                wide = jnp.where(lanes < at, wide, roll(piece, at, 1))
-        turned = wide.T
-        for kind in range(count):
-            strips[kind, group : group + 1, :] = turned[kind : kind + 1]
-    for copy in copies:
-        copy.wait()
-
-
-def base_moments(after, image, kap_lines, diag, res_own, moments, strips, smooth_a, smooth_b, second):
-    in_plane = plane_smoother()
-
-    @pl.loop(0, 10)
-    def _(x):
-        kap = kap_lines[x]
-        for c in range(3):
-            value = image[c, x]
-            smooth_a[c, x] = in_plane(value)
-            smooth_b[c, x] = in_plane(kap * value)
-
-    def finish_line(k, sums):
-        x = k + 1
-        kap, dia = kap_lines[x, 8:40], diag[k]
-        sums = list(sums)
-        for c in range(3):
-            r, p = res_own[c, k], image[c, x, 8:40]
-            q = dia * p - kap * along(smooth_a, c, x)[8:40] - along(smooth_b, c, x)[8:40]
-            if c == 2:
-                second[k] = q
-            for i, (a, b) in enumerate(((r, r), (r, p), (p, p), (p, q))):
-                product = (a * b).reshape(4, 8, LANES)
-                sums[i] = sums[i] + ((product[0] + product[1]) + (product[2] + product[3]))
-        return tuple(sums)
-
-    sums = lax.fori_loop(0, 8, finish_line, (jnp.zeros((8, LANES), F32),) * 4)
-    for i in range(4):
-        moments[i] = sums[i]
-    strips[...] = jnp.zeros(strips.shape, F32)
-    for group in range(2):
-        turned = second[4 * group : 4 * group + 4].reshape(LANES, LANES).T
-        for kind in range(2):
-            strips[kind, 1 + group : 2 + group, :] = turned[kind : kind + 1]
+
+    return run
 
 
 def spread_row(select_rows, rows):
@@ -510,7 +508,7 @@
 
 def measure_moments(
     partner, select_rows, rows, state, mortar, strips, edges, second, moved, beside,
-    more_strips, moments, package, image_out, padded, surf0, surf1,
+    moments, more_moments, package, image_out, padded, surf0, surf1,
 ):
     body, gx = lax.axis_index("body"), lax.axis_index("gx")
     half = rows.shape[0] // 2
@@ -556,16 +554,16 @@
         return total(jnp.where(own, value, 0.0))
 
     im0, im1 = strips[IM0], strips[IM1]
-    mu0 = total(moments[0]) + surface_sum(first * (2.0 * strips[RES0] + first))
-    mu1 = total(moments[1]) + surface_sum(first * (2.0 * im0 + k_first)) + once * total(push_sum)
-    mu2 = total(moments[2]) + surface_sum(top * (2.0 * im0 + top) + below * (2.0 * im1 + below))
+    mu0 = total(moments[0] + more_moments[0]) + surface_sum(first * (2.0 * strips[RES0] + first))
+    mu1 = total(moments[1] + more_moments[1]) + surface_sum(first * (2.0 * im0 + k_first)) + once * total(push_sum)
+    mu2 = total(moments[2] + more_moments[2]) + surface_sum(top * (2.0 * im0 + top) + below * (2.0 * im1 + below))
     t_top = line_smooth(row_smooth(top + 0.5 * below))
     t_below = line_smooth(row_smooth(0.5 * top + below))
     mu3 = (
-        total(moments[3])
+        total(moments[3] + more_moments[3])
         + surface_sum(
-            top * (2.0 * more_strips[0] + strips[DIA0] * top - 2.0 * kap0 * t_top)
-            + below * (2.0 * more_strips[1] + strips[DIA1] * below - 2.0 * kap1 * t_below)
+            top * (2.0 * strips[SEC0] + strips[DIA0] * top - 2.0 * kap0 * t_top)
+            + below * (2.0 * strips[SEC1] + strips[DIA1] * below - 2.0 * kap1 * t_below)
         )
         + once * total(gap_sum)
     )
@@ -605,7 +603,7 @@
     fill(package, jnp.where(index % 2 == 0, sums, 0.0))
 
 
-def finish(rows, res, image, state, edges, second, last, increment, new_press):
+def finish(rows, res, image, res_2, image_2, state, edges, second, last, increment, new_press):
     sums = jnp.sum(rows[...], axis=0, keepdims=True)
     lane = iota((1, LANES), 1)
     m0, m1, m2, m3 = [
@@ -630,8 +628,8 @@
     wide_im = jnp.broadcast_to(c_im, (8, LANES)).reshape(1, 8, LANES)
     for c in range(3):
         for x in range(8):
-            r = res[c, x].reshape(4, 8, LANES)
-            p = image[c, x + 1, 8:40].reshape(4, 8, LANES)
+            r = (res_2[0, x] if c == 2 else res[c, x]).reshape(4, 8, LANES)
+            p = (image_2[0, x] if c == 2 else image[c, x]).reshape(4, 8, LANES)
             increment[0, c, x] = (wide_res * r + wide_im * p).reshape(32, LANES)
     for k in range(2):
         top = c_res * edges[1 + k : 2 + k, :] + c_im * last[9 + k : 10 + k, :]
@@ -688,15 +686,7 @@
         scratch=[lines, lines, lines, lines, lines, (8, 32, LANES)],
     )
     rows = trade(package, row)
-    wide, near = (3, *lines), (10, ROWS, LANES)
-    res, strips, image, ext_kappa, diag = call(
-        base,
-        [(3, 8, 32, LANES), (8, 8, LANES), (3, *near), near, (8, 32, LANES)],
-        (*tile, *rims),
-        far=(0,),
-        scratch=[(8, *lines), lines, wide, wide, wide, wide, lines],
-        more=[pltpu.SemaphoreType.DMA((3,))],
-    )
+    res_2, image_2, moments, strips = base((2,), True)((*tile, *rims, package))
     half = 4 * nx
     work = [(half + 16, LANES), (half, LANES), (half, LANES)]
     edges, second, moved, message, package = call(
@@ -710,16 +700,11 @@
     message = lax.ppermute(message, ("body", "gy"), pairs)
     beside = lax.all_gather(message, "body", axis=0, tiled=True)
     rows = trade(package, row)
-    moments, more_strips = call(
-        base_moments,
-        [(4, 8, LANES), (2, 8, LANES)],
-        (edges, image, ext_kappa, diag, res),
-        scratch=[(3, *near), (3, *near), (8, 32, LANES)],
-    )
+    res, image, more_moments = base((0, 1), False)((*tile, *rims, edges))
     package, last = call(
         measure_moments,
         [(4 * ny, LANES), (24, LANES)],
-        (partner, surfaces, rows, state, mortar, strips, edges, second, moved, beside, more_strips, moments),
+        (partner, surfaces, rows, state, mortar, strips, edges, second, moved, beside, moments, more_moments),
         smem=(0,),
         scratch=work,
     )
@@ -728,7 +713,7 @@
     increment, new_press = call(
         finish,
         [disp.shape, gap0.shape],
-        (sums, res, image, state, edges, second, last),
+        (sums, res, image, res_2, image_2, state, edges, second, last),
     )
     return (increment, new_press)
 

time: 127 us -> 124 us (0.976)
  Pallas kernels: 19 us -> 15.5 us
  waiting for transfers between devices: 24.3 us -> 27.7 us
  starting transfers between devices: 44.2 us -> 42.2 us
  local copies, waits for them, and re-layouts: 1.39 us -> 0.05 us
    all_to_all x3, waiting for transfers between devices: 22.2 us -> 26.1 us  [trade(): return lax.all_to_all(package, axes, 0, 0, tiled=True)]
    pallas_call x10, Pallas kernels: 19 us -> 15.5 us  [call(): pl.pallas_call(body, out_shape=shapes if many else shapes[0], in_specs=sp...]
    all_to_all x3, starting transfers between devices: 32.4 us -> 30.5 us  [trade(): return lax.all_to_all(package, axes, 0, 0, tiled=True)]
    unnamed x26 -> x18, local copies, waits for them, and re-layouts: 1.39 us -> 0.05 us
  transfers between devices with their start and end apart: 8 -> 8, of which waited for: 4 -> 4; matrix products, arithmetic and copies ran while one was open for 0% -> 0% of each run, Pallas kernels for 7% -> 5%
where the time goes in v5:
time: 124 us
  starting transfers between devices  42.2 us (34%)
  blocking collectives  37.3 us (30%)
  waiting for transfers between devices  27.7 us (22%)
  Pallas kernels  15.5 us (12%)
    all_to_all x2, blocking collectives, trade(): return lax.all_to_all(package, axes, 0, 0, tiled=True)  35.2 us
    all_to_all x3, starting transfers between devices, trade(): return lax.all_to_all(package, axes, 0, 0, tiled=True)  30.5 us
    all_to_all x3, waiting for transfers between devices, trade(): return lax.all_to_all(package, axes, 0, 0, tiled=True)  26.1 us
    pallas_call x10, Pallas kernels, call(): pl.pallas_call(body, out_shape=shapes if many else shapes[0], in_specs=sp...  15.5 us
    ppermute x4, starting transfers between devices, shifted(): return lax.ppermute(block, axis, pairs)  10.4 us
  transfers between devices with their start and end apart: 8, of which 4 were waited for; matrix products, arithmetic and copies ran while one was open for 0% of the time, Pallas kernels for 5%

profile of v5, /device:TPU:1, one launch (start us, length us, event | category | flops | bytes accessed | tf_op | source)
XLA Modules:
  0.0 123.7 jit_solution(17600178352190920972)
XLA Ops:
  0.7 3.0 %shard_map.104 = (f32[20,32,128]{2,1,0:T(8,128)}, f32[20,32,128]{2,1,0:T(8,128)}, f32[128,128]{1,0:T(8,128)}) custom-call(s32[2]{0:T(128)} %partner.7, f32[1,3,8,32,128]{4,3,2,1,0:T(8,128)} %disp.9, f32[1,3,8,32,128]{4,3,2,1,0:T(8,128)} %force.9, f32[1,8,32,128]{3,2,1,0:T(8,128)} %kappa.9, f32[1,8,32,128]{3,2,1,0:T(8,128)} %sigma.9), custom_call_target="tpu_custom_call" | custom-call | tf_op jit(solution)/shard_map/pallas_call | solution.py:37
  3.6 4.5 %collective-permute-start = (f32[20,32,128]{2,1,0:T(8,128)}, f32[20,32,128]{2,1,0:T(8,128)S(1)}, u32[]{:S(2)}, u32[]{:S(2)}) collective-permute-start(f32[20,32,128]{2,1,0:T(8,128)} %get-tuple-element.22), channel_id=1, source_target_pairs={{0,16},{16,32},{32,48},{48,64},{64,80},{80,96},{96,112},{112,128},... | collective-permute-start | bytes 983048 | tf_op jit(solution)/shard_map/ppermute | solution.py:646
  8.2 1.3 %collective-permute-start.1 = (f32[20,32,128]{2,1,0:T(8,128)}, f32[20,32,128]{2,1,0:T(8,128)S(1)}, u32[]{:S(2)}, u32[]{:S(2)}) collective-permute-start(f32[20,32,128]{2,1,0:T(8,128)} %get-tuple-element.23), channel_id=1, source_target_pairs={{16,0},{32,16},{48,32},{64,48},{80,64},{96,80},{112,96},{128,112},... | collective-permute-start | bytes 983048 | tf_op jit(solution)/shard_map/ppermute | solution.py:646
  9.5 18.1 %all-to-all-start = ((f32[32,4,128]{2,1,0:T(4,128)}), f32[32,4,128]{2,1,0:T(4,128)S(1)}, u32[]{:S(2)}, u32[]{:S(2)}) async-start(f32[32,4,128]{2,1,0:T(4,128)} %bitcast.19), calls=%async_computation | async-start | bytes 131072 | tf_op jit(solution)/shard_map/all_to_all | solution.py:656
  27.8 3.2 %collective-permute-start.2 = (f32[14,24,128]{2,1,0:T(8,128)S(1)}, f32[14,24,128]{2,1,0:T(8,128)S(1)}, u32[]{:S(2)}, u32[]{:S(2)}) collective-permute-start(f32[14,24,128]{2,1,0:T(8,128)S(1)} %get-tuple-element.24), channel_id=1, source_target_pairs={{0,1},{1,2},{2,3},{3,4},{4,5},{5,6},{6,7},{7,8},{8,9},{9,10},{10,1... | collective-permute-start | bytes 516104 | tf_op jit(solution)/shard_map/ppermute | solution.py:646
  31.0 1.4 %collective-permute-start.3 = (f32[14,24,128]{2,1,0:T(8,128)S(1)}, f32[14,24,128]{2,1,0:T(8,128)S(1)}, u32[]{:S(2)}, u32[]{:S(2)}) collective-permute-start(f32[14,24,128]{2,1,0:T(8,128)S(1)} %get-tuple-element.25), channel_id=1, source_target_pairs={{1,0},{2,1},{3,2},{4,3},{5,4},{6,5},{7,6},{8,7},{9,8},{10,9},{11,1... | collective-permute-start | bytes 516104 | tf_op jit(solution)/shard_map/ppermute | solution.py:646
  32.5 8.9 %all-to-all-done = f32[32,4,128]{2,1,0:T(4,128)S(1)} async-done(((f32[32,4,128]{2,1,0:T(4,128)}), f32[32,4,128]{2,1,0:T(4,128)S(1)}, u32[]{:S(2)}, u32[]{:S(2)}) %all-to-all-start) | async-done | bytes 65568 | tf_op jit(solution)/shard_map/all_to_all | solution.py:656
  41.4 1.5 %shard_map.106.state = f32[16,128]{1,0:T(8,128)S(1)} custom-call(s32[2]{0:T(128)S(1)} %copy-done.5, s32[2]{0:T(128)S(1)} %copy-done.8, f32[128,128]{1,0:T(8,128)S(1)} %bitcast.10, f32[2,128]{1,0:T(2,128)S(1)} %copy-done.6, f32[2,128]{1,0:T(2,128)S(1)} %copy-done.7, f32[2,128,128]{2,1,0:T(8,128)S(1)} %copy-done.4), custom_call_target="tpu_custom_call" | custom-call | tf_op jit(solution)/shard_map/pallas_call | solution.py:37
  42.9 1.2 shard_map.107.after
  44.1 8.7 %all-to-all-start.1 = ((f32[32,4,128]{2,1,0:T(4,128)}), f32[32,4,128]{2,1,0:T(4,128)S(1)}, u32[]{:S(2)}, u32[]{:S(2)}) async-start(f32[32,4,128]{2,1,0:T(4,128)} %bitcast.2), calls=%async_computation.1 | async-start | bytes 131072 | tf_op jit(solution)/shard_map/all_to_all | solution.py:656
  52.8 2.5 %shard_map.108 = (f32[1,8,32,128]{3,2,1,0:T(8,128)S(1)}, f32[1,8,32,128]{3,2,1,0:T(8,128)S(1)}, f32[4,8,128]{2,1,0:T(8,128)S(1)}, f32[16,8,128]{2,1,0:T(8,128)S(1)}) custom-call(f32[1,3,8,32,128]{4,3,2,1,0:T(8,128)S(1)} %copy-done, f32[1,3,8,32,128]{4,3,2,1,0:T(8,128)S(1)} %copy-done.1, f32[1,8,32,128]{3,2,1,0:T(8,128)S(1)} %copy-done.2, ...), custom_call_target="tpu_custom_call" | custom-call | tf_op jit(solution)/shard_map/pallas_call | solution.py:37
  55.3 11.3 %all-to-all-done.1 = f32[32,4,128]{2,1,0:T(4,128)S(1)} async-done(((f32[32,4,128]{2,1,0:T(4,128)}), f32[32,4,128]{2,1,0:T(4,128)S(1)}, u32[]{:S(2)}, u32[]{:S(2)}) %all-to-all-start.1) | async-done | bytes 65568 | tf_op jit(solution)/shard_map/all_to_all | solution.py:656
  66.6 2.3 %shard_map.109 = (f32[8,128]{1,0:T(8,128)S(1)}, f32[8,128]{1,0:T(8,128)S(1)}, f32[16,128]{1,0:T(8,128)S(1)}, f32[128,128]{1,0:T(8,128)S(1)}, f32[128,128]{1,0:T(8,128)}) custom-call(s32[2]{0:T(128)S(1)} %copy-done.5, f32[128,128]{1,0:T(8,128)S(1)} %bitcast.11, f32[128,128]{1,0:T(8,128)S(1)} %bitcast.14, f32[16,128]{1,0:T(8,128)S(1)} %shard_map.106.state, ...), custom_call_target="tpu_custom_call" | custom-call | tf_op jit(solution)/shard_map/pallas_call | solution.py:37
  68.9 3.6 %all-to-all-start.2 = ((f32[32,4,128]{2,1,0:T(4,128)}), f32[32,4,128]{2,1,0:T(4,128)S(1)}, u32[]{:S(2)}, u32[]{:S(2)}) async-start(f32[32,4,128]{2,1,0:T(4,128)} %bitcast.4), calls=%async_computation.2 | async-start | bytes 131072 | tf_op jit(solution)/shard_map/all_to_all | solution.py:656
  72.6 1.3 %collective-permute-start.4 = (f32[128,128]{1,0:T(8,128)S(1)}, f32[128,128]{1,0:T(8,128)S(1)}, u32[]{:S(2)}, u32[]{:S(2)}) collective-permute-start(f32[128,128]{1,0:T(8,128)S(1)} %get-tuple-element.31), channel_id=1, source_target_pairs={{0,1},{1,2},{2,3},{3,4},{4,5},{5,6},{6,7},{7,8},{8,9},{9,10},{10,1... | collective-permute-start | bytes 196616 | tf_op jit(solution)/shard_map/ppermute | solution.py:700
  73.9 2.4 %shard_map.110 = (f32[2,8,32,128]{3,2,1,0:T(8,128)S(1)}, f32[2,8,32,128]{3,2,1,0:T(8,128)S(1)}, f32[4,8,128]{2,1,0:T(8,128)S(1)}) custom-call(f32[1,3,8,32,128]{4,3,2,1,0:T(8,128)S(1)} %copy-done, f32[1,3,8,32,128]{4,3,2,1,0:T(8,128)S(1)} %copy-done.1, f32[1,8,32,128]{3,2,1,0:T(8,128)S(1)} %copy-done.2, f32[1,8,32,128]{3,2,1,0:T(8,128)S(1)} %copy-done.3, ...), custom_call_target="tpu_custom_call" | custom-call | tf_op jit(solution)/shard_map/pallas_call | solution.py:37
  76.3 1.6 %collective-permute-done.4 = f32[128,128]{1,0:T(8,128)S(1)} collective-permute-done((f32[128,128]{1,0:T(8,128)S(1)}, f32[128,128]{1,0:T(8,128)S(1)}, u32[]{:S(2)}, u32[]{:S(2)}) %collective-permute-start.4) | collective-permute-done | bytes 65568 | tf_op jit(solution)/shard_map/ppermute | solution.py:700
  77.9 2.0 %all_gather.3.beside = f32[256,128]{1,0:T(8,128)S(1)} all-gather(f32[128,128]{1,0:T(8,128)S(1)} %collective-permute-done.4), channel_id=1, replica_groups=mesh['body'=2,'gx'=16,'gy'=16] {'body'}, dimensions={0}, use_global_device_ids=true | all-gather | bytes 196608 | tf_op jit(solution)/shard_map/all_gather | solution.py:701
  79.9 6.0 %all-to-all-done.2 = f32[32,4,128]{2,1,0:T(4,128)S(1)} async-done(((f32[32,4,128]{2,1,0:T(4,128)}), f32[32,4,128]{2,1,0:T(4,128)S(1)}, u32[]{:S(2)}, u32[]{:S(2)}) %all-to-all-start.2) | async-done | bytes 65568 | tf_op jit(solution)/shard_map/all_to_all | solution.py:656
  85.9 1.3 %shard_map.111 = (f32[64,128]{1,0:T(8,128)S(1)}, f32[24,128]{1,0:T(8,128)S(1)}) custom-call(s32[2]{0:T(128)S(1)} %copy-done.5, f32[128,128]{1,0:T(8,128)S(1)} %bitcast.12, f32[128,128]{1,0:T(8,128)S(1)} %bitcast.13, f32[16,128]{1,0:T(8,128)S(1)} %shard_map.106.state, f32[2,128,128]{2,1,0:T(8,128)S(1)} %copy-done.4, ...), custom_call_target="tpu_custom_call" | custom-call | tf_op jit(solution)/shard_map/pallas_call | solution.py:37
  87.2 14.2 %all_to_all.55 = f32[16,4,128]{2,1,0:T(4,128)S(1)} all-to-all(f32[16,4,128]{2,1,0:T(4,128)S(1)} %bitcast.18), channel_id=1, replica_groups=mesh['body'=2,'gx'=16,'gy'=16] {'gy'}, dimensions={0} | all-to-all | bytes 65536 | tf_op jit(solution)/shard_map/all_to_all | solution.py:656
  101.4 0.3 shard_map.112
  101.7 21.0 %all_to_all.56 = f32[32,2,128]{2,1,0:T(2,128)S(1)} all-to-all(f32[32,2,128]{2,1,0:T(2,128)S(1)} %bitcast.17), channel_id=1, replica_groups=mesh['body'=2,'gx'=16,'gy'=16] {'body','gx'}, dimensions={0} | all-to-all | bytes 65536 | tf_op jit(solution)/shard_map/all_to_all | solution.py:656
  122.7 1.0 shard_map.113
  (23 shorter events, 0.1 us)
Async XLA Ops:
  0.6 27.0 %copy-start.1 = (f32[1,3,8,32,128]{4,3,2,1,0:T(8,128)S(1)}, f32[1,3,8,32,128]{4,3,2,1,0:T(8,128)}, u32[]{:S(2)}) copy-start(f32[1,3,8,32,128]{4,3,2,1,0:T(8,128)} %force.9) | copy-start | bytes 1179652
  0.6 27.0 %copy-start = (f32[1,3,8,32,128]{4,3,2,1,0:T(8,128)S(1)}, f32[1,3,8,32,128]{4,3,2,1,0:T(8,128)}, u32[]{:S(2)}) copy-start(f32[1,3,8,32,128]{4,3,2,1,0:T(8,128)} %disp.9) | copy-start | bytes 1179652
  0.6 27.0 %copy-start.3 = (f32[1,8,32,128]{3,2,1,0:T(8,128)S(1)}, f32[1,8,32,128]{3,2,1,0:T(8,128)}, u32[]{:S(2)}) copy-start(f32[1,8,32,128]{3,2,1,0:T(8,128)} %sigma.9) | copy-start | bytes 393220
  3.6 24.1 %copy-start.2 = (f32[1,8,32,128]{3,2,1,0:T(8,128)S(1)}, f32[1,8,32,128]{3,2,1,0:T(8,128)}, u32[]{:S(2)}) copy-start(f32[1,8,32,128]{3,2,1,0:T(8,128)} %kappa.9) | copy-start | bytes 393220
  3.6 24.0 %collective-permute-start = (f32[20,32,128]{2,1,0:T(8,128)}, f32[20,32,128]{2,1,0:T(8,128)S(1)}, u32[]{:S(2)}, u32[]{:S(2)}) collective-permute-start(f32[20,32,128]{2,1,0:T(8,128)} %get-tuple-element.22), channel_id=1, source_target_pairs={{0,16},{16,32},{32,48},{48,64},{64,80},{80,96},{96,112},{112,128},... | collective-permute-start | bytes 983048 | tf_op jit(solution)/shard_map/ppermute | solution.py:646
  8.2 19.5 %collective-permute-start.1 = (f32[20,32,128]{2,1,0:T(8,128)}, f32[20,32,128]{2,1,0:T(8,128)S(1)}, u32[]{:S(2)}, u32[]{:S(2)}) collective-permute-start(f32[20,32,128]{2,1,0:T(8,128)} %get-tuple-element.23), channel_id=1, source_target_pairs={{16,0},{32,16},{48,32},{64,48},{80,64},{96,80},{112,96},{128,112},... | collective-permute-start | bytes 983048 | tf_op jit(solution)/shard_map/ppermute | solution.py:646
  9.5 31.9 %all-to-all-start = ((f32[32,4,128]{2,1,0:T(4,128)}), f32[32,4,128]{2,1,0:T(4,128)S(1)}, u32[]{:S(2)}, u32[]{:S(2)}) async-start(f32[32,4,128]{2,1,0:T(4,128)} %bitcast.19), calls=%async_computation | async-start | bytes 131072 | tf_op jit(solution)/shard_map/all_to_all | solution.py:656
  27.6 13.8 %copy-start.4 = (f32[2,128,128]{2,1,0:T(8,128)S(1)}, f32[2,128,128]{2,1,0:T(8,128)}, u32[]{:S(2)}) copy-start(f32[2,128,128]{2,1,0:T(8,128)} %mortar.5) | copy-start | bytes 393220
  27.8 15.2 %collective-permute-start.2 = (f32[14,24,128]{2,1,0:T(8,128)S(1)}, f32[14,24,128]{2,1,0:T(8,128)S(1)}, u32[]{:S(2)}, u32[]{:S(2)}) collective-permute-start(f32[14,24,128]{2,1,0:T(8,128)S(1)} %get-tuple-element.24), channel_id=1, source_target_pairs={{0,1},{1,2},{2,3},{3,4},{4,5},{5,6},{6,7},{7,8},{8,9},{9,10},{10,1... | collective-permute-start | bytes 516104 | tf_op jit(solution)/shard_map/ppermute | solution.py:646
  31.0 10.4 %copy-start.7 = (f32[2,128]{1,0:T(2,128)S(1)}, f32[2,128]{1,0:T(2,128)}, u32[]{:S(2)}) copy-start(f32[2,128]{1,0:T(2,128)} %pressure.1) | copy-start | bytes 3076
  31.0 10.4 %copy-start.8 = (s32[2]{0:T(128)S(1)}, s32[2]{0:T(128)}, u32[]{:S(2)}) copy-start(s32[2]{0:T(128)} %active.1) | copy-start | bytes 28
  31.0 10.4 %copy-start.5 = (s32[2]{0:T(128)S(1)}, s32[2]{0:T(128)}, u32[]{:S(2)}) copy-start(s32[2]{0:T(128)} %partner.7) | copy-start | bytes 28
  31.0 10.4 %copy-start.6 = (f32[2,128]{1,0:T(2,128)S(1)}, f32[2,128]{1,0:T(2,128)}, u32[]{:S(2)}) copy-start(f32[2,128]{1,0:T(2,128)} %gap0.1) | copy-start | bytes 3076
  31.0 11.9 %collective-permute-start.3 = (f32[14,24,128]{2,1,0:T(8,128)S(1)}, f32[14,24,128]{2,1,0:T(8,128)S(1)}, u32[]{:S(2)}, u32[]{:S(2)}) collective-permute-start(f32[14,24,128]{2,1,0:T(8,128)S(1)} %get-tuple-element.25), channel_id=1, source_target_pairs={{1,0},{2,1},{3,2},{4,3},{5,4},{6,5},{7,6},{8,7},{9,8},{10,9},{11,1... | collective-permute-start | bytes 516104 | tf_op jit(solution)/shard_map/ppermute | solution.py:646
  44.1 22.5 %all-to-all-start.1 = ((f32[32,4,128]{2,1,0:T(4,128)}), f32[32,4,128]{2,1,0:T(4,128)S(1)}, u32[]{:S(2)}, u32[]{:S(2)}) async-start(f32[32,4,128]{2,1,0:T(4,128)} %bitcast.2), calls=%async_computation.1 | async-start | bytes 131072 | tf_op jit(solution)/shard_map/all_to_all | solution.py:656
  68.9 17.0 %all-to-all-start.2 = ((f32[32,4,128]{2,1,0:T(4,128)}), f32[32,4,128]{2,1,0:T(4,128)S(1)}, u32[]{:S(2)}, u32[]{:S(2)}) async-start(f32[32,4,128]{2,1,0:T(4,128)} %bitcast.4), calls=%async_computation.2 | async-start | bytes 131072 | tf_op jit(solution)/shard_map/all_to_all | solution.py:656
  72.6 5.3 %collective-permute-start.4 = (f32[128,128]{1,0:T(8,128)S(1)}, f32[128,128]{1,0:T(8,128)S(1)}, u32[]{:S(2)}, u32[]{:S(2)}) collective-permute-start(f32[128,128]{1,0:T(8,128)S(1)} %get-tuple-element.31), channel_id=1, source_target_pairs={{0,1},{1,2},{2,3},{3,4},{4,5},{5,6},{6,7},{7,8},{8,9},{9,10},{10,1... | collective-permute-start | bytes 196616 | tf_op jit(solution)/shard_map/ppermute | solution.py:700

commit v6 on v5

--- a/solution.py
+++ b/solution.py
@@ -579,6 +579,55 @@
     fill(package, stack_rows([send, send]))
 
 
+def two_sum(a, b):
+    total_of = a + b
+    shift = total_of - a
+    return total_of, (a - (total_of - shift)) + (b - shift)
+
+
+def halves(a):
+    big = 4097.0 * a
+    high = big - (big - a)
+    return high, a - high
+
+
+def pair_add(x, y):
+    high, low = two_sum(x[0], y[0])
+    return two_sum(high, low + (x[1] + y[1]))
+
+
+def pair_mul(x, y):
+    product = x[0] * y[0]
+    a, b = halves(x[0])
+    c, d = halves(y[0])
+    error = ((a * c - product) + a * d + b * c) + b * d
+    return two_sum(product, error + (x[0] * y[1] + x[1] * y[0]))
+
+
+def pair_scale(x, factor):
+    return x[0] * factor, x[1] * factor
+
+
+def pair_div(x, y):
+    first = x[0] / y[0]
+    zero = jnp.zeros_like(first)
+    rest = pair_add(x, pair_scale(pair_mul(y, (first, zero)), -1.0))
+    return two_sum(first, rest[0] / y[0])
+
+
+def pair_rows(high, low):
+    while high.shape[0] > 8:
+        half = high.shape[0] // 2
+        sums, error = two_sum(high[:half], high[half:])
+        low = (low[:half] + low[half:]) + error
+        high = sums
+    for step in (4, 2, 1):
+        sums, error = two_sum(high, roll(high, step, 0))
+        low = (low + roll(low, step, 0)) + error
+        high = sums
+    return high, low
+
+
 def reduce_column(rows, package):
     value = rows[...]
     count = value.shape[0]
@@ -595,24 +644,34 @@
     )
     counted = ((place == 1) | (place == 2)) & (lane % 32 == 0) & (row < count - 4)
     across = total(jnp.where(counted, across, 0.0))
-    sums = jnp.sum(jnp.where(place == 0, value, 0.0), axis=0, keepdims=True)
-    lane1 = iota((1, LANES), 1)
-    sums = jnp.where((lane1 >= 16) & (lane1 < 20), sums, 0.0)
-    sums = sums - jnp.where(lane1 == 19, across, 0.0)
-    index = iota((8, LANES), 0)
-    fill(package, jnp.where(index % 2 == 0, sums, 0.0))
+    kept = jnp.where((place == 0) & (lane >= 16) & (lane < 20), value, 0.0)
+    high, low = pair_rows(kept, jnp.zeros_like(kept))
+    row, lane = iota((8, LANES), 0), iota((8, LANES), 1)
+    high, error = two_sum(high, jnp.where(lane == 19, -across, 0.0))
+    low = roll(low + error, 4, 1)
+    fill(package, jnp.where(row % 2 == 0, high + low, 0.0))
 
 
 def finish(rows, res, image, res_2, image_2, state, edges, second, last, increment, new_press):
-    sums = jnp.sum(rows[...], axis=0, keepdims=True)
+    value = rows[...]
+    lane = iota(value.shape, 1)
+    high = jnp.where((lane >= 16) & (lane < 20), value, 0.0)
+    low = roll(jnp.where((lane >= 20) & (lane < 24), value, 0.0), -4, 1)
+    high, low = pair_rows(high, low)
     lane = iota((1, LANES), 1)
-    m0, m1, m2, m3 = [
-        jnp.sum(jnp.where(lane == 16 + k, sums, 0.0), axis=1, keepdims=True) for k in range(4)
-    ]
-    alpha = m0 / m1
-    left = alpha * alpha * m2 - m0
-    beta = left / m0
-    energy = (m1 - 2.0 * alpha * m2 + alpha * alpha * m3) - beta * left / alpha
+
+    def at_lane(part, k):
+        return jnp.sum(jnp.where(lane == 16 + k, part[0:1], 0.0), axis=1, keepdims=True)
+
+    m0, m1, m2, m3 = [two_sum(at_lane(high, k), at_lane(low, k)) for k in range(4)]
+    alpha = pair_div(m0, m1)
+    square = pair_mul(alpha, alpha)
+    left = pair_add(pair_mul(square, m2), pair_scale(m0, -1.0))
+    energy = pair_add(m1, pair_scale(pair_mul(alpha, m2), -2.0))
+    energy = pair_add(energy, pair_mul(square, m3))
+    left, alpha = left[0], alpha[0]
+    beta = left / m0[0]
+    energy = energy[0] - beta * left / alpha
     step = left / energy
     c_res = alpha + step * (1.0 + beta)
     c_im = -step * alpha
@@ -659,12 +718,11 @@
     up, down, package = call(
         pack_x,
         [slabs, slabs, whole],
-        (partner, *tile),
+        tuple(pltpu.with_memory_space_constraint(a, pltpu.HBM) for a in (partner, *tile)),
         smem=(0,),
         away=range(1, 5),
         scratch=[(2, 8, 32, LANES)],
         more=[pltpu.SemaphoreType.DMA((18,))],
-        limit=60,
     )
     surfaces = trade(package, row)
     low_x, high_x = shifted(up, "gx", 1), shifted(down, "gx", -1)

time: 124 us -> 124 us (level)
  no operation moved by 1% of the time
where the time goes in v6:
time: 124 us
  starting transfers between devices  42.2 us (34%)
  blocking collectives  37.1 us (30%)
  waiting for transfers between devices  28 us (23%)
  Pallas kernels  15.3 us (12%)
    all_to_all x2, blocking collectives, trade(): return lax.all_to_all(package, axes, 0, 0, tiled=True)  35.2 us
    all_to_all x3, starting transfers between devices, trade(): return lax.all_to_all(package, axes, 0, 0, tiled=True)  30.5 us
    all_to_all x3, waiting for transfers between devices, trade(): return lax.all_to_all(package, axes, 0, 0, tiled=True)  26.3 us
    pallas_call x10, Pallas kernels, call(): pl.pallas_call(body, out_shape=shapes if many else shapes[0], in_specs=sp...  15.3 us
    ppermute x4, starting transfers between devices, shifted(): return lax.ppermute(block, axis, pairs)  10.4 us
  transfers between devices with their start and end apart: 8, of which 4 were waited for; matrix products, arithmetic and copies ran while one was open for 0% of the time, Pallas kernels for 5%

profile of v6, /device:TPU:1, one launch (start us, length us, event | category | flops | bytes accessed | tf_op | source)
XLA Modules:
  0.0 123.6 jit_solution(6553740253824264013)
XLA Ops:
  0.7 2.7 %shard_map.104 = (f32[20,32,128]{2,1,0:T(8,128)S(1)}, f32[20,32,128]{2,1,0:T(8,128)S(1)}, f32[128,128]{1,0:T(8,128)}) custom-call(s32[2]{0:T(128)} %partner.7, f32[1,3,8,32,128]{4,3,2,1,0:T(8,128)} %disp.9, f32[1,3,8,32,128]{4,3,2,1,0:T(8,128)} %force.9, f32[1,8,32,128]{3,2,1,0:T(8,128)} %kappa.9, f32[1,8,32,128]{3,2,1,0:T(8,128)} %sigma.9), custom_call_target="tpu_custom_call" | custom-call | tf_op jit(solution)/shard_map/pallas_call | solution.py:37
  3.4 4.5 %collective-permute-start = (f32[20,32,128]{2,1,0:T(8,128)S(1)}, f32[20,32,128]{2,1,0:T(8,128)S(1)}, u32[]{:S(2)}, u32[]{:S(2)}) collective-permute-start(f32[20,32,128]{2,1,0:T(8,128)S(1)} %get-tuple-element.22), channel_id=1, source_target_pairs={{0,16},{16,32},{32,48},{48,64},{64,80},{80,96},{96,112},{112,128},... | collective-permute-start | bytes 983048 | tf_op jit(solution)/shard_map/ppermute | solution.py:705
  7.9 1.3 %collective-permute-start.1 = (f32[20,32,128]{2,1,0:T(8,128)S(1)}, f32[20,32,128]{2,1,0:T(8,128)S(1)}, u32[]{:S(2)}, u32[]{:S(2)}) collective-permute-start(f32[20,32,128]{2,1,0:T(8,128)S(1)} %get-tuple-element.23), channel_id=1, source_target_pairs={{16,0},{32,16},{48,32},{64,48},{80,64},{96,80},{112,96},{128,112},... | collective-permute-start | bytes 983048 | tf_op jit(solution)/shard_map/ppermute | solution.py:705
  9.2 18.1 %all-to-all-start = ((f32[32,4,128]{2,1,0:T(4,128)}), f32[32,4,128]{2,1,0:T(4,128)S(1)}, u32[]{:S(2)}, u32[]{:S(2)}) async-start(f32[32,4,128]{2,1,0:T(4,128)} %bitcast), calls=%async_computation | async-start | bytes 131072 | tf_op jit(solution)/shard_map/all_to_all | solution.py:715
  27.5 3.2 %collective-permute-start.2 = (f32[14,24,128]{2,1,0:T(8,128)S(1)}, f32[14,24,128]{2,1,0:T(8,128)S(1)}, u32[]{:S(2)}, u32[]{:S(2)}) collective-permute-start(f32[14,24,128]{2,1,0:T(8,128)S(1)} %get-tuple-element.24), channel_id=1, source_target_pairs={{0,1},{1,2},{2,3},{3,4},{4,5},{5,6},{6,7},{7,8},{8,9},{9,10},{10,1... | collective-permute-start | bytes 516104 | tf_op jit(solution)/shard_map/ppermute | solution.py:705
  30.8 1.4 %collective-permute-start.3 = (f32[14,24,128]{2,1,0:T(8,128)S(1)}, f32[14,24,128]{2,1,0:T(8,128)S(1)}, u32[]{:S(2)}, u32[]{:S(2)}) collective-permute-start(f32[14,24,128]{2,1,0:T(8,128)S(1)} %get-tuple-element.25), channel_id=1, source_target_pairs={{1,0},{2,1},{3,2},{4,3},{5,4},{6,5},{7,6},{8,7},{9,8},{10,9},{11,1... | collective-permute-start | bytes 516104 | tf_op jit(solution)/shard_map/ppermute | solution.py:705
  32.2 8.9 %all-to-all-done = f32[32,4,128]{2,1,0:T(4,128)S(1)} async-done(((f32[32,4,128]{2,1,0:T(4,128)}), f32[32,4,128]{2,1,0:T(4,128)S(1)}, u32[]{:S(2)}, u32[]{:S(2)}) %all-to-all-start) | async-done | bytes 65568 | tf_op jit(solution)/shard_map/all_to_all | solution.py:715
  41.2 1.5 %shard_map.106.state = f32[16,128]{1,0:T(8,128)S(1)} custom-call(s32[2]{0:T(128)S(1)} %copy-done.5, s32[2]{0:T(128)S(1)} %copy-done.8, f32[128,128]{1,0:T(8,128)S(1)} %bitcast.10, f32[2,128]{1,0:T(2,128)S(1)} %copy-done.6, f32[2,128]{1,0:T(2,128)S(1)} %copy-done.7, f32[2,128,128]{2,1,0:T(8,128)S(1)} %copy-done.4), custom_call_target="tpu_custom_call" | custom-call | tf_op jit(solution)/shard_map/pallas_call | solution.py:37
  42.7 1.2 shard_map.107.after
  43.9 8.7 %all-to-all-start.1 = ((f32[32,4,128]{2,1,0:T(4,128)}), f32[32,4,128]{2,1,0:T(4,128)S(1)}, u32[]{:S(2)}, u32[]{:S(2)}) async-start(f32[32,4,128]{2,1,0:T(4,128)} %bitcast.2), calls=%async_computation.1 | async-start | bytes 131072 | tf_op jit(solution)/shard_map/all_to_all | solution.py:715
  52.6 2.5 %shard_map.108 = (f32[1,8,32,128]{3,2,1,0:T(8,128)S(1)}, f32[1,8,32,128]{3,2,1,0:T(8,128)S(1)}, f32[4,8,128]{2,1,0:T(8,128)S(1)}, f32[16,8,128]{2,1,0:T(8,128)S(1)}) custom-call(f32[1,3,8,32,128]{4,3,2,1,0:T(8,128)S(1)} %copy-done, f32[1,3,8,32,128]{4,3,2,1,0:T(8,128)S(1)} %copy-done.1, f32[1,8,32,128]{3,2,1,0:T(8,128)S(1)} %copy-done.2, ...), custom_call_target="tpu_custom_call" | custom-call | tf_op jit(solution)/shard_map/pallas_call | solution.py:37
  55.1 11.3 %all-to-all-done.1 = f32[32,4,128]{2,1,0:T(4,128)S(1)} async-done(((f32[32,4,128]{2,1,0:T(4,128)}), f32[32,4,128]{2,1,0:T(4,128)S(1)}, u32[]{:S(2)}, u32[]{:S(2)}) %all-to-all-start.1) | async-done | bytes 65568 | tf_op jit(solution)/shard_map/all_to_all | solution.py:715
  66.3 2.3 %shard_map.109 = (f32[8,128]{1,0:T(8,128)S(1)}, f32[8,128]{1,0:T(8,128)S(1)}, f32[16,128]{1,0:T(8,128)S(1)}, f32[128,128]{1,0:T(8,128)S(1)}, f32[128,128]{1,0:T(8,128)}) custom-call(s32[2]{0:T(128)S(1)} %copy-done.5, f32[128,128]{1,0:T(8,128)S(1)} %bitcast.11, f32[128,128]{1,0:T(8,128)S(1)} %bitcast.14, f32[16,128]{1,0:T(8,128)S(1)} %shard_map.106.state, ...), custom_call_target="tpu_custom_call" | custom-call | tf_op jit(solution)/shard_map/pallas_call | solution.py:37
  68.7 3.6 %all-to-all-start.2 = ((f32[32,4,128]{2,1,0:T(4,128)}), f32[32,4,128]{2,1,0:T(4,128)S(1)}, u32[]{:S(2)}, u32[]{:S(2)}) async-start(f32[32,4,128]{2,1,0:T(4,128)} %bitcast.4), calls=%async_computation.2 | async-start | bytes 131072 | tf_op jit(solution)/shard_map/all_to_all | solution.py:715
  72.3 1.3 %collective-permute-start.4 = (f32[128,128]{1,0:T(8,128)S(1)}, f32[128,128]{1,0:T(8,128)S(1)}, u32[]{:S(2)}, u32[]{:S(2)}) collective-permute-start(f32[128,128]{1,0:T(8,128)S(1)} %get-tuple-element.31), channel_id=1, source_target_pairs={{0,1},{1,2},{2,3},{3,4},{4,5},{5,6},{6,7},{7,8},{8,9},{9,10},{10,1... | collective-permute-start | bytes 196616 | tf_op jit(solution)/shard_map/ppermute | solution.py:758
  73.6 2.3 %shard_map.110 = (f32[2,8,32,128]{3,2,1,0:T(8,128)S(1)}, f32[2,8,32,128]{3,2,1,0:T(8,128)S(1)}, f32[4,8,128]{2,1,0:T(8,128)S(1)}) custom-call(f32[1,3,8,32,128]{4,3,2,1,0:T(8,128)S(1)} %copy-done, f32[1,3,8,32,128]{4,3,2,1,0:T(8,128)S(1)} %copy-done.1, f32[1,8,32,128]{3,2,1,0:T(8,128)S(1)} %copy-done.2, f32[1,8,32,128]{3,2,1,0:T(8,128)S(1)} %copy-done.3, ...), custom_call_target="tpu_custom_call" | custom-call | tf_op jit(solution)/shard_map/pallas_call | solution.py:37
  75.9 1.7 %collective-permute-done.4 = f32[128,128]{1,0:T(8,128)S(1)} collective-permute-done((f32[128,128]{1,0:T(8,128)S(1)}, f32[128,128]{1,0:T(8,128)S(1)}, u32[]{:S(2)}, u32[]{:S(2)}) %collective-permute-start.4) | collective-permute-done | bytes 65568 | tf_op jit(solution)/shard_map/ppermute | solution.py:758
  77.6 1.9 %all_gather.3.beside = f32[256,128]{1,0:T(8,128)S(1)} all-gather(f32[128,128]{1,0:T(8,128)S(1)} %collective-permute-done.4), channel_id=1, replica_groups=mesh['body'=2,'gx'=16,'gy'=16] {'body'}, dimensions={0}, use_global_device_ids=true | all-gather | bytes 196608 | tf_op jit(solution)/shard_map/all_gather | solution.py:759
  79.5 6.1 %all-to-all-done.2 = f32[32,4,128]{2,1,0:T(4,128)S(1)} async-done(((f32[32,4,128]{2,1,0:T(4,128)}), f32[32,4,128]{2,1,0:T(4,128)S(1)}, u32[]{:S(2)}, u32[]{:S(2)}) %all-to-all-start.2) | async-done | bytes 65568 | tf_op jit(solution)/shard_map/all_to_all | solution.py:715
  85.7 1.3 %shard_map.111 = (f32[64,128]{1,0:T(8,128)S(1)}, f32[24,128]{1,0:T(8,128)S(1)}) custom-call(s32[2]{0:T(128)S(1)} %copy-done.5, f32[128,128]{1,0:T(8,128)S(1)} %bitcast.12, f32[128,128]{1,0:T(8,128)S(1)} %bitcast.13, f32[16,128]{1,0:T(8,128)S(1)} %shard_map.106.state, f32[2,128,128]{2,1,0:T(8,128)S(1)} %copy-done.4, ...), custom_call_target="tpu_custom_call" | custom-call | tf_op jit(solution)/shard_map/pallas_call | solution.py:37
  86.9 14.2 %all_to_all.55 = f32[16,4,128]{2,1,0:T(4,128)S(1)} all-to-all(f32[16,4,128]{2,1,0:T(4,128)S(1)} %bitcast.18), channel_id=1, replica_groups=mesh['body'=2,'gx'=16,'gy'=16] {'gy'}, dimensions={0} | all-to-all | bytes 65536 | tf_op jit(solution)/shard_map/all_to_all | solution.py:715
  101.1 0.4 shard_map.112
  101.5 21.0 %all_to_all.56 = f32[32,2,128]{2,1,0:T(2,128)S(1)} all-to-all(f32[32,2,128]{2,1,0:T(2,128)S(1)} %bitcast.17), channel_id=1, replica_groups=mesh['body'=2,'gx'=16,'gy'=16] {'body','gx'}, dimensions={0} | all-to-all | bytes 65536 | tf_op jit(solution)/shard_map/all_to_all | solution.py:715
  122.5 1.1 shard_map.113
  (23 shorter events, 0.1 us)
Async XLA Ops:
  0.6 26.8 %copy-start.1 = (f32[1,3,8,32,128]{4,3,2,1,0:T(8,128)S(1)}, f32[1,3,8,32,128]{4,3,2,1,0:T(8,128)}, u32[]{:S(2)}) copy-start(f32[1,3,8,32,128]{4,3,2,1,0:T(8,128)} %force.9) | copy-start | bytes 1179652
  0.6 26.8 %copy-start = (f32[1,3,8,32,128]{4,3,2,1,0:T(8,128)S(1)}, f32[1,3,8,32,128]{4,3,2,1,0:T(8,128)}, u32[]{:S(2)}) copy-start(f32[1,3,8,32,128]{4,3,2,1,0:T(8,128)} %disp.9) | copy-start | bytes 1179652
  0.6 26.8 %copy-start.3 = (f32[1,8,32,128]{3,2,1,0:T(8,128)S(1)}, f32[1,8,32,128]{3,2,1,0:T(8,128)}, u32[]{:S(2)}) copy-start(f32[1,8,32,128]{3,2,1,0:T(8,128)} %sigma.9) | copy-start | bytes 393220
  3.4 24.1 %copy-start.2 = (f32[1,8,32,128]{3,2,1,0:T(8,128)S(1)}, f32[1,8,32,128]{3,2,1,0:T(8,128)}, u32[]{:S(2)}) copy-start(f32[1,8,32,128]{3,2,1,0:T(8,128)} %kappa.9) | copy-start | bytes 393220
  3.4 24.0 %collective-permute-start = (f32[20,32,128]{2,1,0:T(8,128)S(1)}, f32[20,32,128]{2,1,0:T(8,128)S(1)}, u32[]{:S(2)}, u32[]{:S(2)}) collective-permute-start(f32[20,32,128]{2,1,0:T(8,128)S(1)} %get-tuple-element.22), channel_id=1, source_target_pairs={{0,16},{16,32},{32,48},{48,64},{64,80},{80,96},{96,112},{112,128},... | collective-permute-start | bytes 983048 | tf_op jit(solution)/shard_map/ppermute | solution.py:705
  7.9 19.5 %collective-permute-start.1 = (f32[20,32,128]{2,1,0:T(8,128)S(1)}, f32[20,32,128]{2,1,0:T(8,128)S(1)}, u32[]{:S(2)}, u32[]{:S(2)}) collective-permute-start(f32[20,32,128]{2,1,0:T(8,128)S(1)} %get-tuple-element.23), channel_id=1, source_target_pairs={{16,0},{32,16},{48,32},{64,48},{80,64},{96,80},{112,96},{128,112},... | collective-permute-start | bytes 983048 | tf_op jit(solution)/shard_map/ppermute | solution.py:705
  9.2 31.9 %all-to-all-start = ((f32[32,4,128]{2,1,0:T(4,128)}), f32[32,4,128]{2,1,0:T(4,128)S(1)}, u32[]{:S(2)}, u32[]{:S(2)}) async-start(f32[32,4,128]{2,1,0:T(4,128)} %bitcast), calls=%async_computation | async-start | bytes 131072 | tf_op jit(solution)/shard_map/all_to_all | solution.py:715
  27.4 13.8 %copy-start.4 = (f32[2,128,128]{2,1,0:T(8,128)S(1)}, f32[2,128,128]{2,1,0:T(8,128)}, u32[]{:S(2)}) copy-start(f32[2,128,128]{2,1,0:T(8,128)} %mortar.5) | copy-start | bytes 393220
  27.5 15.2 %collective-permute-start.2 = (f32[14,24,128]{2,1,0:T(8,128)S(1)}, f32[14,24,128]{2,1,0:T(8,128)S(1)}, u32[]{:S(2)}, u32[]{:S(2)}) collective-permute-start(f32[14,24,128]{2,1,0:T(8,128)S(1)} %get-tuple-element.24), channel_id=1, source_target_pairs={{0,1},{1,2},{2,3},{3,4},{4,5},{5,6},{6,7},{7,8},{8,9},{9,10},{10,1... | collective-permute-start | bytes 516104 | tf_op jit(solution)/shard_map/ppermute | solution.py:705
  30.8 10.4 %copy-start.7 = (f32[2,128]{1,0:T(2,128)S(1)}, f32[2,128]{1,0:T(2,128)}, u32[]{:S(2)}) copy-start(f32[2,128]{1,0:T(2,128)} %pressure.1) | copy-start | bytes 3076
  30.8 10.4 %copy-start.8 = (s32[2]{0:T(128)S(1)}, s32[2]{0:T(128)}, u32[]{:S(2)}) copy-start(s32[2]{0:T(128)} %active.1) | copy-start | bytes 28
  30.8 10.4 %copy-start.5 = (s32[2]{0:T(128)S(1)}, s32[2]{0:T(128)}, u32[]{:S(2)}) copy-start(s32[2]{0:T(128)} %partner.7) | copy-start | bytes 28
  30.8 10.4 %copy-start.6 = (f32[2,128]{1,0:T(2,128)S(1)}, f32[2,128]{1,0:T(2,128)}, u32[]{:S(2)}) copy-start(f32[2,128]{1,0:T(2,128)} %gap0.1) | copy-start | bytes 3076
  30.8 11.9 %collective-permute-start.3 = (f32[14,24,128]{2,1,0:T(8,128)S(1)}, f32[14,24,128]{2,1,0:T(8,128)S(1)}, u32[]{:S(2)}, u32[]{:S(2)}) collective-permute-start(f32[14,24,128]{2,1,0:T(8,128)S(1)} %get-tuple-element.25), channel_id=1, source_target_pairs={{1,0},{2,1},{3,2},{4,3},{5,4},{6,5},{7,6},{8,7},{9,8},{10,9},{11,1... | collective-permute-start | bytes 516104 | tf_op jit(solution)/shard_map/ppermute | solution.py:705
  43.9 22.5 %all-to-all-start.1 = ((f32[32,4,128]{2,1,0:T(4,128)}), f32[32,4,128]{2,1,0:T(4,128)S(1)}, u32[]{:S(2)}, u32[]{:S(2)}) async-start(f32[32,4,128]{2,1,0:T(4,128)} %bitcast.2), calls=%async_computation.1 | async-start | bytes 131072 | tf_op jit(solution)/shard_map/all_to_all | solution.py:715
  68.7 17.0 %all-to-all-start.2 = ((f32[32,4,128]{2,1,0:T(4,128)}), f32[32,4,128]{2,1,0:T(4,128)S(1)}, u32[]{:S(2)}, u32[]{:S(2)}) async-start(f32[32,4,128]{2,1,0:T(4,128)} %bitcast.4), calls=%async_computation.2 | async-start | bytes 131072 | tf_op jit(solution)/shard_map/all_to_all | solution.py:715
  72.3 5.3 %collective-permute-start.4 = (f32[128,128]{1,0:T(8,128)S(1)}, f32[128,128]{1,0:T(8,128)S(1)}, u32[]{:S(2)}, u32[]{:S(2)}) collective-permute-start(f32[128,128]{1,0:T(8,128)S(1)} %get-tuple-element.31), channel_id=1, source_target_pairs={{0,1},{1,2},{2,3},{3,4},{4,5},{5,6},{6,7},{7,8},{8,9},{9,10},{10,1... | collective-permute-start | bytes 196616 | tf_op jit(solution)/shard_map/ppermute | solution.py:758

commit v7 on v6

--- a/solution.py
+++ b/solution.py
@@ -147,31 +147,21 @@
         down[x, 16:24] = jnp.where(sub < 2, first[7], roll(first[6], 2, 0))
 
 
-def mat_vec(matrix, row):
-    return lax.dot_general(
-        jnp.broadcast_to(row, (8, LANES)),
-        matrix,
-        (((1,), (1,)), ((), ())),
-        precision=HIGH,
-        preferred_element_type=F32,
-    )[0:1]
+def turn(mortar, turned):
+    for k in range(2):
+        turned[k] = mortar[k].T
 
 
 def vec_mat(row, matrix):
-    return lax.dot_general(
-        jnp.broadcast_to(row, (8, LANES)),
-        matrix,
-        (((1,), (0,)), ((), ())),
-        precision=HIGH,
-        preferred_element_type=F32,
-    )[0:1]
+    column = jnp.broadcast_to(row, (LANES, LANES)).T
+    return jnp.sum(column * matrix, axis=0, keepdims=True)
 
 
 def surface_row(q):
     return 4 * (q // 2) + q % 2
 
 
-def contact_first(partner, active, rows, gap0, pressure, mortar, state):
+def contact_first(partner, active, rows, gap0, pressure, mortar, turned, state):
     gx = lax.axis_index("gx")
     half = rows.shape[0] // 2
     for k in range(2):
@@ -180,7 +170,7 @@
         matrix = mortar[k]
         press = pressure[k : k + 1, :]
         flag = jnp.full((1, LANES), active[k], jnp.int32).astype(F32)
-        gap = gap0[k : k + 1, :] - own - mat_vec(matrix, master)
+        gap = gap0[k : k + 1, :] - own - vec_mat(master, turned[k])
         radius = jnp.sqrt(gap * gap + press * press + 0.01)
         complement = gap + press - radius
         slope_gap = 1.0 - gap / radius
@@ -441,7 +431,7 @@
 
 
 def contact_second(
-    partner, select_rows, rows, state, mortar, strips,
+    partner, select_rows, rows, state, mortar, turned, strips,
     edges, out, moved, message, package, padded, surf0, surf1,
 ):
     body, gx = lax.axis_index("body"), lax.axis_index("gx")
@@ -460,8 +450,8 @@
     sent = []
     for k in range(2):
         matrix = mortar[k]
-        gap = -surf0[pl.ds(4 * gx + k, 1), :] - mat_vec(
-            matrix, surf1[pl.ds(surface_row(partner[k]), 1), :]
+        gap = -surf0[pl.ds(4 * gx + k, 1), :] - vec_mat(
+            surf1[pl.ds(surface_row(partner[k]), 1), :], turned[k]
         )
         push = state[k : k + 1, :] * gap
         pulled = vec_mat(push, matrix)
@@ -507,7 +497,7 @@
 
 
 def measure_moments(
-    partner, select_rows, rows, state, mortar, strips, edges, second, moved, beside,
+    partner, select_rows, rows, state, turned, strips, edges, second, moved, beside,
     moments, more_moments, package, image_out, padded, surf0, surf1,
 ):
     body, gx = lax.axis_index("body"), lax.axis_index("gx")
@@ -538,8 +528,8 @@
     push_sum = jnp.zeros((1, LANES), F32)
     gap_sum = jnp.zeros((1, LANES), F32)
     for k in range(2):
-        gap = -surf0[pl.ds(4 * gx + k, 1), :] - mat_vec(
-            mortar[k], surf1[pl.ds(surface_row(partner[k]), 1), :]
+        gap = -surf0[pl.ds(4 * gx + k, 1), :] - vec_mat(
+            surf1[pl.ds(surface_row(partner[k]), 1), :], turned[k]
         )
         image_out[k : k + 1, :] = gap
         push_sum = push_sum + second[k : k + 1, :] * second[2 + k : 3 + k, :]
@@ -729,10 +719,11 @@
     rims = (LINES, 24, LANES)
     up, down = call(pack_y, [rims, rims], (*tile, low_x, high_x))
     low_y, high_y = shifted(up, "gy", 1), shifted(down, "gy", -1)
+    turned = call(turn, mortar.shape, (mortar,))
     state = call(
         contact_first,
         (16, LANES),
-        (partner, active, surfaces, gap0, pressure, mortar),
+        (partner, active, surfaces, gap0, pressure, mortar, turned),
         smem=(0, 1),
     )
     lines = (LINES, ROWS, LANES)
@@ -750,7 +741,7 @@
     edges, second, moved, message, package = call(
         contact_second,
         [(8, LANES), (8, LANES), (16, LANES), whole, whole],
-        (partner, surfaces, rows, state, mortar, strips),
+        (partner, surfaces, rows, state, mortar, turned, strips),
         smem=(0,),
         scratch=work,
     )
@@ -762,7 +753,7 @@
     package, last = call(
         measure_moments,
         [(4 * ny, LANES), (24, LANES)],
-        (partner, surfaces, rows, state, mortar, strips, edges, second, moved, beside, moments, more_moments),
+        (partner, surfaces, rows, state, turned, strips, edges, second, moved, beside, moments, more_moments),
         smem=(0,),
         scratch=work,
     )

time: 124 us -> 123 us (level)
  Pallas kernels: 15.3 us -> 14 us
    pallas_call x10 -> x11, Pallas kernels: 15.3 us -> 14 us  [call(): pl.pallas_call(body, out_shape=shapes if many else shapes[0], in_specs=sp...]
where the time goes in v7:
time: 123 us
  starting transfers between devices  42.6 us (35%)
  blocking collectives  37.1 us (30%)
  waiting for transfers between devices  28 us (23%)
  Pallas kernels  14 us (11%)
    all_to_all x2, blocking collectives, trade(): return lax.all_to_all(package, axes, 0, 0, tiled=True)  35.2 us
    all_to_all x3, starting transfers between devices, trade(): return lax.all_to_all(package, axes, 0, 0, tiled=True)  31 us
    all_to_all x3, waiting for transfers between devices, trade(): return lax.all_to_all(package, axes, 0, 0, tiled=True)  26.3 us
    pallas_call x11, Pallas kernels, call(): pl.pallas_call(body, out_shape=shapes if many else shapes[0], in_specs=sp...  14 us
    ppermute x4, starting transfers between devices, shifted(): return lax.ppermute(block, axis, pairs)  10.3 us
  transfers between devices with their start and end apart: 8, of which 4 were waited for; matrix products, arithmetic and copies ran while one was open for 0% of the time, Pallas kernels for 5%

profile of v7, /device:TPU:1, one launch (start us, length us, event | category | flops | bytes accessed | tf_op | source)
XLA Modules:
  0.0 122.7 jit_solution(8801803296234901849)
XLA Ops:
  0.7 2.7 %shard_map.104 = (f32[20,32,128]{2,1,0:T(8,128)S(1)}, f32[20,32,128]{2,1,0:T(8,128)S(1)}, f32[128,128]{1,0:T(8,128)}) custom-call(s32[2]{0:T(128)} %partner.7, f32[1,3,8,32,128]{4,3,2,1,0:T(8,128)} %disp.9, f32[1,3,8,32,128]{4,3,2,1,0:T(8,128)} %force.9, f32[1,8,32,128]{3,2,1,0:T(8,128)} %kappa.9, f32[1,8,32,128]{3,2,1,0:T(8,128)} %sigma.9), custom_call_target="tpu_custom_call" | custom-call | tf_op jit(solution)/shard_map/pallas_call | solution.py:37
  3.4 4.5 %collective-permute-start = (f32[20,32,128]{2,1,0:T(8,128)S(1)}, f32[20,32,128]{2,1,0:T(8,128)S(1)}, u32[]{:S(2)}, u32[]{:S(2)}) collective-permute-start(f32[20,32,128]{2,1,0:T(8,128)S(1)} %get-tuple-element.22), channel_id=1, source_target_pairs={{0,16},{16,32},{32,48},{48,64},{64,80},{80,96},{96,112},{112,128},... | collective-permute-start | bytes 983048 | tf_op jit(solution)/shard_map/ppermute | solution.py:695
  7.9 1.3 %collective-permute-start.1 = (f32[20,32,128]{2,1,0:T(8,128)S(1)}, f32[20,32,128]{2,1,0:T(8,128)S(1)}, u32[]{:S(2)}, u32[]{:S(2)}) collective-permute-start(f32[20,32,128]{2,1,0:T(8,128)S(1)} %get-tuple-element.23), channel_id=1, source_target_pairs={{16,0},{32,16},{48,32},{64,48},{80,64},{96,80},{112,96},{128,112},... | collective-permute-start | bytes 983048 | tf_op jit(solution)/shard_map/ppermute | solution.py:695
  9.2 18.1 %all-to-all-start = ((f32[32,4,128]{2,1,0:T(4,128)}), f32[32,4,128]{2,1,0:T(4,128)S(1)}, u32[]{:S(2)}, u32[]{:S(2)}) async-start(f32[32,4,128]{2,1,0:T(4,128)} %bitcast), calls=%async_computation | async-start | bytes 131072 | tf_op jit(solution)/shard_map/all_to_all | solution.py:705
  27.5 3.2 %collective-permute-start.2 = (f32[14,24,128]{2,1,0:T(8,128)S(1)}, f32[14,24,128]{2,1,0:T(8,128)S(1)}, u32[]{:S(2)}, u32[]{:S(2)}) collective-permute-start(f32[14,24,128]{2,1,0:T(8,128)S(1)} %get-tuple-element.24), channel_id=1, source_target_pairs={{0,1},{1,2},{2,3},{3,4},{4,5},{5,6},{6,7},{7,8},{8,9},{9,10},{10,1... | collective-permute-start | bytes 516104 | tf_op jit(solution)/shard_map/ppermute | solution.py:695
  30.8 1.3 %collective-permute-start.3 = (f32[14,24,128]{2,1,0:T(8,128)S(1)}, f32[14,24,128]{2,1,0:T(8,128)S(1)}, u32[]{:S(2)}, u32[]{:S(2)}) collective-permute-start(f32[14,24,128]{2,1,0:T(8,128)S(1)} %get-tuple-element.25), channel_id=1, source_target_pairs={{1,0},{2,1},{3,2},{4,3},{5,4},{6,5},{7,6},{8,7},{9,8},{10,9},{11,1... | collective-permute-start | bytes 516104 | tf_op jit(solution)/shard_map/ppermute | solution.py:695
  32.2 8.9 %all-to-all-done = f32[32,4,128]{2,1,0:T(4,128)S(1)} async-done(((f32[32,4,128]{2,1,0:T(4,128)}), f32[32,4,128]{2,1,0:T(4,128)S(1)}, u32[]{:S(2)}, u32[]{:S(2)}) %all-to-all-start) | async-done | bytes 65568 | tf_op jit(solution)/shard_map/all_to_all | solution.py:705
  41.2 0.8 shard_map.107.state
  42.0 1.1 shard_map.108.after
  43.1 9.3 %all-to-all-start.1 = ((f32[32,4,128]{2,1,0:T(4,128)}), f32[32,4,128]{2,1,0:T(4,128)S(1)}, u32[]{:S(2)}, u32[]{:S(2)}) async-start(f32[32,4,128]{2,1,0:T(4,128)} %bitcast.2), calls=%async_computation.1 | async-start | bytes 131072 | tf_op jit(solution)/shard_map/all_to_all | solution.py:705
  52.4 2.5 %shard_map.109 = (f32[1,8,32,128]{3,2,1,0:T(8,128)S(1)}, f32[1,8,32,128]{3,2,1,0:T(8,128)S(1)}, f32[4,8,128]{2,1,0:T(8,128)S(1)}, f32[16,8,128]{2,1,0:T(8,128)S(1)}) custom-call(f32[1,3,8,32,128]{4,3,2,1,0:T(8,128)S(1)} %copy-done, f32[1,3,8,32,128]{4,3,2,1,0:T(8,128)S(1)} %copy-done.1, f32[1,8,32,128]{3,2,1,0:T(8,128)S(1)} %copy-done.2, ...), custom_call_target="tpu_custom_call" | custom-call | tf_op jit(solution)/shard_map/pallas_call | solution.py:37
  54.9 11.3 %all-to-all-done.1 = f32[32,4,128]{2,1,0:T(4,128)S(1)} async-done(((f32[32,4,128]{2,1,0:T(4,128)}), f32[32,4,128]{2,1,0:T(4,128)S(1)}, u32[]{:S(2)}, u32[]{:S(2)}) %all-to-all-start.1) | async-done | bytes 65568 | tf_op jit(solution)/shard_map/all_to_all | solution.py:705
  66.2 1.7 %shard_map.110 = (f32[8,128]{1,0:T(8,128)S(1)}, f32[8,128]{1,0:T(8,128)S(1)}, f32[16,128]{1,0:T(8,128)S(1)}, f32[128,128]{1,0:T(8,128)S(1)}, f32[128,128]{1,0:T(8,128)}) custom-call(s32[2]{0:T(128)S(1)} %copy-done.5, f32[128,128]{1,0:T(8,128)S(1)} %bitcast.11, f32[128,128]{1,0:T(8,128)S(1)} %bitcast.14, f32[16,128]{1,0:T(8,128)S(1)} %shard_map.107.state, ...), custom_call_target="tpu_custom_call" | custom-call | tf_op jit(solution)/shard_map/pallas_call | solution.py:37
  67.9 3.6 %all-to-all-start.2 = ((f32[32,4,128]{2,1,0:T(4,128)}), f32[32,4,128]{2,1,0:T(4,128)S(1)}, u32[]{:S(2)}, u32[]{:S(2)}) async-start(f32[32,4,128]{2,1,0:T(4,128)} %bitcast.4), calls=%async_computation.2 | async-start | bytes 131072 | tf_op jit(solution)/shard_map/all_to_all | solution.py:705
  71.5 1.3 %collective-permute-start.4 = (f32[128,128]{1,0:T(8,128)S(1)}, f32[128,128]{1,0:T(8,128)S(1)}, u32[]{:S(2)}, u32[]{:S(2)}) collective-permute-start(f32[128,128]{1,0:T(8,128)S(1)} %get-tuple-element.31), channel_id=1, source_target_pairs={{0,1},{1,2},{2,3},{3,4},{4,5},{5,6},{6,7},{7,8},{8,9},{9,10},{10,1... | collective-permute-start | bytes 196616 | tf_op jit(solution)/shard_map/ppermute | solution.py:749
  72.8 2.3 %shard_map.111 = (f32[2,8,32,128]{3,2,1,0:T(8,128)S(1)}, f32[2,8,32,128]{3,2,1,0:T(8,128)S(1)}, f32[4,8,128]{2,1,0:T(8,128)S(1)}) custom-call(f32[1,3,8,32,128]{4,3,2,1,0:T(8,128)S(1)} %copy-done, f32[1,3,8,32,128]{4,3,2,1,0:T(8,128)S(1)} %copy-done.1, f32[1,8,32,128]{3,2,1,0:T(8,128)S(1)} %copy-done.2, f32[1,8,32,128]{3,2,1,0:T(8,128)S(1)} %copy-done.3, ...), custom_call_target="tpu_custom_call" | custom-call | tf_op jit(solution)/shard_map/pallas_call | solution.py:37
  75.1 1.7 %collective-permute-done.4 = f32[128,128]{1,0:T(8,128)S(1)} collective-permute-done((f32[128,128]{1,0:T(8,128)S(1)}, f32[128,128]{1,0:T(8,128)S(1)}, u32[]{:S(2)}, u32[]{:S(2)}) %collective-permute-start.4) | collective-permute-done | bytes 65568 | tf_op jit(solution)/shard_map/ppermute | solution.py:749
  76.8 1.9 %all_gather.3.beside = f32[256,128]{1,0:T(8,128)S(1)} all-gather(f32[128,128]{1,0:T(8,128)S(1)} %collective-permute-done.4), channel_id=1, replica_groups=mesh['body'=2,'gx'=16,'gy'=16] {'body'}, dimensions={0}, use_global_device_ids=true | all-gather | bytes 196608 | tf_op jit(solution)/shard_map/all_gather | solution.py:750
  78.7 6.1 %all-to-all-done.2 = f32[32,4,128]{2,1,0:T(4,128)S(1)} async-done(((f32[32,4,128]{2,1,0:T(4,128)}), f32[32,4,128]{2,1,0:T(4,128)S(1)}, u32[]{:S(2)}, u32[]{:S(2)}) %all-to-all-start.2) | async-done | bytes 65568 | tf_op jit(solution)/shard_map/all_to_all | solution.py:705
  84.8 1.2 shard_map.112
  86.0 14.2 %all_to_all.55 = f32[16,4,128]{2,1,0:T(4,128)S(1)} all-to-all(f32[16,4,128]{2,1,0:T(4,128)S(1)} %bitcast.18), channel_id=1, replica_groups=mesh['body'=2,'gx'=16,'gy'=16] {'gy'}, dimensions={0} | all-to-all | bytes 65536 | tf_op jit(solution)/shard_map/all_to_all | solution.py:705
  100.2 0.4 shard_map.113
  100.6 21.0 %all_to_all.56 = f32[32,2,128]{2,1,0:T(2,128)S(1)} all-to-all(f32[32,2,128]{2,1,0:T(2,128)S(1)} %bitcast.17), channel_id=1, replica_groups=mesh['body'=2,'gx'=16,'gy'=16] {'body','gx'}, dimensions={0} | all-to-all | bytes 65536 | tf_op jit(solution)/shard_map/all_to_all | solution.py:705
  121.6 1.1 shard_map.114
  (24 shorter events, 0.2 us)
Async XLA Ops:
  0.6 26.8 %copy-start.1 = (f32[1,3,8,32,128]{4,3,2,1,0:T(8,128)S(1)}, f32[1,3,8,32,128]{4,3,2,1,0:T(8,128)}, u32[]{:S(2)}) copy-start(f32[1,3,8,32,128]{4,3,2,1,0:T(8,128)} %force.9) | copy-start | bytes 1179652
  0.6 26.8 %copy-start = (f32[1,3,8,32,128]{4,3,2,1,0:T(8,128)S(1)}, f32[1,3,8,32,128]{4,3,2,1,0:T(8,128)}, u32[]{:S(2)}) copy-start(f32[1,3,8,32,128]{4,3,2,1,0:T(8,128)} %disp.9) | copy-start | bytes 1179652
  0.6 26.8 %copy-start.3 = (f32[1,8,32,128]{3,2,1,0:T(8,128)S(1)}, f32[1,8,32,128]{3,2,1,0:T(8,128)}, u32[]{:S(2)}) copy-start(f32[1,8,32,128]{3,2,1,0:T(8,128)} %sigma.9) | copy-start | bytes 393220
  3.4 24.1 %copy-start.2 = (f32[1,8,32,128]{3,2,1,0:T(8,128)S(1)}, f32[1,8,32,128]{3,2,1,0:T(8,128)}, u32[]{:S(2)}) copy-start(f32[1,8,32,128]{3,2,1,0:T(8,128)} %kappa.9) | copy-start | bytes 393220
  3.4 24.0 %collective-permute-start = (f32[20,32,128]{2,1,0:T(8,128)S(1)}, f32[20,32,128]{2,1,0:T(8,128)S(1)}, u32[]{:S(2)}, u32[]{:S(2)}) collective-permute-start(f32[20,32,128]{2,1,0:T(8,128)S(1)} %get-tuple-element.22), channel_id=1, source_target_pairs={{0,16},{16,32},{32,48},{48,64},{64,80},{80,96},{96,112},{112,128},... | collective-permute-start | bytes 983048 | tf_op jit(solution)/shard_map/ppermute | solution.py:695
  7.9 19.5 %collective-permute-start.1 = (f32[20,32,128]{2,1,0:T(8,128)S(1)}, f32[20,32,128]{2,1,0:T(8,128)S(1)}, u32[]{:S(2)}, u32[]{:S(2)}) collective-permute-start(f32[20,32,128]{2,1,0:T(8,128)S(1)} %get-tuple-element.23), channel_id=1, source_target_pairs={{16,0},{32,16},{48,32},{64,48},{80,64},{96,80},{112,96},{128,112},... | collective-permute-start | bytes 983048 | tf_op jit(solution)/shard_map/ppermute | solution.py:695
  9.2 31.9 %all-to-all-start = ((f32[32,4,128]{2,1,0:T(4,128)}), f32[32,4,128]{2,1,0:T(4,128)S(1)}, u32[]{:S(2)}, u32[]{:S(2)}) async-start(f32[32,4,128]{2,1,0:T(4,128)} %bitcast), calls=%async_computation | async-start | bytes 131072 | tf_op jit(solution)/shard_map/all_to_all | solution.py:705
  27.4 4.7 %copy-start.4 = (f32[2,128,128]{2,1,0:T(8,128)S(1)}, f32[2,128,128]{2,1,0:T(8,128)}, u32[]{:S(2)}) copy-start(f32[2,128,128]{2,1,0:T(8,128)} %mortar.5) | copy-start | bytes 393220
  27.5 14.4 %collective-permute-start.2 = (f32[14,24,128]{2,1,0:T(8,128)S(1)}, f32[14,24,128]{2,1,0:T(8,128)S(1)}, u32[]{:S(2)}, u32[]{:S(2)}) collective-permute-start(f32[14,24,128]{2,1,0:T(8,128)S(1)} %get-tuple-element.24), channel_id=1, source_target_pairs={{0,1},{1,2},{2,3},{3,4},{4,5},{5,6},{6,7},{7,8},{8,9},{9,10},{10,1... | collective-permute-start | bytes 516104 | tf_op jit(solution)/shard_map/ppermute | solution.py:695
  30.8 11.2 %collective-permute-start.3 = (f32[14,24,128]{2,1,0:T(8,128)S(1)}, f32[14,24,128]{2,1,0:T(8,128)S(1)}, u32[]{:S(2)}, u32[]{:S(2)}) collective-permute-start(f32[14,24,128]{2,1,0:T(8,128)S(1)} %get-tuple-element.25), channel_id=1, source_target_pairs={{1,0},{2,1},{3,2},{4,3},{5,4},{6,5},{7,6},{8,7},{9,8},{10,9},{11,1... | collective-permute-start | bytes 516104 | tf_op jit(solution)/shard_map/ppermute | solution.py:695
  32.1 9.1 %copy-start.7 = (f32[2,128]{1,0:T(2,128)S(1)}, f32[2,128]{1,0:T(2,128)}, u32[]{:S(2)}) copy-start(f32[2,128]{1,0:T(2,128)} %pressure.1) | copy-start | bytes 3076
  32.1 9.1 %copy-start.8 = (s32[2]{0:T(128)S(1)}, s32[2]{0:T(128)}, u32[]{:S(2)}) copy-start(s32[2]{0:T(128)} %active.1) | copy-start | bytes 28
  32.2 9.0 %copy-start.5 = (s32[2]{0:T(128)S(1)}, s32[2]{0:T(128)}, u32[]{:S(2)}) copy-start(s32[2]{0:T(128)} %partner.7) | copy-start | bytes 28
  32.2 9.0 %copy-start.6 = (f32[2,128]{1,0:T(2,128)S(1)}, f32[2,128]{1,0:T(2,128)}, u32[]{:S(2)}) copy-start(f32[2,128]{1,0:T(2,128)} %gap0.1) | copy-start | bytes 3076
  43.1 23.0 %all-to-all-start.1 = ((f32[32,4,128]{2,1,0:T(4,128)}), f32[32,4,128]{2,1,0:T(4,128)S(1)}, u32[]{:S(2)}, u32[]{:S(2)}) async-start(f32[32,4,128]{2,1,0:T(4,128)} %bitcast.2), calls=%async_computation.1 | async-start | bytes 131072 | tf_op jit(solution)/shard_map/all_to_all | solution.py:705
  67.9 17.0 %all-to-all-start.2 = ((f32[32,4,128]{2,1,0:T(4,128)}), f32[32,4,128]{2,1,0:T(4,128)S(1)}, u32[]{:S(2)}, u32[]{:S(2)}) async-start(f32[32,4,128]{2,1,0:T(4,128)} %bitcast.4), calls=%async_computation.2 | async-start | bytes 131072 | tf_op jit(solution)/shard_map/all_to_all | solution.py:705
  71.5 5.3 %collective-permute-start.4 = (f32[128,128]{1,0:T(8,128)S(1)}, f32[128,128]{1,0:T(8,128)S(1)}, u32[]{:S(2)}, u32[]{:S(2)}) collective-permute-start(f32[128,128]{1,0:T(8,128)S(1)} %get-tuple-element.31), channel_id=1, source_target_pairs={{0,1},{1,2},{2,3},{3,4},{4,5},{5,6},{6,7},{7,8},{8,9},{9,10},{10,1... | collective-permute-start | bytes 196616 | tf_op jit(solution)/shard_map/ppermute | solution.py:749
